TPU v7x, 32 devices: a whole 2x2x4 slice. The times are simulated.
32 devices in a mesh: fsdp: 16 (over z, x, core), rep: 2 (over y).
Axes of the slice: x: 2, y: 2, z: 4, core: 2. Of those that a mesh axis runs over, the one named last changes fastest.
Arguments:
- tokens: bfloat16 [32768, 1024], P(('fsdp', 'rep')), may hold values from -6 to 6
- seq_lengths: int32 [64, 4], P(('fsdp', 'rep')), may hold values from 0 to 512, as said below
- out_cotangent: bfloat16 [32768, 1024], P(('fsdp', 'rep')), may hold values from -6 to 6
- project_in: bfloat16 [1024, 3072], P('fsdp'), may hold values from -0.1875 to 0.1875
- project_out: bfloat16 [1024, 1024], P('fsdp'), may hold values from -1.5 to 1.5
- expand: bfloat16 [1024, 4096], P('fsdp'), may hold values from -0.1875 to 0.1875
- contract: bfloat16 [4096, 1024], P('fsdp'), may hold values from -0.09375 to 0.09375
- query_bias: bfloat16 [1024], P('fsdp'), may hold values from -3 to 3
- value_bias: bfloat16 [1024], P('fsdp'), may hold values from -3 to 3
- out_bias: bfloat16 [1024], P('fsdp'), may hold values from -2 to 2
- expand_bias: bfloat16 [4096], P('fsdp'), may hold values from -3 to 3
- contract_bias: bfloat16 [1024], P('fsdp'), may hold values from -2 to 2
- first_gain: bfloat16 [1024], P('fsdp'), may hold values from 0.5 to 1.5
- first_shift: bfloat16 [1024], P('fsdp'), may hold values from -2 to 2
- second_gain: bfloat16 [1024], P('fsdp'), may hold values from 0.5 to 1.5
- second_shift: bfloat16 [1024], P('fsdp'), may hold values from -2 to 2
Outputs:
- layer_output: bfloat16 [32768, 1024], P(('fsdp', 'rep'))
- grad_tokens: bfloat16 [32768, 1024], P(('fsdp', 'rep'))
- grad_project_in: float32 [1024, 3072], P('fsdp')
- grad_project_out: float32 [1024, 1024], P('fsdp')
- grad_expand: float32 [1024, 4096], P('fsdp')
- grad_contract: float32 [4096, 1024], P('fsdp')
- grad_query_bias: float32 [1024], P('fsdp')
- grad_value_bias: float32 [1024], P('fsdp')
- grad_out_bias: float32 [1024], P('fsdp')
- grad_expand_bias: float32 [4096], P('fsdp')
- grad_contract_bias: float32 [1024], P('fsdp')
- grad_first_gain: float32 [1024], P('fsdp')
- grad_first_shift: float32 [1024], P('fsdp')
- grad_second_gain: float32 [1024], P('fsdp')
- grad_second_shift: float32 [1024], P('fsdp')
Inputs may be any that keep to these rules, and one draw needn't show every extreme that they name: In each row of seq_lengths the lengths sum to at most 512; rows of a micro-batch past that sum are padding. In every draw one row holds a single sequence of exactly 512 and zeros.
All inputs are finite; a program needn't handle non-finite values.
Results may differ from a plain program's by a relative error of at most 0.015.
Values may be sent and summed in bfloat16 or wider, within the bound.
No kernel may reach another device: no remote copies, remote signals or barrier semaphores. Data moves between devices by JAX's collectives and lax.ppermute only.
A program may use at most 256 MiB of HBM per device.

v0:
```python
import jax
import jax.numpy as jnp
from jax import lax
from jax.sharding import PartitionSpec as P

H = 16
HD = 64


EPSILON = 1e-12
SCALE = 0.125


def segment_mask(row_lengths, row_count):
    boundary = jnp.cumsum(row_lengths, dtype=jnp.int32)
    position = lax.iota(jnp.int32, row_count)
    slot_index = jnp.sum((position[:, None] >= boundary[None, :]).astype(jnp.int32), axis=1)
    inside = slot_index < row_lengths.shape[0]
    together = (slot_index[:, None] == slot_index[None, :]) & inside[None, :]
    return together | (position[:, None] == position[None, :])


def normalize(summed, gain, shift):
    centre = jnp.mean(summed, axis=-1, keepdims=True)
    centred = summed - centre
    spread = jnp.mean(centred * centred, axis=-1, keepdims=True)
    return centred * lax.rsqrt(spread + EPSILON) * gain + shift


def exact_gelu(values):
    return jax.nn.gelu(values, approximate=False)


def outer_sum(left, right):
    return lax.dot_general(
        left, right, (((0,), (0,)), ((), ())), preferred_element_type=jnp.float32
    )


def through(gradient, weight):
    return lax.dot_general(
        gradient, weight, (((1,), (1,)), ((), ())), preferred_element_type=jnp.float32
    )


def split_heads(projected, row_count):
    width = projected.shape[1] // 3
    return tuple(
        (
            projected[:, column_block * width : (column_block + 1) * width].reshape(
                row_count, H, HD
            )
            for column_block in range(3)
        )
    )


def masked_scores(queries, keyed, allowed):
    scores = jnp.einsum("qhd,khd->hqk", queries, keyed, preferred_element_type=jnp.float32) * SCALE
    return jnp.where(allowed[None], scores, -1e30)


def layer_forward(block_rows, allowed, whole):
    (
        project_in,
        project_out,
        expand,
        contract,
        query_bias,
        value_bias,
        out_bias,
        expand_bias,
        contract_bias,
        first_gain,
        first_shift,
        second_gain,
        second_shift,
    ) = whole
    row_count = block_rows.shape[0]
    offsets = jnp.concatenate([query_bias, jnp.zeros_like(query_bias), value_bias]).astype(
        jnp.float32
    )
    projected = (
        jnp.dot(block_rows, project_in, preferred_element_type=jnp.float32) + offsets
    ).astype(jnp.bfloat16)
    queries, keyed, valued = split_heads(projected, row_count)
    scores = masked_scores(queries, keyed, allowed)
    highest = jnp.max(scores, axis=-1, keepdims=True)
    weights = jnp.exp(scores - highest)
    row_totals = jnp.sum(weights, axis=-1, keepdims=True)
    attention = (weights / row_totals).astype(jnp.bfloat16)
    log_total = highest + jnp.log(row_totals)
    attended = jnp.einsum("hqk,khd->qhd", attention, valued, preferred_element_type=jnp.float32)
    attended = attended.reshape(row_count, -1).astype(jnp.bfloat16)
    residual_one = (
        block_rows.astype(jnp.float32)
        + jnp.dot(attended, project_out, preferred_element_type=jnp.float32)
        + out_bias.astype(jnp.float32)
    )
    first_norm = normalize(
        residual_one, first_gain.astype(jnp.float32), first_shift.astype(jnp.float32)
    )
    first_low = first_norm.astype(jnp.bfloat16)
    expanded = jnp.dot(first_low, expand, preferred_element_type=jnp.float32) + expand_bias.astype(
        jnp.float32
    )
    active = exact_gelu(expanded).astype(jnp.bfloat16)
    residual_two = (
        first_norm
        + jnp.dot(active, contract, preferred_element_type=jnp.float32)
        + contract_bias.astype(jnp.float32)
    )
    result = normalize(
        residual_two, second_gain.astype(jnp.float32), second_shift.astype(jnp.float32)
    )
    kept = (projected, log_total, attended, residual_one, first_low, expanded, active, residual_two)
    return (result.astype(jnp.bfloat16), kept)


def layer_backward(block_rows, allowed, kept, whole, block_cot):
    (
        project_in,
        project_out,
        expand,
        contract,
        query_bias,
        value_bias,
        out_bias,
        expand_bias,
        contract_bias,
        first_gain,
        first_shift,
        second_gain,
        second_shift,
    ) = whole
    projected, log_total, attended, residual_one, first_low, expanded, active, residual_two = kept
    row_count = block_rows.shape[0]
    width = projected.shape[1] // 3
    unused, pull_second = jax.vjp(
        normalize, residual_two, second_gain.astype(jnp.float32), second_shift.astype(jnp.float32)
    )
    grad_second, grad_second_gain, grad_second_shift = pull_second(block_cot.astype(jnp.float32))
    grad_second_low = grad_second.astype(jnp.bfloat16)
    grad_contract = outer_sum(active, grad_second_low)
    grad_contract_bias = jnp.sum(grad_second_low.astype(jnp.float32), axis=0)
    unused_gelu, pull_gelu = jax.vjp(exact_gelu, expanded)
    grad_expanded = pull_gelu(through(grad_second_low, contract))[0].astype(jnp.bfloat16)
    grad_expand = outer_sum(first_low, grad_expanded)
    grad_expand_bias = jnp.sum(grad_expanded.astype(jnp.float32), axis=0)
    grad_first = grad_second + through(grad_expanded, expand)
    unused_first, pull_first = jax.vjp(
        normalize, residual_one, first_gain.astype(jnp.float32), first_shift.astype(jnp.float32)
    )
    grad_residual, grad_first_gain, grad_first_shift = pull_first(grad_first)
    grad_branch = grad_residual.astype(jnp.bfloat16)
    grad_project_out = outer_sum(attended, grad_branch)
    grad_out_bias = jnp.sum(grad_branch.astype(jnp.float32), axis=0)
    grad_attended = through(grad_branch, project_out).astype(jnp.bfloat16).reshape(row_count, H, HD)
    queries, keyed, valued = split_heads(projected, row_count)
    scores = masked_scores(queries, keyed, allowed)
    attention = jnp.exp(scores - log_total)
    grad_attention = jnp.einsum(
        "qhd,khd->hqk", grad_attended, valued, preferred_element_type=jnp.float32
    )
    grad_values = jnp.einsum(
        "hqk,qhd->khd",
        attention.astype(jnp.bfloat16),
        grad_attended,
        preferred_element_type=jnp.float32,
    )
    inner_sum = jnp.sum(attention * grad_attention, axis=-1, keepdims=True)
    grad_scores = (attention * (grad_attention - inner_sum)).astype(jnp.bfloat16)
    grad_queries = (
        jnp.einsum("hqk,khd->qhd", grad_scores, keyed, preferred_element_type=jnp.float32) * SCALE
    )
    grad_keys = (
        jnp.einsum("hqk,qhd->khd", grad_scores, queries, preferred_element_type=jnp.float32) * SCALE
    )
    grad_projected = jnp.concatenate(
        [
            grad_queries.reshape(row_count, -1),
            grad_keys.reshape(row_count, -1),
            grad_values.reshape(row_count, -1),
        ],
        axis=1,
    ).astype(jnp.bfloat16)
    grad_project_in = outer_sum(block_rows, grad_projected)
    column_sums = jnp.sum(grad_projected.astype(jnp.float32), axis=0)
    grad_rows = grad_residual + through(grad_projected, project_in)
    gradients = (
        grad_project_in,
        grad_project_out,
        grad_expand,
        grad_contract,
        column_sums[:width],
        column_sums[2 * width :],
        grad_out_bias,
        grad_expand_bias,
        grad_contract_bias,
        grad_first_gain,
        grad_first_shift,
        grad_second_gain,
        grad_second_shift,
    )
    return (grad_rows.astype(jnp.bfloat16), gradients)


def accumulate(running, gradients):
    if running is None:
        return gradients
    return tuple((left + right for left, right in zip(running, gradients)))


def body(
    tokens,
    seq_lengths,
    out_cotangent,
    project_in,
    project_out,
    expand,
    contract,
    query_bias,
    value_bias,
    out_bias,
    expand_bias,
    contract_bias,
    first_gain,
    first_shift,
    second_gain,
    second_shift,
):
    block_count = seq_lengths.shape[0]
    row_span = tokens.shape[0] // block_count
    masks = [
        segment_mask(seq_lengths[buffer_index], row_span) for buffer_index in range(block_count)
    ]
    outputs = []
    grad_list = []
    saved = []
    running = None
    for buffer_index in range(block_count):
        whole = (
            lax.all_gather(project_in, "fsdp", axis=0, tiled=True),
            lax.all_gather(project_out, "fsdp", axis=0, tiled=True),
            lax.all_gather(expand, "fsdp", axis=0, tiled=True),
            lax.all_gather(contract, "fsdp", axis=0, tiled=True),
            lax.all_gather(query_bias, "fsdp", axis=0, tiled=True),
            lax.all_gather(value_bias, "fsdp", axis=0, tiled=True),
            lax.all_gather(out_bias, "fsdp", axis=0, tiled=True),
            lax.all_gather(expand_bias, "fsdp", axis=0, tiled=True),
            lax.all_gather(contract_bias, "fsdp", axis=0, tiled=True),
            lax.all_gather(first_gain, "fsdp", axis=0, tiled=True),
            lax.all_gather(first_shift, "fsdp", axis=0, tiled=True),
            lax.all_gather(second_gain, "fsdp", axis=0, tiled=True),
            lax.all_gather(second_shift, "fsdp", axis=0, tiled=True),
        )
        block_rows = tokens[buffer_index * row_span : (buffer_index + 1) * row_span]
        result, kept = layer_forward(block_rows, masks[buffer_index], whole)
        outputs.append(result)
        saved.append(kept)
    for buffer_index in range(block_count):
        whole = (
            lax.all_gather(project_in, "fsdp", axis=0, tiled=True),
            lax.all_gather(project_out, "fsdp", axis=0, tiled=True),
            lax.all_gather(expand, "fsdp", axis=0, tiled=True),
            lax.all_gather(contract, "fsdp", axis=0, tiled=True),
            lax.all_gather(query_bias, "fsdp", axis=0, tiled=True),
            lax.all_gather(value_bias, "fsdp", axis=0, tiled=True),
            lax.all_gather(out_bias, "fsdp", axis=0, tiled=True),
            lax.all_gather(expand_bias, "fsdp", axis=0, tiled=True),
            lax.all_gather(contract_bias, "fsdp", axis=0, tiled=True),
            lax.all_gather(first_gain, "fsdp", axis=0, tiled=True),
            lax.all_gather(first_shift, "fsdp", axis=0, tiled=True),
            lax.all_gather(second_gain, "fsdp", axis=0, tiled=True),
            lax.all_gather(second_shift, "fsdp", axis=0, tiled=True),
        )
        block_rows = tokens[buffer_index * row_span : (buffer_index + 1) * row_span]
        block_cot = out_cotangent[buffer_index * row_span : (buffer_index + 1) * row_span]
        grad_rows, gradients = layer_backward(
            block_rows, masks[buffer_index], saved[buffer_index], whole, block_cot
        )
        grad_list.append(grad_rows)
        running = accumulate(running, gradients)
    owned = (
        lax.psum_scatter(running[0], "fsdp", scatter_dimension=0, tiled=True),
        lax.psum_scatter(running[1], "fsdp", scatter_dimension=0, tiled=True),
        lax.psum_scatter(running[2], "fsdp", scatter_dimension=0, tiled=True),
        lax.psum_scatter(running[3], "fsdp", scatter_dimension=0, tiled=True),
        lax.psum_scatter(running[4], "fsdp", scatter_dimension=0, tiled=True),
        lax.psum_scatter(running[5], "fsdp", scatter_dimension=0, tiled=True),
        lax.psum_scatter(running[6], "fsdp", scatter_dimension=0, tiled=True),
        lax.psum_scatter(running[7], "fsdp", scatter_dimension=0, tiled=True),
        lax.psum_scatter(running[8], "fsdp", scatter_dimension=0, tiled=True),
        lax.psum_scatter(running[9], "fsdp", scatter_dimension=0, tiled=True),
        lax.psum_scatter(running[10], "fsdp", scatter_dimension=0, tiled=True),
        lax.psum_scatter(running[11], "fsdp", scatter_dimension=0, tiled=True),
        lax.psum_scatter(running[12], "fsdp", scatter_dimension=0, tiled=True),
    )
    reduced = (
        lax.psum(owned[0].astype(jnp.bfloat16), "rep").astype(jnp.float32),
        lax.psum(owned[1].astype(jnp.bfloat16), "rep").astype(jnp.float32),
        lax.psum(owned[2].astype(jnp.bfloat16), "rep").astype(jnp.float32),
        lax.psum(owned[3].astype(jnp.bfloat16), "rep").astype(jnp.float32),
        lax.psum(owned[4].astype(jnp.bfloat16), "rep").astype(jnp.float32),
        lax.psum(owned[5].astype(jnp.bfloat16), "rep").astype(jnp.float32),
        lax.psum(owned[6].astype(jnp.bfloat16), "rep").astype(jnp.float32),
        lax.psum(owned[7].astype(jnp.bfloat16), "rep").astype(jnp.float32),
        lax.psum(owned[8].astype(jnp.bfloat16), "rep").astype(jnp.float32),
        lax.psum(owned[9].astype(jnp.bfloat16), "rep").astype(jnp.float32),
        lax.psum(owned[10].astype(jnp.bfloat16), "rep").astype(jnp.float32),
        lax.psum(owned[11].astype(jnp.bfloat16), "rep").astype(jnp.float32),
        lax.psum(owned[12].astype(jnp.bfloat16), "rep").astype(jnp.float32),
    )
    return (
        jnp.concatenate(outputs, axis=0),
        jnp.concatenate(grad_list, axis=0),
        reduced[0],
        reduced[1],
        reduced[2],
        reduced[3],
        reduced[4],
        reduced[5],
        reduced[6],
        reduced[7],
        reduced[8],
        reduced[9],
        reduced[10],
        reduced[11],
        reduced[12],
    )


def solution(mesh):
    return jax.shard_map(
        body,
        mesh=mesh,
        in_specs=(
            P(("fsdp", "rep"), None),
            P(("fsdp", "rep"), None),
            P(("fsdp", "rep"), None),
            P("fsdp", None),
            P("fsdp", None),
            P("fsdp", None),
            P("fsdp", None),
            P("fsdp"),
            P("fsdp"),
            P("fsdp"),
            P("fsdp"),
            P("fsdp"),
            P("fsdp"),
            P("fsdp"),
            P("fsdp"),
            P("fsdp"),
        ),
        out_specs=(
            P(("fsdp", "rep"), None),
            P(("fsdp", "rep"), None),
            P("fsdp", None),
            P("fsdp", None),
            P("fsdp", None),
            P("fsdp", None),
            P("fsdp"),
            P("fsdp"),
            P("fsdp"),
            P("fsdp"),
            P("fsdp"),
            P("fsdp"),
            P("fsdp"),
            P("fsdp"),
            P("fsdp"),
        ),
        check_vma=False,
    )
```

profile of v0, /device:TPU:0, one launch (start us, length us, event | category | flops | bytes accessed | tf_op | source)
XLA Modules:
  0.0 1068.1 jit_solution(15132398910199987622)
XLA Ops:
  20.7 63.9 %all-reduce.18 = (bf16[1024]{0:T(1024)(128)(2,1)S(1)}, bf16[1024]{0:T(1024)(128)(2,1)S(1)}, bf16[1024]{0:T(1024)(128)(2,1)S(1)}, bf16[1024]{0:T(1024)(128)(2,1)S...) all-reduce(bf16[1024]{0:T(1024)(128)(2,1)S(1)} %dynamic-update-slic, ...), channel_id=1, replica_groups=mesh['fsdp'=16,'rep'=2] {'fsdp'}, use_global_device_ids=true, to_apply=%add.1 | all-reduce | flops 8192 | bytes 32768
  86.3 17.1 %all-gather = bf16[16,1,256]{2,1,0:T(2,128)(2,1)S(1)} all-gather(bf16[1,1,256]{2,1,0:T(2,128)(2,1)S(1)} %reshape.459), channel_id=1, replica_groups=mesh['fsdp'=16,'rep'=2] {'fsdp'}, dimensions={0}, use_global_device_ids=true | all-gather | bytes 8704 | tf_op jit(solution)/shard_map/all_gather | solution.py:250
  149.1 9.6 fusion.35
  164.0 18.2 %fusion.71 = (f32[16,512]{1,0:T(8,128)S(1)}, f32[16,512,512]{1,2,0:T(8,128)}) fusion(bf16[512,16,64]{0,2,1:T(8,128)(2,1)S(1)} %bitcast.114, bf16[512,16,64]{0,2,1:T(8,128)(2,1)S(1)} %bitcast.107, pred[512,512]{0,1:T(8,128)(4,1)S(1)} %fusion.42), kind=kOutput, calls=%fused_computation.190 | convolution fusion | flops 549445632 | bytes 19169280 | tf_op jit(solution)/shard_map/qhd,khd->hqk/dot_general | solution.py:59
  212.2 49.0 %multiply_convert_fusion.3 = (bf16[512,4096]{1,0:T(8,128)(2,1)}, f32[512,4096]{1,0:T(8,128)}, bf16[512,4096]{1,0:T(8,128)(2,1)}, f32[512,4096]{1,0:T(8,128)}, f32[512,4096]{1,0:T(8,128)}) fusion(f32[4096]{0:T(1024)S(1)} %bitcast.142, f32[512,4096]{1,0:T(8,128)S(1)} %fusion.54, bf16[1024,4096]{1,0:T(8,128)(2,1)S(1)} %copy-done.77, ...), kind=kOutput, calls=%fused_computation.42 | convolution fusion | flops 4574412800 | bytes 52457472 | tf_op jit(solution)/shard_map/dot_general | solution.py:104
  268.9 10.0 fusion.74
  299.1 26.9 %convert_reduce_fusion.1 = (f32[4096]{0:T(1024)}, bf16[512,4096]{1,0:T(8,128)(2,1)}, f32[4096]{0:T(1024)}, bf16[512,4096]{1,0:T(8,128)(2,1)}) fusion(f32[512,4096]{1,0:T(8,128)} %get-tuple-element.144, f32[512,4096]{1,0:T(8,128)} %get-tuple-element.181, f32[4096]{0:T(1024)S(1)} %bitcast.143, f32[512,4096]{1,0:T(8,128)} %fusion.75, ...), kind=kOutput, calls=%fused_computation.24 | convolution fusion | flops 4366262272 | bytes 59817984 | tf_op jit(solution)/shard_map/dot_general | solution.py:41
  326.0 9.8 add_add_fusion.8
  335.9 12.0 %multiply_reduce_fusion.3 = (f32[1024]{0:T(1024)}, f32[512]{0:T(512)S(1)}, f32[1024]{0:T(1024)}, f32[1024]{0:T(1024)}, f32[512]{0:T(512)S(1)}, /*index=5*/f32[1024]{0:T(1024)}, f32[512,1024]{1,0:T(8,128)}) fusion(f32[512,1024]{1,0:T(8,128)S(1)} %copy-done.5, f32[512]{0:T(512)S(1)} %fusion.49, f32[512]{0:T(512)S(1)} %broadcast_multiply_fusion.3, ...), kind=kOutput, calls=%fused_computation.89 | convolution fusion | flops 4304399360 | bytes 23103488 | tf_op jit(solution)/shard_map/dot_general | solution.py:41
  358.2 15.3 %multiply_reduce_fusion.1 = (f32[16,512]{1,0:T(8,128)}, f32[16,512,512]{1,2,0:T(8,128)}) fusion(f32[16,512,512]{1,2,0:T(8,128)} %get-tuple-element.174, f32[16,512]{1,0:T(8,128)} %log_add_fusion.1, bf16[512,16,64]{0,2,1:T(8,128)(2,1)S(1)} %bitcast.121, bf16[512,16,64]{0,2,1:T(8,128)(2,1)} %bitcast.138), kind=kOutput, calls=%fused_computation.4 | convolution fusion | flops 549445632 | bytes 35717120 | tf_op jit(solution)/shard_map/qhd,khd->hqk/dot_general | solution.py:162
  375.3 10.6 multiply_convert_fusion.1
  405.5 11.5 %multiply_reduce_fusion = (f32[16,512]{1,0:T(8,128)S(1)}, f32[16,512,512]{1,2,0:T(8,128)}) fusion(f32[16,512,512]{1,2,0:T(8,128)} %get-tuple-element.178, f32[16,512]{1,0:T(8,128)S(1)} %copy-done.43, bf16[512,16,64]{0,2,1:T(8,128)(2,1)S(1)} %bitcast.123, bf16[512,16,64]{0,2,1:T(8,128)(2,1)S(1)} %bitcast.134), kind=kOutput, calls=%fused_computation.1 | convolution fusion | flops 549445632 | bytes 35717120 | tf_op jit(solution)/shard_map/qhd,khd->hqk/dot_general | solution.py:162
  417.0 16.5 %multiply_convert_fusion = bf16[16,512,512]{1,2,0:T(8,128)(2,1)} fusion(f32[16,512,512]{1,2,0:T(8,128)} %get-tuple-element.188, f32[16,512,512]{1,2,0:T(8,128)} %get-tuple-element.178, f32[16,512]{1,0:T(8,128)S(1)} %get-tuple-element.187, f32[16,512]{1,0:T(8,128)S(1)} %copy-done.43), kind=kLoop, calls=%fused_computation | loop fusion | flops 16777216 | bytes 42008576 | tf_op jit(solution)/shard_map/convert_element_type | solution.py:172
  467.2 11.9 %add_bitcast_fusion = f32[1024,3072]{0,1:T(8,128)} fusion(f32[3072,1024]{1,0:T(8,128)S(1)} %fusion.46, bf16[1024,1024]{1,0:T(8,128)(2,1)} %param.16, bf16[512,1024]{0,1:T(8,128)(2,1)S(1)} %bitcast.116, bf16[512,1024]{0,1:T(8,128)(2,1)S(1)} %bitcast.111, bf16[512,1024]{0,1:T(8,128)(2,1)S(1)} %bitcast.104), kind=kOutput, calls=%fused_computation.16 | convolution fusion | flops 3233808384 | bytes 29360128 | tf_op jit(solution)/shard_map/dot_general | solution.py:35
  479.1 12.6 %copy.115 = f32[1024,3072]{1,0:T(8,128)} copy(f32[1024,3072]{0,1:T(8,128)} %add_bitcast_fusion) | data formatting | bytes 25165824
  492.3 15.9 %fusion.56 = f32[1024,4096]{1,0:T(8,128)} fusion(bf16[512,4096]{1,0:T(8,128)(2,1)} %get-tuple-element.130, f32[512,1024]{1,0:T(8,128)} %copy-done.3, f32[1024]{0:T(1024)S(1)} %copy-done.46, f32[1024]{0:T(1024)S(1)} %convert_element_type.261, f32[512]{0:T(512)S(1)} %copy-done.66, f32[512]{0:T(512)S(1)} %copy-done.49), kind=kOutput, calls=%fused_computation.179 | convolution fusion | flops 4297588736 | bytes 23080960 | tf_op jit(solution)/shard_map/dot_general | solution.py:35
  508.2 13.7 %convolution_add_fusion = f32[1024,4096]{1,0:T(8,128)} fusion(f32[1024,4096]{1,0:T(8,128)} %fusion.56, bf16[512,4096]{1,0:T(8,128)(2,1)S(1)} %copy-done.32, f32[512,1024]{1,0:T(8,128)S(1)} %copy-done.2, f32[512]{0:T(512)S(1)} %fusion.51, f32[512]{0:T(512)S(1)} %broadcast_multiply_fusion.1, f32[1024]{0:T(1024)S(1)} %copy-done.46, ...), kind=kOutput, calls=%fused_computation.59 | convolution fusion | flops 4301783040 | bytes 39858176 | tf_op jit(solution)/shard_map/dot_general | solution.py:35
  523.1 12.0 %fusion.77 = f32[4096,1024]{1,0:T(8,128)} fusion(bf16[512,4096]{1,0:T(8,128)(2,1)} %get-tuple-element.143, bf16[512,1024]{1,0:T(8,128)(2,1)S(1)} %copy-done.40), kind=kOutput, calls=%fused_computation.196 | convolution fusion | flops 4294967296 | bytes 22020096 | tf_op jit(solution)/shard_map/dot_general | solution.py:35
  535.1 11.6 %convolution_add_fusion.1 = f32[4096,1024]{1,0:T(8,128)} fusion(f32[4096,1024]{1,0:T(8,128)} %fusion.77, bf16[512,4096]{1,0:T(8,128)(2,1)S(1)} %copy-done.28, bf16[512,1024]{1,0:T(8,128)(2,1)S(1)} %copy-done.37), kind=kOutput, calls=%fused_computation.64 | convolution fusion | flops 4299161600 | bytes 38797312 | tf_op jit(solution)/shard_map/dot_general | solution.py:35
  551.9 62.3 %all-reduce.17 = (bf16[1024]{0:T(1024)(128)(2,1)S(1)}, bf16[1024]{0:T(1024)(128)(2,1)S(1)}, bf16[1024]{0:T(1024)(128)(2,1)S(1)}, bf16[4096]{0:T(1024)(128)(2,1)S...) all-reduce(f32[1024]{0:T(1024)S(1)} %get-tuple-element.159, ...), channel_id=6, replica_groups=mesh['fsdp'=16,'rep'=2] {'fsdp'}, use_global_device_ids=true, to_apply=%region_36.37.clone | all-reduce | flops 12288 | bytes 73728
  624.7 8.9 add_convert_fusion.5
  637.5 170.7 %reduce-scatter.9.cloned.1.call-done = f32[64,4096]{1,0:T(8,128)} async-done(((f32[1024,4096]{1,0:T(8,128)}), f32[64,4096]{1,0:T(8,128)}) %reduce-scatter.9.cloned.1.call-update) | async-done | bytes 1048592 | tf_op jit(solution)/shard_map/reduce_scatter | solution.py:287
  810.3 180.2 %reduce-scatter.11.cloned.1.call-done = f32[256,1024]{1,0:T(8,128)} async-done(((f32[4096,1024]{1,0:T(8,128)}), f32[256,1024]{1,0:T(8,128)}) %reduce-scatter.11.cloned.1.call-update) | async-done | bytes 1048592 | tf_op jit(solution)/shard_map/reduce_scatter | solution.py:288
  1004.8 48.5 %all-reduce.23.cloned.1.call-done = (bf16[64,3072]{0,1:T(8,128)(2,1)}, bf16[64,1024]{1,0:T(8,128)(2,1)}, bf16[64,4096]{1,0:T(8,128)(2,1)}, bf16[256,1024]{1,0:T(8,128)(2,1)}) async-done(((bf16[64,3072]{0,1:T(8,128)(2,1)}, bf16[64,1024]{1,0:T(8,128)(2,1)}, bf16[64,4096]{1,0:T(8,128)(2,1)}, bf16[256,1024]{1,0:T(8,128)(2,1)}), (bf16[64,3072]{0,1:T(8,128)(2,1)}, bf16[64,1024]{1,0:T(8,128)(2,1)}, ...) | async-done | bytes 1572880 | tf_op jit(solution)/shard_map/psum | solution.py:300
  (338 shorter events, 232.3 us)
Async XLA Ops:
  7.2 97.6 %all-gather.6.cloned.1.call-start = ((), (), s32[]{:S(2)}) async-start(), calls=%async_computation.4 | async-start | bytes 6684672 | tf_op jit(solution)/shard_map/all_gather | solution.py:243
  7.9 150.8 %all-gather.8.cloned.1.call-start = ((), (), s32[]{:S(2)}) async-start(), calls=%async_computation.5 | async-start | bytes 2228224 | tf_op jit(solution)/shard_map/all_gather | solution.py:244
  8.7 192.3 %all-gather.10.cloned.1.call-start = ((), (), s32[]{:S(2)}) async-start(), calls=%async_computation.6 | async-start | bytes 8912896 | tf_op jit(solution)/shard_map/all_gather | solution.py:245
  9.4 259.4 %all-gather.12.cloned.1.call-start = ((), (), s32[]{:S(2)}) async-start(), calls=%async_computation.7 | async-start | bytes 8912896 | tf_op jit(solution)/shard_map/all_gather | solution.py:246
  10.0 623.6 %reduce-scatter.7.cloned.1.call-start = ((), (), s32[]{:S(2)}) async-start(), calls=%async_computation.8 | async-start | bytes 4456448 | tf_op jit(solution)/shard_map/reduce_scatter | solution.py:286
  84.6 194.7 %copy-start.45 = (f32[1024]{0:T(1024)}, f32[1024]{0:T(1024)S(1)}, u32[]{:S(2)}) copy-start(f32[1024]{0:T(1024)S(1)} %convert_element_type.262) | copy-start | bytes 12292
  113.6 50.4 %copy-start.6 = (bf16[512,1024]{0,1:T(8,128)(2,1)}, bf16[512,1024]{0,1:T(8,128)(2,1)S(1)}, u32[]{:S(2)}) copy-start(bf16[512,1024]{0,1:T(8,128)(2,1)S(1)} %copy.96) | copy-start | bytes 3145732
  115.5 48.5 %copy-start.12 = (bf16[512,1024]{0,1:T(8,128)(2,1)}, bf16[512,1024]{0,1:T(8,128)(2,1)S(1)}, u32[]{:S(2)}) copy-start(bf16[512,1024]{0,1:T(8,128)(2,1)S(1)} %copy.95) | copy-start | bytes 3145732
  162.3 185.6 %copy-start.48 = (f32[512]{0:T(512)}, f32[512]{0:T(512)S(1)}, u32[]{:S(2)}) copy-start(f32[512]{0:T(512)S(1)} %broadcast_multiply_fusion.3) | copy-start | bytes 6148
  164.0 18.3 %copy-start.50 = (f32[512]{0:T(512)}, f32[512]{0:T(512)S(1)}, u32[]{:S(2)}) copy-start(f32[512]{0:T(512)S(1)} %multiply_reduce_fusion.9) | copy-start | bytes 6148
  164.0 183.9 %copy-start.65 = (f32[512]{0:T(512)}, f32[512]{0:T(512)S(1)}, u32[]{:S(2)}) copy-start(f32[512]{0:T(512)S(1)} %fusion.49) | copy-start | bytes 6148
  200.6 147.3 %copy-start.1 = (f32[512,1024]{1,0:T(8,128)}, f32[512,1024]{1,0:T(8,128)S(1)}, u32[]{:S(2)}) copy-start(f32[512,1024]{1,0:T(8,128)S(1)} %get-tuple-element.180) | copy-start | bytes 6291460
  212.2 56.7 %copy-start.76 = (f32[1024]{0:T(1024)S(1)}, f32[1024]{0:T(1024)}, u32[]{:S(2)}) copy-start(f32[1024]{0:T(1024)} %convert_element_type.266) | copy-start | bytes 12292
  358.2 17.1 %slice-start.3 = ((s8[16777216]{0:T(1024)(128)(4,1)}), s8[4194304]{0:T(1024)(128)(4,1)S(1)}, s32[]{:S(2)}) async-start(s8[16777216]{0:T(1024)(128)(4,1)} %bitcast.100), calls=%async_computation.16 | async-start | bytes 8388608
  405.4 229.8 %reduce-scatter.13.cloned.1.call-start = ((), (), s32[]{:S(2)}) async-start(), calls=%async_computation.11 | async-start | bytes 13369344
  417.0 29.3 %slice-start.4 = ((s8[16777216]{0:T(1024)(128)(4,1)}), s8[4194304]{0:T(1024)(128)(4,1)S(1)}, s32[]{:S(2)}) async-start(s8[16777216]{0:T(1024)(128)(4,1)} %bitcast.102), calls=%async_computation.17 | async-start | bytes 8388608
  417.0 29.3 %slice-start.5 = ((s8[16777216]{0:T(1024)(128)(4,1)}), s8[4194304]{0:T(1024)(128)(4,1)S(1)}, s32[]{:S(2)}) async-start(s8[16777216]{0:T(1024)(128)(4,1)} %bitcast.102), calls=%async_computation.18 | async-start | bytes 8388608
  417.0 29.3 %slice-start.6 = ((s8[16777216]{0:T(1024)(128)(4,1)}), s8[4194304]{0:T(1024)(128)(4,1)S(1)}, s32[]{:S(2)}) async-start(s8[16777216]{0:T(1024)(128)(4,1)} %bitcast.102), calls=%async_computation.19 | async-start | bytes 8388608
  491.7 16.5 %copy-start.2 = (f32[512,1024]{1,0:T(8,128)S(1)}, f32[512,1024]{1,0:T(8,128)}, u32[]{:S(2)}) copy-start(f32[512,1024]{1,0:T(8,128)} %copy-done.1) | copy-start | bytes 6291460
  491.7 316.5 %reduce-scatter.9.cloned.1.call-start = ((), (), s32[]{:S(2)}) async-start(), calls=%async_computation.9 | async-start | bytes 17825792 | tf_op jit(solution)/shard_map/reduce_scatter | solution.py:287
  521.9 468.5 %reduce-scatter.11.cloned.1.call-start = ((), (), s32[]{:S(2)}) async-start(), calls=%async_computation.10 | async-start | bytes 17825792 | tf_op jit(solution)/shard_map/reduce_scatter | solution.py:288
  546.8 77.8 %copy-start.71 = (f32[512]{0:T(512)S(1)}, f32[512]{0:T(512)}, u32[]{:S(2)}) copy-start(f32[512]{0:T(512)} %copy-done.70) | copy-start | bytes 6148
  546.9 506.4 %all-reduce.23.cloned.1.call-start = ((), (), s32[]{:S(2)}) async-start(), calls=%async_computation.12 | async-start | bytes 3932160 | tf_op jit(solution)/shard_map/psum | solution.py:300
  633.6 362.1 %copy-start.69 = (f32[512]{0:T(512)S(1)}, f32[512]{0:T(512)}, u32[]{:S(2)}) copy-start(f32[512]{0:T(512)} %copy-done.68) | copy-start | bytes 6148
  (73 other events, 440.3 us)
Sparse Core Ops, SparseCore 0:
  10.3 65.2 all-gather.5
  77.7 40.0 all-gather.7
  119.9 73.6 all-gather.9
  195.7 73.1 all-gather.11
  405.5 70.5 reduce-scatter.6
  491.8 133.8 reduce-scatter.12
  630.4 177.7 reduce-scatter.8
  812.9 177.5 reduce-scatter.10
  993.7 59.5 all-reduce.22
where the time goes:
time: 1070 us
  waiting for transfers between devices  410 us (38%)
  matrix products  352 us (33%)
  blocking collectives  148 us (14%)
  other arithmetic  87.9 us (8%)
  local copies, waits for them, and re-layouts  52.7 us (5%)
  between operations  17.3 us (2%)
    reduce_scatter x1, waiting for transfers between devices, body(): lax.psum_scatter(running[3], 'fsdp', scatter_dimension=0, tiled=True)  180 us
    reduce_scatter x1, waiting for transfers between devices, body(): lax.psum_scatter(running[2], 'fsdp', scatter_dimension=0, tiled=True)  171 us
    unnamed x2, blocking collectives  126 us
    dot_general x8, matrix products, outer_sum(): lax.dot_general(left, right, (((0,), (0,)), ((), ())), preferred_element_...  80.2 us
    dot_general x8, matrix products, through(): lax.dot_general(gradient, weight, (((1,), (1,)), ((), ())), preferred_ele...  74.8 us
    dot_general x2, matrix products, layer_forward(): jnp.dot(first_low, expand, preferred_element_type=jnp.float32)  56.8 us
    psum x1, waiting for transfers between devices, body(): lax.psum(owned[0].astype(jnp.bfloat16), 'rep').astype(jnp.float32)  48.5 us
    unnamed x207, local copies, waits for them, and re-layouts  37.1 us
  transfers between devices with their start and end apart: 9, of which 4 were waited for; matrix products, arithmetic and copies ran while one was open for 32% of the time, Pallas kernels for 0%

commit v1 on v0

v1 whole, which is shorter than its diff:
```python
import functools

import jax
import jax.numpy as jnp
from jax import lax
from jax.experimental import pallas as pl
from jax.experimental.pallas import tpu as pltpu
from jax.sharding import PartitionSpec as P

H = 16
HD = 64
SLOTS = 4
CAP = 512
EPSILON = 1e-12
SCALE = 0.125
BIG = 1e30
LOW = jnp.bfloat16
F32 = jnp.float32
VMEM_LIMIT = 60 * 1024 * 1024
ANY = pl.BlockSpec(memory_space=pl.ANY)
OWN, ACROSS, OTHER, CORNER = (0, 0), (1, 0), (0, 1), (1, 1)
GROUPS = (OWN, ACROSS, OTHER, CORNER)


def params(limit=VMEM_LIMIT):
    return pltpu.CompilerParams(vmem_limit_bytes=limit, dimension_semantics=("arbitrary",))


def dot(left, right, over):
    return lax.dot_general(left, right, ((over[:1], over[1:]), ((), ())), preferred_element_type=F32)


def nn(left, right):
    return dot(left, right, (1, 0))


def nt(left, right):
    return dot(left, right, (1, 1))


def tn(left, right):
    return dot(left, right, (0, 0))


class Plan:
    def __init__(self, shards, copies):
        self.shards, self.copies = shards, copies
        self.split = shards == 16 and copies == 2

    def flip(self, value, bits):
        return lax.ppermute(value, "fsdp", [(i, i ^ bits) for i in range(self.shards)])

    def other_copy(self, value):
        return lax.ppermute(value, "rep", [(0, 1), (1, 0)])

    def gather(self, shard):
        if not self.split:
            return [lax.all_gather(shard, "fsdp", axis=0, tiled=True)]
        half = shard.shape[0] // 2
        rep = lax.axis_index("rep")
        own = lax.dynamic_slice_in_dim(shard, rep * half, half, 0)
        own = jnp.concatenate([own] + [self.flip(own, 4 * k) for k in (1, 2, 3)], axis=0)
        across = self.flip(own, 2)
        other = self.other_copy(own)
        corner_a = self.flip(other[: 2 * half], 2)
        corner_b = self.other_copy(across[2 * half :])
        pieces = [own, across, other, corner_a, corner_b]
        return pieces + [self.flip(piece, 1) for piece in pieces]

    def piece_list(self):
        out = []
        for core in (0, 1):
            for piece, (group, first, count) in enumerate(
                ((OWN, 0, 4), (ACROSS, 0, 4), (OTHER, 0, 4), (CORNER, 0, 2), (CORNER, 2, 2))
            ):
                for k in range(count):
                    out.append((piece + 5 * core, k, first + k, group[0], core, group[1]))
        return out

    def scatter(self, mine, theirs):
        half = mine.shape[0] // 16
        rep = lax.axis_index("rep")
        got = self.flip(theirs, 1)

        def part(group, first=0, count=4):
            start = (GROUPS.index(group) * 4 + first) * half
            stop = start + count * half
            return mine[start:stop].astype(F32) + got[start:stop].astype(F32)

        corner_a = self.flip(part(CORNER, 0, 2).astype(LOW), 2)
        corner_b = self.other_copy(part(CORNER, 2, 2).astype(LOW))
        other = jnp.concatenate(
            [part(OTHER, 0, 2) + corner_a.astype(F32), part(OTHER, 2, 2)], axis=0
        ).astype(LOW)
        across = jnp.concatenate(
            [part(ACROSS, 0, 2), part(ACROSS, 2, 2) + corner_b.astype(F32)], axis=0
        ).astype(LOW)
        own = part(OWN) + self.flip(across, 2).astype(F32) + self.other_copy(other).astype(F32)
        total = own[:half]
        low = own.astype(LOW)
        for k in (1, 2, 3):
            total = total + self.flip(low[k * half : (k + 1) * half], 4 * k).astype(F32)
        total = total.astype(LOW)
        away = self.other_copy(total)
        first = jnp.where(rep == 0, total, away)
        second = jnp.where(rep == 0, away, total)
        return jnp.concatenate([first, second], axis=0).astype(F32)


def place():
    shard = lax.axis_index("fsdp")
    return jnp.stack([shard // 4, (shard // 2) % 2, shard % 2, lax.axis_index("rep")]).astype(jnp.int32)


def load_copies(plan, at, pieces, target, sems, rows):
    if not plan.split:
        return [pltpu.make_async_copy(pieces[0], target, sems)]
    half = rows // plan.shards // 2
    copies = []
    for piece, k, dz, dx, dc, dy in plan.piece_list():
        shard = (at[0] ^ dz) * 4 + (at[1] ^ dx) * 2 + (at[2] ^ dc)
        row = pl.multiple_of(shard * 2 * half + (at[3] ^ dy) * half, half)
        copies.append(
            pltpu.make_async_copy(
                pieces[piece].at[pl.ds(k * half, half)], target.at[pl.ds(row, half)], sems
            )
        )
    return copies


def fetch(plan, at, groups, sems):
    started = []
    for index, (pieces, target, rows) in enumerate(groups):
        for copy in load_copies(plan, at, pieces, target, sems.at[index], rows):
            copy.start()
            started.append(copy)
    for copy in started:
        copy.wait()


def project_kernel(plan, count, at, rows_ref, bias_ref, *refs):
    pieces, (out_ref, weight, sems) = refs[:count], refs[count:]

    @pl.when(pl.program_id(0) == 0)
    def _():
        fetch(plan, at, [(pieces, weight, weight.shape[0])], sems)

    out_ref[...] = (nn(rows_ref[...], weight[...]) + bias_ref[0:1].astype(F32)).astype(LOW)


def project(plan, at, rows, bias, pieces, depth, width, tile=256):
    count = len(pieces)
    return pl.pallas_call(
        functools.partial(project_kernel, plan, count),
        out_shape=jax.ShapeDtypeStruct((rows.shape[0], width), LOW),
        grid_spec=pltpu.PrefetchScalarGridSpec(
            num_scalar_prefetch=1,
            grid=(rows.shape[0] // tile,),
            in_specs=[
                pl.BlockSpec((tile, depth), lambda i, at: (i, 0)),
                pl.BlockSpec((1, width), lambda i, at: (0, 0)),
            ]
            + [ANY] * count,
            out_specs=pl.BlockSpec((tile, width), lambda i, at: (i, 0)),
            scratch_shapes=[pltpu.VMEM((depth, width), LOW), pltpu.SemaphoreType.DMA((1,))],
        ),
        compiler_params=params(),
        cost_estimate=pl.CostEstimate(
            flops=2 * rows.shape[0] * depth * width, bytes_accessed=2 * depth * width, transcendentals=0
        ),
    )(at, rows, bias, *pieces)


def slot_rows(lengths_ref, block, row_count):
    along = lax.broadcasted_iota(jnp.int32, (1, row_count), 1)
    down = lax.broadcasted_iota(jnp.int32, (row_count, 1), 0)
    bound, lane_slot, row_slot = 0, jnp.zeros_like(along), jnp.zeros_like(down)
    for slot in range(SLOTS):
        bound = bound + lengths_ref[block, slot]
        lane_slot = lane_slot + (along >= bound).astype(jnp.int32)
        row_slot = row_slot + (down >= bound).astype(jnp.int32)
    return lane_slot, row_slot


def query_rows(lane_slot):
    line = lax.broadcasted_iota(jnp.int32, (8, lane_slot.shape[1]), 0)
    return jnp.where(line == lane_slot, -BIG, 0.0)


def key_columns(row_slot, offset):
    column = lax.broadcasted_iota(jnp.int32, (row_slot.shape[0], 128), 1) - offset
    barred = (column >= 0) & (column <= SLOTS) & ((column != row_slot) | (row_slot == SLOTS))
    return jnp.where(barred, 1.0, 0.0).astype(LOW)


def attend_kernel(lengths_ref, q_ref, k_ref, v_ref, out_ref, log_ref):
    block = pl.program_id(0) // (H // 2)
    row_count = q_ref.shape[0]
    lane_slot, row_slot = slot_rows(lengths_ref, block, row_count)
    inside = lane_slot < SLOTS
    lane = lax.broadcasted_iota(jnp.int32, (row_count, 128), 1)
    barred = query_rows(lane_slot).astype(LOW)
    padded = jnp.concatenate([barred, jnp.zeros((HD - 8, row_count), LOW)], axis=0)
    q_turned = (q_ref[...].astype(F32) * SCALE).T.astype(LOW)
    v_turned = v_ref[...].astype(F32).T
    v_low = v_turned.astype(LOW)
    ones = jnp.ones((16, row_count), LOW)
    results = []
    for head in range(2):
        own = (lane < HD) if head == 0 else (lane >= HD)
        keyed = jnp.where(own, k_ref[...], key_columns(row_slot, HD * (1 - head)))
        half = q_turned[head * HD : (head + 1) * HD]
        query = jnp.concatenate([half, padded] if head == 0 else [padded, half], axis=0)
        scores = nn(keyed, query)
        highest = jnp.max(scores, axis=0, keepdims=True)
        weights = jnp.exp(scores - highest)
        low = weights.astype(LOW)
        values = jnp.concatenate([v_low[head * HD : (head + 1) * HD], ones], axis=0)
        mixed = nn(values, low)
        total = mixed[HD : HD + 1]
        result = mixed[:HD] / total
        results.append(jnp.where(inside, result, v_turned[head * HD : (head + 1) * HD]))
        log_ref[0, head : head + 1] = jnp.where(inside, highest + jnp.log(total), BIG)
    out_ref[...] = jnp.concatenate(results, axis=0).T.astype(LOW)


def attend(lengths, projected):
    rows = projected.shape[0]
    blocks, pairs = rows // CAP, H // 2
    width = H * HD

    def column(part):
        return pl.BlockSpec((CAP, 128), lambda i, n: (i // pairs, part * pairs + i % pairs))

    return pl.pallas_call(
        attend_kernel,
        out_shape=(
            jax.ShapeDtypeStruct((rows, width), LOW),
            jax.ShapeDtypeStruct((blocks * pairs, 8, CAP), F32),
        ),
        grid_spec=pltpu.PrefetchScalarGridSpec(
            num_scalar_prefetch=1,
            grid=(blocks * pairs,),
            in_specs=[column(0), column(1), column(2)],
            out_specs=(column(0), pl.BlockSpec((1, 8, CAP), lambda i, n: (i, 0, 0))),
        ),
        compiler_params=params(),
        cost_estimate=pl.CostEstimate(
            flops=4 * 4 * rows * CAP * width, bytes_accessed=8 * rows * width, transcendentals=rows * CAP * H
        ),
    )(lengths, projected, projected, projected)


def three(value):
    first = value.astype(LOW).astype(F32)
    rest = value - first
    second = rest.astype(LOW).astype(F32)
    return first, second, rest - second


def attend_back_kernel(lengths_ref, q_ref, k_ref, v_ref, att_ref, grad_ref, log_ref, dq_ref, dk_ref, dv_ref):
    block = pl.program_id(0) // (H // 2)
    row_count = q_ref.shape[0]
    lane_slot, row_slot = slot_rows(lengths_ref, block, row_count)
    outside = row_slot >= SLOTS
    lane = lax.broadcasted_iota(jnp.int32, (row_count, 128), 1)
    barred = query_rows(lane_slot)
    q_scaled = (q_ref[...].astype(F32) * SCALE)
    q_turned = q_scaled.T.astype(LOW)
    k_scaled = k_ref[...].astype(F32) * SCALE
    k_turned = k_scaled.T.astype(LOW)
    grads = grad_ref[...]
    grad_wide = grads.astype(F32)
    grad_turned = grad_wide.T
    mixed = grad_turned * att_ref[...].astype(F32).T
    grad_turned = grad_turned.astype(LOW)
    q_low = q_scaled.astype(LOW)
    line = lax.broadcasted_iota(jnp.int32, (8, row_count), 0)
    none = jnp.zeros((HD - 16, row_count), F32)

    def lines(value):
        first, second, third = three(value)
        return jnp.where(
            line == 0, -first, jnp.where(line == 1, -second, jnp.where(line == 2, -third, 0.0))
        )

    dqs, dks, dvs = [], [], []
    for head in range(2):
        own = (lane < HD) if head == 0 else (lane >= HD)
        start = HD * (1 - head)
        unit = (lane >= start + 8) & (lane < start + 11)
        keyed = jnp.where(own, k_ref[...], jnp.where(unit, jnp.ones((), LOW), key_columns(row_slot, start)))
        valued = jnp.where(own, v_ref[...], jnp.where(unit, jnp.ones((), LOW), jnp.zeros((), LOW)))
        extra = jnp.concatenate([barred, lines(log_ref[0, head : head + 1]), none], axis=0).astype(LOW)
        half = slice(head * HD, (head + 1) * HD)
        query = jnp.concatenate([q_turned[half], extra] if head == 0 else [extra, q_turned[half]], axis=0)
        weights = jnp.exp(nn(keyed, query))
        inner = jnp.sum(mixed[half], axis=0, keepdims=True)
        extra = jnp.concatenate([jnp.zeros_like(barred), lines(inner), none], axis=0).astype(LOW)
        grad = jnp.concatenate([grad_turned[half], extra] if head == 0 else [extra, grad_turned[half]], axis=0)
        moved = (weights * nn(valued, grad)).astype(LOW)
        dvs.append(nn(weights.astype(LOW), grads))
        dks.append(nn(moved, q_low))
        dqs.append(nn(k_turned[half], moved))
    dq_ref[...] = jnp.concatenate(dqs, axis=0).T.astype(LOW)
    dk_ref[...] = jnp.where(lane < HD, dks[0], dks[1]).astype(LOW)
    dv = jnp.where(lane < HD, dvs[0], dvs[1])
    dv_ref[...] = jnp.where(outside, dv + grad_wide, dv).astype(LOW)


def attend_back(lengths, projected, attended, grad_attended, logs):
    rows = projected.shape[0]
    blocks, pairs = rows // CAP, H // 2
    width = H * HD

    def column(part):
        return pl.BlockSpec((CAP, 128), lambda i, n: (i // pairs, part * pairs + i % pairs))

    return pl.pallas_call(
        attend_back_kernel,
        out_shape=(jax.ShapeDtypeStruct((rows, width), LOW),) * 3,
        grid_spec=pltpu.PrefetchScalarGridSpec(
            num_scalar_prefetch=1,
            grid=(blocks * pairs,),
            in_specs=[column(0), column(1), column(2), column(0), column(0)]
            + [pl.BlockSpec((1, 8, CAP), lambda i, n: (i, 0, 0))],
            out_specs=(column(0),) * 3,
        ),
        compiler_params=params(),
        cost_estimate=pl.CostEstimate(
            flops=10 * 4 * rows * CAP * width, bytes_accessed=16 * rows * width, transcendentals=rows * CAP * H
        ),
    )(lengths, projected, projected, projected, attended, grad_attended, logs)


def norm(values):
    centre = jnp.mean(values, axis=-1, keepdims=True)
    centred = values - centre
    scale = lax.rsqrt(jnp.mean(centred * centred, axis=-1, keepdims=True) + EPSILON)
    return centred * scale, scale


def norm_back(grad, normal, scale):
    return scale * (
        grad
        - jnp.mean(grad, axis=-1, keepdims=True)
        - normal * jnp.mean(grad * normal, axis=-1, keepdims=True)
    )


ROOT_HALF = 0.7071067811865476
ROOT_TAU = 0.3989422804014327


def middle_kernel(plan, count, chunk, at, rows_ref, att_ref, cot_ref, small_ref, wide_ref, *refs):
    out_pieces, expand_pieces, contract_pieces = (refs[i * count : (i + 1) * count] for i in range(3))
    (
        result_ref, active_ref, first_ref, second_ref, expanded_ref, branch_ref, grad_att_ref,
        sums_ref, wide_sums_ref, w_out, w_expand, w_contract, slope, sems,
    ) = refs[3 * count :]
    depth, hidden = w_expand.shape

    @pl.when(pl.program_id(0) == 0)
    def _():
        fetch(
            plan,
            at,
            [(out_pieces, w_out, depth), (expand_pieces, w_expand, depth), (contract_pieces, w_contract, hidden)],
            sems,
        )
        sums_ref[...] = jnp.zeros_like(sums_ref)
        wide_sums_ref[...] = jnp.zeros_like(wide_sums_ref)

    def small(index):
        return small_ref[index : index + 1].astype(F32)

    def add(index, value):
        sums_ref[index : index + 1] += jnp.sum(value, axis=0, keepdims=True)

    out_bias, contract_bias, gain_one, shift_one, gain_two, shift_two = (small(i) for i in range(6))
    residual = rows_ref[...].astype(F32) + nn(att_ref[...], w_out[...]) + out_bias
    normal_one, scale_one = norm(residual)
    first = normal_one * gain_one + shift_one
    low = first.astype(LOW)
    first_ref[...] = low
    total = first + contract_bias
    for start in range(0, hidden, chunk):
        span = slice(start, start + chunk)
        wide = nn(low, w_expand[:, span]) + wide_ref[0:1, span].astype(F32)
        cumulative = 0.5 * (1.0 + lax.erf(wide * ROOT_HALF))
        active = (wide * cumulative).astype(LOW)
        slope[:, span] = cumulative + wide * (ROOT_TAU * jnp.exp(-0.5 * wide * wide))
        active_ref[:, span] = active
        total = total + nn(active, w_contract[span])
    normal_two, scale_two = norm(total)
    result_ref[...] = (normal_two * gain_two + shift_two).astype(LOW)
    cot = cot_ref[...].astype(F32)
    add(4, cot * normal_two)
    add(5, cot)
    second = norm_back(cot * gain_two, normal_two, scale_two)
    second_low = second.astype(LOW)
    second_ref[...] = second_low
    add(1, second_low.astype(F32))
    total = second
    for start in range(0, hidden, chunk):
        span = slice(start, start + chunk)
        grad = (nt(second_low, w_contract[span]) * slope[:, span]).astype(LOW)
        expanded_ref[:, span] = grad
        wide_sums_ref[0:1, span] += jnp.sum(grad.astype(F32), axis=0, keepdims=True)
        total = total + nt(grad, w_expand[:, span])
    add(2, total * normal_one)
    add(3, total)
    branch = norm_back(total * gain_one, normal_one, scale_one)
    branch_low = branch.astype(LOW)
    branch_ref[...] = branch_low
    add(0, branch_low.astype(F32))
    grad_att_ref[...] = nt(branch_low, w_out[...]).astype(LOW)


def middle(plan, at, rows, attended, cot, small, wide, out_pieces, expand_pieces, contract_pieces, tile=256, chunk=1024):
    count = len(out_pieces)
    height, depth = rows.shape
    hidden = wide.shape[1]

    def tiled(width):
        return pl.BlockSpec((tile, width), lambda i, at: (i, 0))

    def whole(height, width):
        return pl.BlockSpec((height, width), lambda i, at: (0, 0))

    return pl.pallas_call(
        functools.partial(middle_kernel, plan, count, chunk),
        out_shape=(
            jax.ShapeDtypeStruct((height, depth), LOW),
            jax.ShapeDtypeStruct((height, hidden), LOW),
            jax.ShapeDtypeStruct((height, depth), LOW),
            jax.ShapeDtypeStruct((height, depth), LOW),
            jax.ShapeDtypeStruct((height, hidden), LOW),
            jax.ShapeDtypeStruct((height, depth), LOW),
            jax.ShapeDtypeStruct((height, depth), LOW),
            jax.ShapeDtypeStruct((8, depth), F32),
            jax.ShapeDtypeStruct((8, hidden), F32),
        ),
        grid_spec=pltpu.PrefetchScalarGridSpec(
            num_scalar_prefetch=1,
            grid=(height // tile,),
            in_specs=[tiled(depth), tiled(depth), tiled(depth), whole(8, depth), whole(1, hidden)]
            + [ANY] * (3 * count),
            out_specs=(
                tiled(depth), tiled(hidden), tiled(depth), tiled(depth), tiled(hidden), tiled(depth),
                tiled(depth), whole(8, depth), whole(8, hidden),
            ),
            scratch_shapes=[
                pltpu.VMEM((depth, depth), LOW),
                pltpu.VMEM((depth, hidden), LOW),
                pltpu.VMEM((hidden, depth), LOW),
                pltpu.VMEM((tile, hidden), F32),
                pltpu.SemaphoreType.DMA((3,)),
            ],
        ),
        compiler_params=params(),
        cost_estimate=pl.CostEstimate(
            flops=4 * height * depth * (depth + 2 * hidden),
            bytes_accessed=2 * depth * (depth + 2 * hidden) + 4 * height * (depth * 4 + hidden),
            transcendentals=2 * height * hidden,
        ),
    )(at, rows, attended, cot, small, wide, *out_pieces, *expand_pieces, *contract_pieces)


def outer_kernel(plan, rows, count, at, left_ref, *refs):
    rights, outs = refs[:count], refs[count:]
    tile = left_ref.shape[1]
    step = pl.program_id(0)
    turned = left_ref[...].T
    start = 0
    for right in rights:
        span = slice(start, start + right.shape[1])
        start += right.shape[1]
        result = nn(turned, right[...])
        if not plan.split:
            outs[0][:, span] = result.astype(LOW)
            continue
        half = rows // plan.shards // 2
        result = result.astype(LOW)
        for j in range(tile // half):
            shard = step * (tile // half // 2) + j // 2
            group = ((shard // 2) % 2 ^ at[1]) + 2 * (j % 2 ^ at[3])
            row = pl.multiple_of((group * 4 + ((shard // 4) ^ at[0])) * half, half)
            same = at[2] == (j // 2) % 2

            @pl.when(same)
            def _(j=j, row=row, result=result, span=span):
                outs[0][pl.ds(row, half), span] = result[j * half : (j + 1) * half]

            @pl.when(jnp.logical_not(same))
            def _(j=j, row=row, result=result, span=span):
                outs[1][pl.ds(row, half), span] = result[j * half : (j + 1) * half]


def outer(plan, at, left, rights, tile):
    height, rows = left.shape
    width = sum(right.shape[1] for right in rights)
    if plan.split:
        out_shape = (jax.ShapeDtypeStruct((rows // 2, width), LOW),) * 2
        out_specs = (pl.BlockSpec((rows // 2, width), lambda i, at: (0, 0)),) * 2
    else:
        out_shape = (jax.ShapeDtypeStruct((rows, width), LOW),)
        out_specs = (pl.BlockSpec((tile, width), lambda i, at: (i, 0)),)
    return pl.pallas_call(
        functools.partial(outer_kernel, plan, rows, len(rights)),
        out_shape=out_shape,
        grid_spec=pltpu.PrefetchScalarGridSpec(
            num_scalar_prefetch=1,
            grid=(rows // tile,),
            in_specs=[pl.BlockSpec((height, tile), lambda i, at: (0, i))]
            + [pl.BlockSpec(right.shape, lambda i, at: (0, 0)) for right in rights],
            out_specs=out_specs,
        ),
        compiler_params=params(),
        cost_estimate=pl.CostEstimate(
            flops=2 * height * rows * width, bytes_accessed=2 * (rows * width + height * (rows + width)), transcendentals=0
        ),
    )(at, left, *rights)


def reduce_outer(plan, parts):
    if plan.split:
        return plan.scatter(*parts)
    owned = lax.psum_scatter(parts[0], "fsdp", scatter_dimension=0, tiled=True)
    return lax.psum(owned.astype(LOW), "rep").astype(F32)


def back_kernel(plan, count, at, branch_ref, dq_ref, dk_ref, dv_ref, *refs):
    pieces, (out_ref, sums_ref, weight, sems) = refs[:count], refs[count:]
    width = dq_ref.shape[1]

    @pl.when(pl.program_id(0) == 0)
    def _():
        fetch(plan, at, [(pieces, weight, weight.shape[0])], sems)
        sums_ref[...] = jnp.zeros_like(sums_ref)

    total = branch_ref[...].astype(F32)
    for index, ref in enumerate((dq_ref, dk_ref, dv_ref)):
        total = total + nt(ref[...], weight[:, index * width : (index + 1) * width])
    out_ref[...] = total.astype(LOW)
    sums_ref[0:1] += jnp.sum(dq_ref[...].astype(F32), axis=0, keepdims=True)
    sums_ref[1:2] += jnp.sum(dv_ref[...].astype(F32), axis=0, keepdims=True)


def back(plan, at, branch, dq, dk, dv, pieces, tile=256):
    count = len(pieces)
    height, depth = branch.shape
    width = dq.shape[1]
    tiled = pl.BlockSpec((tile, depth), lambda i, at: (i, 0))
    return pl.pallas_call(
        functools.partial(back_kernel, plan, count),
        out_shape=(jax.ShapeDtypeStruct((height, depth), LOW), jax.ShapeDtypeStruct((8, width), F32)),
        grid_spec=pltpu.PrefetchScalarGridSpec(
            num_scalar_prefetch=1,
            grid=(height // tile,),
            in_specs=[tiled] * 4 + [ANY] * count,
            out_specs=(tiled, pl.BlockSpec((8, width), lambda i, at: (0, 0))),
            scratch_shapes=[pltpu.VMEM((depth, 3 * width), LOW), pltpu.SemaphoreType.DMA((1,))],
        ),
        compiler_params=params(),
        cost_estimate=pl.CostEstimate(
            flops=6 * height * depth * width, bytes_accessed=6 * depth * width + 10 * height * depth, transcendentals=0
        ),
    )(at, branch, dq, dk, dv, *pieces)


def body(
    tokens, seq_lengths, out_cotangent, project_in, project_out, expand, contract,
    query_bias, value_bias, out_bias, expand_bias, contract_bias,
    first_gain, first_shift, second_gain, second_shift,
    *, shards, copies,
):
    plan = Plan(shards, copies)
    at = place()
    depth = tokens.shape[1]
    hidden = expand.shape[1]
    part, wide_part = query_bias.shape[0], expand_bias.shape[0]
    vectors = (query_bias, value_bias, out_bias, contract_bias, first_gain, first_shift, second_gain, second_shift)
    packed = jnp.concatenate(vectors + (expand_bias,))[None]
    packed = lax.all_gather(packed, "fsdp", axis=0, tiled=True)
    small = [packed[:, i * part : (i + 1) * part].reshape(-1) for i in range(8)]
    wide = packed[:, 8 * part :].reshape(1, -1)
    bias = jnp.concatenate([small[0], jnp.zeros_like(small[0]), small[1]])[None]
    table = jnp.stack(small[2:] + [jnp.zeros_like(small[0])] * 2)

    in_pieces = plan.gather(project_in)
    out_pieces = plan.gather(project_out)
    expand_pieces = plan.gather(expand)
    contract_pieces = plan.gather(contract)

    projected = project(plan, at, tokens, bias, in_pieces, depth, project_in.shape[1])
    attended, logs = attend(seq_lengths, projected)
    result, active, first, second, grad_expanded, branch, grad_attended, sums, wide_sums = middle(
        plan, at, tokens, attended, out_cotangent, table, wide, out_pieces, expand_pieces, contract_pieces
    )
    grad_contract = reduce_outer(plan, outer(plan, at, active, [second], 512))
    grad_expand = reduce_outer(plan, outer(plan, at, first, [grad_expanded], 256))
    grad_project_out = reduce_outer(plan, outer(plan, at, attended, [branch], 256))
    dq, dk, dv = attend_back(seq_lengths, projected, attended, grad_attended, logs)
    grad_project_in = reduce_outer(plan, outer(plan, at, tokens, [dq, dk, dv], 256))
    grad_tokens, back_sums = back(plan, at, branch, dq, dk, dv, in_pieces)

    vector_sums = jnp.concatenate([back_sums[:2], sums[:6]], axis=0)
    by_owner = jnp.concatenate(
        [
            vector_sums.reshape(8, shards, part).transpose(1, 0, 2).reshape(shards, 8 * part),
            wide_sums[0].reshape(shards, wide_part),
        ],
        axis=1,
    )
    owned = lax.psum_scatter(by_owner, "fsdp", scatter_dimension=0, tiled=True)
    owned = lax.psum(owned, "rep")[0]
    vector = [owned[i * part : (i + 1) * part] for i in range(8)]
    grad_query, grad_value, grad_out, grad_down, gain_one, shift_one, gain_two, shift_two = vector
    return (
        result, grad_tokens, grad_project_in, grad_project_out, grad_expand, grad_contract,
        grad_query, grad_value, grad_out, owned[8 * part :], grad_down,
        gain_one, shift_one, gain_two, shift_two,
    )


def solution(mesh):
    split, row, vector = P(("fsdp", "rep"), None), P("fsdp", None), P("fsdp")
    return jax.shard_map(
        functools.partial(body, shards=mesh.shape["fsdp"], copies=mesh.shape["rep"]),
        mesh=mesh,
        in_specs=(split,) * 3 + (row,) * 4 + (vector,) * 9,
        out_specs=(split,) * 2 + (row,) * 4 + (vector,) * 9,
        check_vma=False,
    )
```

time: 1070 us -> 621 us (0.58)
  matrix products: 352 us -> 0 us
  waiting for transfers between devices: 410 us -> 172 us
  Pallas kernels: 0 us -> 200 us
  starting transfers between devices: 0.36 us -> 93.4 us
  other arithmetic: 87.9 us -> 29.6 us
  blocking collectives: 148 us -> 93.1 us
  local copies, waits for them, and re-layouts: 52.7 us -> 21.7 us
  between operations: 17.3 us -> 1.94 us
    dot_general x36 -> x0, matrix products: 352 us -> none  [the longest x8 80.2 us: outer_sum(): lax.dot_general(left, right, (((0,), (0,)), ((), ())), preferred_element_...]
    reduce_scatter x3 -> x0, waiting for transfers between devices: 351 us -> none  [the longest x1 180 us: body(): lax.psum_scatter(running[3], 'fsdp', scatter_dimension=0, tiled=True)]
    pallas_call x0 -> x9, Pallas kernels: none -> 200 us  [the longest x4 60.2 us: outer(): pl.pallas_call(functools.partial(outer_kernel, plan, rows, len(rights)),...]
    ppermute x0 -> x84, waiting for transfers between devices: none -> 172 us  [the longest x64 118 us: flip(): lax.ppermute(value, 'fsdp', [(i, i ^ bits) for i in range(self.shards)])]
    ppermute x0 -> x84, starting transfers between devices: none -> 93.4 us  [the longest x64 65.2 us: flip(): lax.ppermute(value, 'fsdp', [(i, i ^ bits) for i in range(self.shards)])]
    unnamed x2 -> x1, blocking collectives: 126 us -> 62.8 us
    psum x1 -> x0, waiting for transfers between devices: 48.5 us -> none  [body(): lax.psum(owned[0].astype(jnp.bfloat16), 'rep').astype(jnp.float32)]
    reduce_sum x17 -> x0, other arithmetic: 35.2 us -> none  [the longest x2 16.9 us: layer_forward(): row_totals = jnp.sum(weights, axis=-1, keepdims=True)]
  transfers between devices with their start and end apart: 9 -> 84, of which waited for: 4 -> 28; matrix products, arithmetic and copies ran while one was open for 32% -> 8% of each run, Pallas kernels for 0% -> 22%
where the time goes in v1:
time: 621 us; the launch traced here: 612 us
  Pallas kernels  200 us (32%)
  waiting for transfers between devices  172 us (28%)
  starting transfers between devices  93.4 us (15%)
  blocking collectives  93.1 us (15%)
  other arithmetic  29.6 us (5%)
  local copies, waits for them, and re-layouts  21.7 us (3%)
    ppermute x64, waiting for transfers between devices, flip(): lax.ppermute(value, 'fsdp', [(i, i ^ bits) for i in range(self.shards)])  118 us
    ppermute x64, starting transfers between devices, flip(): lax.ppermute(value, 'fsdp', [(i, i ^ bits) for i in range(self.shards)])  65.2 us
    unnamed x1, blocking collectives  62.8 us
    pallas_call x4, Pallas kernels, outer(): pl.pallas_call(functools.partial(outer_kernel, plan, rows, len(rights)),...  60.2 us
    pallas_call x1, Pallas kernels, middle(): pl.pallas_call(functools.partial(middle_kernel, plan, count, chunk), out_...  58.6 us
    ppermute x20, waiting for transfers between devices, other_copy(): return lax.ppermute(value, 'rep', [(0, 1), (1, 0)])  53.5 us
    pallas_call x1, Pallas kernels, attend_back(): pl.pallas_call(attend_back_kernel, out_shape=(jax.ShapeDtypeStruct((rows,...  30.5 us
    ppermute x20, starting transfers between devices, other_copy(): return lax.ppermute(value, 'rep', [(0, 1), (1, 0)])  28.3 us
  transfers between devices with their start and end apart: 84, of which 28 were waited for; matrix products, arithmetic and copies ran while one was open for 8% of the time, Pallas kernels for 22%

profile of v1, /device:TPU:0, one launch (start us, length us, event | category | flops | bytes accessed | tf_op | source)
XLA Modules:
  0.0 611.9 jit_solution(7229048377254883287)
XLA Ops:
  22.9 16.5 %collective-permute-done.1 = bf16[32,3072]{1,0:T(8,128)(2,1)S(1)} collective-permute-done((bf16[32,3072]{1,0:T(8,128)(2,1)S(1)}, bf16[32,3072]{1,0:T(8,128)(2,1)S(1)}, u32[]{:S(2)}, u32[]{:S(2)}) %collective-permute-start.1) | collective-permute-done | bytes 196640 | tf_op jit(solution)/shard_map/ppermute | solution.py:51
  40.2 15.3 %collective-permute-start.36 = (bf16[128,1024]{1,0:T(8,128)(2,1)S(1)}, bf16[128,1024]{1,0:T(8,128)(2,1)S(1)}, u32[]{:S(2)}, u32[]{:S(2)}) collective-permute-start(bf16[128,1024]{1,0:T(8,128)(2,1)S(1)} %constant_dynamic-slice_fusion), channel_id=1, source_target_pairs={{0,8},{2,10},{4,12},{6,14},{8,0},{10,2},{12,4},{14,6},{16,24},{18,... | collective-permute-start | bytes 786440 | tf_op jit(solution)/shard_map/ppermute | solution.py:51
  67.5 9.2 %collective-permute-done.37 = bf16[128,1024]{1,0:T(8,128)(2,1)S(1)} collective-permute-done((bf16[128,1024]{1,0:T(8,128)(2,1)S(1)}, bf16[128,1024]{1,0:T(8,128)(2,1)S(1)}, u32[]{:S(2)}, u32[]{:S(2)}) %collective-permute-start.37) | collective-permute-done | bytes 262176 | tf_op jit(solution)/shard_map/ppermute | solution.py:51
  79.3 8.2 %collective-permute-done.18.refs_4_ = bf16[64,1024]{1,0:T(8,128)(2,1)S(1)} collective-permute-done((bf16[64,1024]{1,0:T(8,128)(2,1)S(1)}, bf16[64,1024]{1,0:T(8,128)(2,1)S(1)}, u32[]{:S(2)}, u32[]{:S(2)}) %collective-permute-start.18) | collective-permute-done | bytes 131104 | tf_op jit(solution)/shard_map/ppermute | solution.py:54
  100.4 13.1 %collective-permute-done.28.refs_12_ = bf16[128,4096]{1,0:T(8,128)(2,1)S(1)} collective-permute-done((bf16[128,4096]{1,0:T(8,128)(2,1)S(1)}, bf16[128,4096]{1,0:T(8,128)(2,1)S(1)}, u32[]{:S(2)}, u32[]{:S(2)}) %collective-permute-start.28) | collective-permute-done | bytes 1048608 | tf_op jit(solution)/shard_map/ppermute | solution.py:54
  122.8 13.2 %collective-permute-done.40.refs_22_ = bf16[512,1024]{1,0:T(8,128)(2,1)S(1)} collective-permute-done((bf16[512,1024]{1,0:T(8,128)(2,1)S(1)}, bf16[512,1024]{1,0:T(8,128)(2,1)S(1)}, u32[]{:S(2)}, u32[]{:S(2)}) %collective-permute-start.40) | collective-permute-done | bytes 1048608 | tf_op jit(solution)/shard_map/ppermute | solution.py:54
  136.0 7.2 %collective-permute-done.39.refs_21_ = bf16[512,1024]{1,0:T(8,128)(2,1)S(1)} collective-permute-done((bf16[512,1024]{1,0:T(8,128)(2,1)S(1)}, bf16[512,1024]{1,0:T(8,128)(2,1)S(1)}, u32[]{:S(2)}, u32[]{:S(2)}) %collective-permute-start.39) | collective-permute-done | bytes 1048608 | tf_op jit(solution)/shard_map/ppermute | solution.py:51
  143.2 8.1 %collective-permute-done.5.refs_3_ = bf16[64,3072]{1,0:T(8,128)(2,1)} collective-permute-done((bf16[64,3072]{1,0:T(8,128)(2,1)S(1)}, bf16[64,3072]{1,0:T(8,128)(2,1)}, u32[]{:S(2)}, u32[]{:S(2)}) %collective-permute-start.5) | collective-permute-done | bytes 393248 | tf_op jit(solution)/shard_map/ppermute | solution.py:51
  154.3 25.1 %all-gather.1 = bf16[16,1,768]{2,1,0:T(2,128)(2,1)S(1)} all-gather(bf16[1,1,768]{2,1,0:T(2,128)(2,1)S(1)} %reshape.60), channel_id=2, replica_groups=mesh['fsdp'=16,'rep'=2] {'fsdp'}, dimensions={0}, use_global_device_ids=true | all-gather | bytes 26112 | tf_op jit(solution)/shard_map/all_gather | solution.py:585
  188.6 7.3 %collective-permute-done.30.refs_14_ = bf16[64,4096]{1,0:T(8,128)(2,1)} collective-permute-done((bf16[64,4096]{1,0:T(8,128)(2,1)S(1)}, bf16[64,4096]{1,0:T(8,128)(2,1)}, u32[]{:S(2)}, u32[]{:S(2)}) %collective-permute-start.30) | collective-permute-done | bytes 524320 | tf_op jit(solution)/shard_map/ppermute | solution.py:54
  197.3 13.0 %shard_map.271.q_ref.k_ref.v_ref = bf16[1024,3072]{1,0:T(8,128)(2,1)} custom-call(s32[4]{0:T(128)} %pad_add_fusion.at, bf16[1024,1024]{1,0:T(8,128)(2,1)} %left_ref.1, bf16[1,3072]{1,0:T(2,128)(2,1)} %broadcast_in_dim.11.bias_ref, bf16[128,3072]{1,0:T(8,128)(2,1)} %copy-done.10, bf16[128,3072]{1,0:T(8,128)(2,1)} %collective-permute-done.3.refs_1_, ...), custom_call_target="tpu_custom_call" | custom-call | flops 6442450944 | bytes 6291456 | tf_op jit(solution)/shard_map/pallas_call | solution.py:153
  211.6 24.0 %shard_map.272 = (bf16[1024,1024]{1,0:T(8,128)(2,1)}, f32[16,8,512]{2,1,0:T(8,128)}) custom-call(s32[2,4]{1,0:T(2,128)} %lengths_ref.3, bf16[1024,3072]{1,0:T(8,128)(2,1)} %shard_map.271.q_ref.k_ref.v_ref, bf16[1024,3072]{1,0:T(8,128)(2,1)} %shard_map.271.q_ref.k_ref.v_ref, bf16[1024,3072]{1,0:T(8,128)(2,1)} %shard_map.271.q_ref.k_ref.v_ref), custom_call_target="tpu_custom_call" | custom-call | flops 8589934592 | bytes 8388608 | tf_op jit(solution)/shard_map/pallas_call | solution.py:235
  236.7 58.6 %shard_map.273 = (bf16[1024,1024]{1,0:T(8,128)(2,1)}, bf16[1024,4096]{1,0:T(8,128)(2,1)}, bf16[1024,1024]{1,0:T(8,128)(2,1)}, bf16[1024,1024]{1,0:T(8,128)(2,1)}...) custom-call(s32[4]{0:T(128)} %pad_add_fusion.at, ...), custom_call_target="tpu_custom_call" | custom-call | flops 38654705664 | bytes 52428800 | tf_op jit(solution)/shard_map/pallas_call | solution.py:431
  295.4 7.5 %shard_map.277 = (bf16[512,1024]{1,0:T(8,128)(2,1)}, bf16[512,1024]{1,0:T(8,128)(2,1)}) custom-call(s32[4]{0:T(128)} %pad_add_fusion.at, bf16[1024,1024]{1,0:T(8,128)(2,1)} %get-tuple-element.39.att_ref.left_ref, bf16[1024,1024]{1,0:T(8,128)(2,1)} %get-tuple-element.41.branch_ref.refs_0_), custom_call_target="tpu_custom_call" | custom-call | flops 2147483648 | bytes 6291456 | tf_op jit(solution)/shard_map/pallas_call | solution.py:509
  303.3 30.5 %shard_map.274 = (bf16[1024,1024]{1,0:T(8,128)(2,1)}, bf16[1024,1024]{1,0:T(8,128)(2,1)}, bf16[1024,1024]{1,0:T(8,128)(2,1)}) custom-call(s32[2,4]{1,0:T(2,128)} %lengths_ref.3, bf16[1024,3072]{1,0:T(8,128)(2,1)} %shard_map.271.q_ref.k_ref.v_ref, bf16[1024,3072]{1,0:T(8,128)(2,1)} %shard_map.271.q_ref.k_ref.v_ref, ...), custom_call_target="tpu_custom_call" | custom-call | flops 21474836480 | bytes 16777216 | tf_op jit(solution)/shard_map/pallas_call | solution.py:319
  333.8 16.7 %shard_map.276 = (bf16[512,3072]{1,0:T(8,128)(2,1)}, bf16[512,3072]{1,0:T(8,128)(2,1)}) custom-call(s32[4]{0:T(128)} %pad_add_fusion.at, bf16[1024,1024]{1,0:T(8,128)(2,1)} %left_ref.1, bf16[1024,1024]{1,0:T(8,128)(2,1)} %get-tuple-element.44.dq_ref.refs_0_, bf16[1024,1024]{1,0:T(8,128)(2,1)} %get-tuple-element.45.dk_ref.refs_1_, ...), custom_call_target="tpu_custom_call" | custom-call | flops 6442450944 | bytes 14680064 | tf_op jit(solution)/shard_map/pallas_call | solution.py:509
  350.6 17.6 %shard_map.279 = (bf16[2048,1024]{1,0:T(8,128)(2,1)}, bf16[2048,1024]{1,0:T(8,128)(2,1)}) custom-call(s32[4]{0:T(128)} %pad_add_fusion.at, bf16[1024,4096]{1,0:T(8,128)(2,1)} %get-tuple-element.56.left_ref, bf16[1024,1024]{1,0:T(8,128)(2,1)} %get-tuple-element.57.refs_0_), custom_call_target="tpu_custom_call" | custom-call | flops 8589934592 | bytes 18874368 | tf_op jit(solution)/shard_map/pallas_call | solution.py:509
  369.5 18.4 %shard_map.278 = (bf16[512,4096]{1,0:T(8,128)(2,1)}, bf16[512,4096]{1,0:T(8,128)(2,1)}) custom-call(s32[4]{0:T(128)} %pad_add_fusion.at, bf16[1024,1024]{1,0:T(8,128)(2,1)} %get-tuple-element.52.left_ref, bf16[1024,4096]{1,0:T(8,128)(2,1)} %get-tuple-element.53.refs_0_), custom_call_target="tpu_custom_call" | custom-call | flops 8589934592 | bytes 18874368 | tf_op jit(solution)/shard_map/pallas_call | solution.py:509
  392.9 14.0 %shard_map.275 = (bf16[1024,1024]{1,0:T(8,128)(2,1)}, f32[8,1024]{1,0:T(8,128)}) custom-call(s32[4]{0:T(128)} %pad_add_fusion.at, bf16[1024,1024]{1,0:T(8,128)(2,1)} %get-tuple-element.41.branch_ref.refs_0_, bf16[1024,1024]{1,0:T(8,128)(2,1)} %get-tuple-element.44.dq_ref.refs_0_, bf16[1024,1024]{1,0:T(8,128)(2,1)} %get-tuple-element.45.dk_ref.refs_1_, ...), custom_call_target="tpu_custom_call" | custom-call | flops 6442450944 | bytes 16777216 | tf_op jit(solution)/shard_map/pallas_call | solution.py:555
  418.2 62.8 %all-reduce = f32[16,768]{1,0:T(8,128)} all-reduce(f32[16,768]{1,0:T(8,128)} %pad_maximum_fusion.12), channel_id=3, replica_groups=mesh['fsdp'=16,'rep'=2] {'fsdp'}, use_global_device_ids=true, to_apply=%region_0.1.clone | all-reduce | flops 12288 | bytes 98304
  500.8 11.8 %collective-permute-done.50 = bf16[128,3072]{1,0:T(8,128)(2,1)S(1)} collective-permute-done((bf16[128,3072]{1,0:T(8,128)(2,1)S(1)}, bf16[128,3072]{1,0:T(8,128)(2,1)S(1)}, u32[]{:S(2)}, u32[]{:S(2)}) %collective-permute-start.50) | collective-permute-done | bytes 786464 | tf_op jit(solution)/shard_map/ppermute | solution.py:51
  547.3 17.8 %collective-permute-done.77 = bf16[512,1024]{1,0:T(8,128)(2,1)S(1)} collective-permute-done((bf16[512,1024]{1,0:T(8,128)(2,1)S(1)}, bf16[512,1024]{1,0:T(8,128)(2,1)S(1)}, u32[]{:S(2)}, u32[]{:S(2)}) %collective-permute-start.77) | collective-permute-done | bytes 1048608 | tf_op jit(solution)/shard_map/ppermute | solution.py:51
  571.8 6.3 %collective-permute-done.68 = bf16[128,4096]{1,0:T(8,128)(2,1)S(1)} collective-permute-done((bf16[128,4096]{1,0:T(8,128)(2,1)S(1)}, bf16[128,4096]{1,0:T(8,128)(2,1)S(1)}, u32[]{:S(2)}, u32[]{:S(2)}) %collective-permute-start.68) | collective-permute-done | bytes 1048608 | tf_op jit(solution)/shard_map/ppermute | solution.py:51
  594.5 9.3 %collective-permute-done.72 = bf16[32,4096]{1,0:T(8,128)(2,1)S(1)} collective-permute-done((bf16[32,4096]{1,0:T(8,128)(2,1)S(1)}, bf16[32,4096]{1,0:T(8,128)(2,1)S(1)}, u32[]{:S(2)}, u32[]{:S(2)}) %collective-permute-start.72) | collective-permute-done | bytes 262176 | tf_op jit(solution)/shard_map/ppermute | solution.py:51
  (328 shorter events, 178.2 us)
Async XLA Ops:
  9.1 31.0 %collective-permute-start.24 = (bf16[32,4096]{1,0:T(8,128)(2,1)S(1)}, bf16[32,4096]{1,0:T(8,128)(2,1)S(1)}, u32[]{:S(2)}, u32[]{:S(2)}) collective-permute-start(bf16[32,4096]{1,0:T(8,128)(2,1)S(1)} %constant_dynamic-slice_fusion.1), channel_id=1, source_target_pairs={{0,8},{2,10},{4,12},{6,14},{8,0},{10,2},{12,4},{14,6},{16,24},{18,... | collective-permute-start | bytes 786440 | tf_op jit(solution)/shard_map/ppermute | solution.py:51
  13.9 41.5 %collective-permute-start.16 = (bf16[128,1024]{1,0:T(8,128)(2,1)S(1)}, bf16[128,1024]{1,0:T(8,128)(2,1)S(1)}, u32[]{:S(2)}, u32[]{:S(2)}) collective-permute-start(bf16[128,1024]{1,0:T(8,128)(2,1)S(1)} %pad_maximum_fusion.9.refs_0_), channel_id=1, source_target_pairs={{0,1},{1,0},{2,3},{3,2},{4,5},{5,4},{6,7},{7,6},{8,9},{9,8},{10,11... | collective-permute-start | bytes 786440 | tf_op jit(solution)/shard_map/ppermute | solution.py:54
  15.5 41.4 %collective-permute-start.15 = (bf16[128,1024]{1,0:T(8,128)(2,1)S(1)}, bf16[128,1024]{1,0:T(8,128)(2,1)S(1)}, u32[]{:S(2)}, u32[]{:S(2)}) collective-permute-start(bf16[128,1024]{1,0:T(8,128)(2,1)S(1)} %pad_maximum_fusion.9.refs_0_), channel_id=1, source_target_pairs={{0,4},{2,6},{4,0},{6,2},{8,12},{10,14},{12,8},{14,10},{16,20},{18,... | collective-permute-start | bytes 786440 | tf_op jit(solution)/shard_map/ppermute | solution.py:51
  60.6 34.1 %collective-permute-start.4 = (bf16[128,3072]{1,0:T(8,128)(2,1)S(1)}, bf16[128,3072]{1,0:T(8,128)(2,1)}, u32[]{:S(2)}, u32[]{:S(2)}) collective-permute-start(bf16[128,3072]{1,0:T(8,128)(2,1)S(1)} %pad_maximum_fusion.6.refs_0_), channel_id=1, source_target_pairs={{0,1},{1,0},{2,3},{3,2},{4,5},{5,4},{6,7},{7,6},{8,9},{9,8},{10,11... | collective-permute-start | bytes 2359304 | tf_op jit(solution)/shard_map/ppermute | solution.py:54
  98.4 37.6 %collective-permute-start.40 = (bf16[512,1024]{1,0:T(8,128)(2,1)S(1)}, bf16[512,1024]{1,0:T(8,128)(2,1)S(1)}, u32[]{:S(2)}, u32[]{:S(2)}) collective-permute-start(bf16[512,1024]{1,0:T(8,128)(2,1)S(1)} %pad_maximum_fusion.1.refs_20_), channel_id=1, source_target_pairs={{0,1},{1,0},{2,3},{3,2},{4,5},{5,4},{6,7},{7,6},{8,9},{9,8},{10,11... | collective-permute-start | bytes 3145736 | tf_op jit(solution)/shard_map/ppermute | solution.py:54
  99.5 43.7 %collective-permute-start.39 = (bf16[512,1024]{1,0:T(8,128)(2,1)S(1)}, bf16[512,1024]{1,0:T(8,128)(2,1)S(1)}, u32[]{:S(2)}, u32[]{:S(2)}) collective-permute-start(bf16[512,1024]{1,0:T(8,128)(2,1)S(1)} %pad_maximum_fusion.1.refs_20_), channel_id=1, source_target_pairs={{0,4},{2,6},{4,0},{6,2},{8,12},{10,14},{12,8},{14,10},{16,20},{18,... | collective-permute-start | bytes 3145736 | tf_op jit(solution)/shard_map/ppermute | solution.py:51
  113.5 38.4 %collective-permute-start.43 = (bf16[512,1024]{1,0:T(8,128)(2,1)S(1)}, bf16[512,1024]{1,0:T(8,128)(2,1)S(1)}, u32[]{:S(2)}, u32[]{:S(2)}) collective-permute-start(bf16[512,1024]{1,0:T(8,128)(2,1)S(1)} %pad_maximum_fusion.1.refs_20_), channel_id=1, source_target_pairs={{0,2},{2,0},{4,6},{6,4},{8,10},{10,8},{12,14},{14,12},{16,18},{18,... | collective-permute-start | bytes 3145736 | tf_op jit(solution)/shard_map/ppermute | solution.py:51
  136.0 47.3 %collective-permute-start.8 = (bf16[128,3072]{1,0:T(8,128)(2,1)}, bf16[128,3072]{1,0:T(8,128)(2,1)}, u32[]{:S(2)}, u32[]{:S(2)}) collective-permute-start(bf16[128,3072]{1,0:T(8,128)(2,1)} %collective-permute-done.3.refs_1_), channel_id=1, source_target_pairs={{0,2},{2,0},{4,6},{6,4},{8,10},{10,8},{12,14},{14,12},{16,18},{18,... | collective-permute-start | bytes 2359304 | tf_op jit(solution)/shard_map/ppermute | solution.py:51
  143.2 40.2 %collective-permute-start.9 = (bf16[128,3072]{1,0:T(8,128)(2,1)}, bf16[128,3072]{1,0:T(8,128)(2,1)}, u32[]{:S(2)}, u32[]{:S(2)}) collective-permute-start(bf16[128,3072]{1,0:T(8,128)(2,1)} %collective-permute-done.4.refs_2_), channel_id=1, source_target_pairs={{0,2},{2,0},{4,6},{6,4},{8,10},{10,8},{12,14},{14,12},{16,18},{18,... | collective-permute-start | bytes 2359304 | tf_op jit(solution)/shard_map/ppermute | solution.py:51
  151.3 31.7 %collective-permute-start.11 = (bf16[64,3072]{1,0:T(8,128)(2,1)}, bf16[64,3072]{1,0:T(8,128)(2,1)}, u32[]{:S(2)}, u32[]{:S(2)}) collective-permute-start(bf16[64,3072]{1,0:T(8,128)(2,1)} %collective-permute-done.6.refs_4_), channel_id=1, source_target_pairs={{0,2},{2,0},{4,6},{6,4},{8,10},{10,8},{12,14},{14,12},{16,18},{18,... | collective-permute-start | bytes 1179656 | tf_op jit(solution)/shard_map/ppermute | solution.py:51
  153.0 30.8 %collective-permute-start.29 = (bf16[64,4096]{1,0:T(8,128)(2,1)S(1)}, bf16[64,4096]{1,0:T(8,128)(2,1)S(1)}, u32[]{:S(2)}, u32[]{:S(2)}) collective-permute-start(bf16[64,4096]{1,0:T(8,128)(2,1)S(1)} %slice.453), channel_id=1, source_target_pairs={{0,4},{2,6},{4,0},{6,2},{8,12},{10,14},{12,8},{14,10},{16,20},{18,... | collective-permute-start | bytes 1572872 | tf_op jit(solution)/shard_map/ppermute | solution.py:51
  197.3 38.2 %collective-permute-start.45 = (bf16[512,1024]{1,0:T(8,128)(2,1)}, bf16[512,1024]{1,0:T(8,128)(2,1)S(1)}, u32[]{:S(2)}, u32[]{:S(2)}) collective-permute-start(bf16[512,1024]{1,0:T(8,128)(2,1)} %copy-done.13), channel_id=1, source_target_pairs={{0,2},{2,0},{4,6},{6,4},{8,10},{10,8},{12,14},{14,12},{16,18},{18,... | collective-permute-start | bytes 3145736 | tf_op jit(solution)/shard_map/ppermute | solution.py:51
  302.9 65.7 %collective-permute-start.57 = (bf16[512,1024]{1,0:T(8,128)(2,1)}, bf16[512,1024]{1,0:T(8,128)(2,1)S(1)}, u32[]{:S(2)}, u32[]{:S(2)}) collective-permute-start(bf16[512,1024]{1,0:T(8,128)(2,1)} %get-tuple-element.51), channel_id=1, source_target_pairs={{0,2},{2,0},{4,6},{6,4},{8,10},{10,8},{12,14},{14,12},{16,18},{18,... | collective-permute-start | bytes 3145736 | tf_op jit(solution)/shard_map/ppermute | solution.py:51
  350.5 63.1 %collective-permute-start.48 = (bf16[512,3072]{1,0:T(8,128)(2,1)}, bf16[512,3072]{1,0:T(8,128)(2,1)}, u32[]{:S(2)}, u32[]{:S(2)}) collective-permute-start(bf16[512,3072]{1,0:T(8,128)(2,1)} %get-tuple-element.49), channel_id=1, source_target_pairs={{0,2},{2,0},{4,6},{6,4},{8,10},{10,8},{12,14},{14,12},{16,18},{18,... | collective-permute-start | bytes 9437192 | tf_op jit(solution)/shard_map/ppermute | solution.py:51
  368.2 126.6 %collective-permute-start.75 = (bf16[2048,1024]{1,0:T(8,128)(2,1)}, bf16[2048,1024]{1,0:T(8,128)(2,1)}, u32[]{:S(2)}, u32[]{:S(2)}) collective-permute-start(bf16[2048,1024]{1,0:T(8,128)(2,1)} %get-tuple-element.59), channel_id=1, source_target_pairs={{0,2},{2,0},{4,6},{6,4},{8,10},{10,8},{12,14},{14,12},{16,18},{18,... | collective-permute-start | bytes 12582920 | tf_op jit(solution)/shard_map/ppermute | solution.py:51
  412.2 68.8 %collective-permute-start.63 = (bf16[32,1024]{1,0:T(8,128)(2,1)}, bf16[32,1024]{1,0:T(8,128)(2,1)}, u32[]{:S(2)}, u32[]{:S(2)}) collective-permute-start(bf16[32,1024]{1,0:T(8,128)(2,1)} %get-tuple-element.112), channel_id=1, source_target_pairs={{0,16},{2,18},{4,20},{6,22},{8,24},{10,26},{12,28},{14,30},{16,0},... | collective-permute-start | bytes 196616 | tf_op jit(solution)/shard_map/ppermute | solution.py:51
  416.3 73.8 %collective-permute-start.49 = (bf16[64,3072]{1,0:T(8,128)(2,1)}, bf16[64,3072]{1,0:T(8,128)(2,1)}, u32[]{:S(2)}, u32[]{:S(2)}) collective-permute-start(bf16[64,3072]{1,0:T(8,128)(2,1)} %get-tuple-element.86), channel_id=1, source_target_pairs={{0,1},{1,0},{2,3},{3,2},{4,5},{5,4},{6,7},{7,6},{8,9},{9,8},{10,11... | collective-permute-start | bytes 1179656 | tf_op jit(solution)/shard_map/ppermute | solution.py:54
  417.6 72.6 %collective-permute-start.51 = (bf16[64,3072]{1,0:T(8,128)(2,1)}, bf16[64,3072]{1,0:T(8,128)(2,1)}, u32[]{:S(2)}, u32[]{:S(2)}) collective-permute-start(bf16[64,3072]{1,0:T(8,128)(2,1)} %get-tuple-element.85), channel_id=1, source_target_pairs={{0,4},{2,6},{4,0},{6,2},{8,12},{10,14},{12,8},{14,10},{16,20},{18,... | collective-permute-start | bytes 1179656 | tf_op jit(solution)/shard_map/ppermute | solution.py:51
  418.2 100.7 %collective-permute-start.66 = (bf16[512,4096]{1,0:T(8,128)(2,1)}, bf16[512,4096]{1,0:T(8,128)(2,1)}, u32[]{:S(2)}, u32[]{:S(2)}) collective-permute-start(bf16[512,4096]{1,0:T(8,128)(2,1)} %get-tuple-element.55), channel_id=1, source_target_pairs={{0,2},{2,0},{4,6},{6,4},{8,10},{10,8},{12,14},{14,12},{16,18},{18,... | collective-permute-start | bytes 12582920 | tf_op jit(solution)/shard_map/ppermute | solution.py:51
  497.3 32.3 %collective-permute-start.76 = (bf16[256,1024]{1,0:T(8,128)(2,1)S(1)}, bf16[256,1024]{1,0:T(8,128)(2,1)S(1)}, u32[]{:S(2)}, u32[]{:S(2)}) collective-permute-start(bf16[256,1024]{1,0:T(8,128)(2,1)S(1)} %get-tuple-element.74), channel_id=1, source_target_pairs={{0,1},{1,0},{2,3},{3,2},{4,5},{5,4},{6,7},{7,6},{8,9},{9,8},{10,11... | collective-permute-start | bytes 1572872 | tf_op jit(solution)/shard_map/ppermute | solution.py:54
  531.5 33.6 %collective-permute-start.77 = (bf16[512,1024]{1,0:T(8,128)(2,1)S(1)}, bf16[512,1024]{1,0:T(8,128)(2,1)S(1)}, u32[]{:S(2)}, u32[]{:S(2)}) collective-permute-start(bf16[512,1024]{1,0:T(8,128)(2,1)S(1)} %pad_maximum_fusion.4), channel_id=1, source_target_pairs={{0,4},{2,6},{4,0},{6,2},{8,12},{10,14},{12,8},{14,10},{16,20},{18,... | collective-permute-start | bytes 3145736 | tf_op jit(solution)/shard_map/ppermute | solution.py:51
  533.7 31.5 %collective-permute-start.79 = (bf16[512,1024]{1,0:T(8,128)(2,1)S(1)}, bf16[512,1024]{1,0:T(8,128)(2,1)S(1)}, u32[]{:S(2)}, u32[]{:S(2)}) collective-permute-start(bf16[512,1024]{1,0:T(8,128)(2,1)S(1)} %pad_maximum_fusion.5), channel_id=1, source_target_pairs={{0,1},{1,0},{2,3},{3,2},{4,5},{5,4},{6,7},{7,6},{8,9},{9,8},{10,11... | collective-permute-start | bytes 3145736 | tf_op jit(solution)/shard_map/ppermute | solution.py:54
  544.4 33.6 %collective-permute-start.68 = (bf16[128,4096]{1,0:T(8,128)(2,1)S(1)}, bf16[128,4096]{1,0:T(8,128)(2,1)S(1)}, u32[]{:S(2)}, u32[]{:S(2)}) collective-permute-start(bf16[128,4096]{1,0:T(8,128)(2,1)S(1)} %pad_maximum_fusion.2), channel_id=1, source_target_pairs={{0,4},{2,6},{4,0},{6,2},{8,12},{10,14},{12,8},{14,10},{16,20},{18,... | collective-permute-start | bytes 3145736 | tf_op jit(solution)/shard_map/ppermute | solution.py:51
  545.1 36.7 %collective-permute-start.70 = (bf16[128,4096]{1,0:T(8,128)(2,1)S(1)}, bf16[128,4096]{1,0:T(8,128)(2,1)S(1)}, u32[]{:S(2)}, u32[]{:S(2)}) collective-permute-start(bf16[128,4096]{1,0:T(8,128)(2,1)S(1)} %pad_maximum_fusion.3), channel_id=1, source_target_pairs={{0,1},{1,0},{2,3},{3,2},{4,5},{5,4},{6,7},{7,6},{8,9},{9,8},{10,11... | collective-permute-start | bytes 3145736 | tf_op jit(solution)/shard_map/ppermute | solution.py:54
  (104 other events, 2560.9 us)

commit v2 on v1

v2 whole, which is shorter than its diff:
```python
import functools

import jax
import jax.numpy as jnp
from jax import lax
from jax.experimental import pallas as pl
from jax.experimental.pallas import tpu as pltpu
from jax.sharding import PartitionSpec as P

H = 16
HD = 64
SLOTS = 4
CAP = 512
EPSILON = 1e-12
SCALE = 0.125
BIG = 1e30
EXTRA = 128
HASTE = 1
LOW = jnp.bfloat16
F32 = jnp.float32
VMEM_LIMIT = 60 * 1024 * 1024
ANY = pl.BlockSpec(memory_space=pl.ANY)
OWN, ACROSS, OTHER, CORNER = (0, 0), (1, 0), (0, 1), (1, 1)
GROUPS = (OWN, ACROSS, OTHER, CORNER)


def params(limit=VMEM_LIMIT):
    return pltpu.CompilerParams(vmem_limit_bytes=limit, dimension_semantics=("arbitrary",))


def cost(flops, slow=2):
    return pl.CostEstimate(flops=slow * flops // HASTE, bytes_accessed=slow * flops // HASTE // 320, transcendentals=0)


def later(kernel, prefetch, after):
    def run(*refs):
        kernel(*refs[:prefetch], *refs[prefetch + len(after) :])

    return run


def dot(left, right, over):
    return lax.dot_general(left, right, ((over[:1], over[1:]), ((), ())), preferred_element_type=F32)


def nn(left, right):
    return dot(left, right, (1, 0))


def nt(left, right):
    return dot(left, right, (1, 1))


def tn(left, right):
    return dot(left, right, (0, 0))


def pinned(at, *values):
    for value in values:
        sample = jnp.clip(value[(0,) * value.ndim].astype(F32), -1.0, 1.0).astype(jnp.int32)
        at = at + jnp.minimum(jnp.abs(sample), 0)
    return at


class Plan:
    def __init__(self, shards, copies):
        self.shards, self.copies = shards, copies
        self.split = shards == 16 and copies == 2

    def flip(self, value, bits):
        return lax.ppermute(value, "fsdp", [(i, i ^ bits) for i in range(self.shards)])

    def other_copy(self, value):
        return lax.ppermute(value, "rep", [(0, 1), (1, 0)])


    def gather_z(self, at, shard, early=False):
        half = shard.shape[0] // 2
        own = lax.dynamic_slice_in_dim(shard, at[3] * half, half, 0)
        beside = self.flip(shard, 2) if early else None
        return beside, [self.flip(own, 4 * k) for k in (1, 2, 3)]

    def gather_xy(self, at, shard, far, early=False):
        half = shard.shape[0] // 2
        far = jnp.concatenate([part + at[4].astype(LOW) for part in far], axis=0)
        own = lax.dynamic_slice_in_dim(shard, at[3] * half, half, 0)
        across = far if early else jnp.concatenate([own, far], axis=0)
        return far, self.flip(across, 2), self.other_copy(far)

    def gather_corner(self, at, shard, across, other, early=False):
        half = shard.shape[0] // 2
        left = lax.dynamic_slice_in_dim(other, at[4], half, 0)
        if not early:
            left = jnp.concatenate([lax.dynamic_slice_in_dim(shard, (1 - at[3]) * half, half, 0), left], axis=0)
        start = across.shape[0] - 2 * half
        return self.flip(left, 2), self.other_copy(lax.dynamic_slice_in_dim(across, start + at[4], 2 * half, 0))

    def gather_core(self, at, *pieces):
        return [self.flip(jnp.concatenate([piece + at[4].astype(LOW) for piece in pieces], axis=0), 1)]

    def piece_list(self, early):
        blocks = [[(0, 0, None)]]
        if early:
            blocks.append([(0, 1, None)])
        blocks.append([(k, 0, 0) for k in (1, 2, 3)])
        blocks.append([(k, 1, 0) for k in ((1, 2, 3) if early else (0, 1, 2, 3))])
        blocks.append([(k, 0, 1) for k in (1, 2, 3)])
        blocks.append([(k, 1, 1) for k in ((1,) if early else (0, 1))])
        blocks.append([(k, 1, 1) for k in (2, 3)])
        main = len(blocks) - 2
        out, first = [], 0
        for core in (0, 1):
            for piece, content in enumerate(blocks):
                if core == 0 or piece in (0, main):
                    first = 0
                for dz, dx, dy in content:
                    size = 2 if dy is None else 1
                    at_piece = piece if core == 0 else len(blocks) + (piece >= main)
                    out.append((at_piece, first, size, dz, dx, core, dy))
                    first += size
        return out


    def part(self, at, mine, got, group, first=0, count=4):
        start = GROUPS.index(group) * 4 + first
        stop = start + count
        return mine[start:stop].astype(F32) + got[start:stop].astype(F32) + at[4].astype(F32)

    def scatter_corner(self, at, mine, got):
        return (
            self.flip(self.part(at, mine, got, CORNER, 0, 2).astype(LOW), 2),
            self.other_copy(self.part(at, mine, got, CORNER, 2, 2).astype(LOW)),
        )

    def scatter_xy(self, at, mine, got, corner_a, corner_b):
        other = jnp.concatenate(
            [self.part(at, mine, got, OTHER, 0, 2) + corner_a.astype(F32), self.part(at, mine, got, OTHER, 2, 2)], axis=0
        ).astype(LOW)
        across = jnp.concatenate(
            [self.part(at, mine, got, ACROSS, 0, 2), self.part(at, mine, got, ACROSS, 2, 2) + corner_b.astype(F32)], axis=0
        ).astype(LOW)
        return self.flip(across, 2), self.other_copy(other)

    def scatter_z(self, at, mine, got, across, other):
        own = self.part(at, mine, got, OWN) + across.astype(F32) + other.astype(F32)
        low = own.astype(LOW)
        return [own[0]] + [self.flip(low[k], 4 * k) for k in (1, 2, 3)]

    def scatter_end(self, at, parts):
        total = parts[0] + at[4].astype(F32)
        for value in parts[1:]:
            total = total + value.astype(F32)
        total = total.astype(LOW)
        away = self.other_copy(total)
        low = at[3] == 0
        return jnp.where(low, total, away).astype(F32), jnp.where(low, away, total).astype(F32)


def place():
    shard = lax.axis_index("fsdp")
    return jnp.stack(
        [shard // 4, (shard // 2) % 2, shard % 2, lax.axis_index("rep"), shard * 0]
    ).astype(jnp.int32)


AT = jax.ShapeDtypeStruct((5,), jnp.int32)
AT_SPEC = pl.BlockSpec(memory_space=pltpu.SMEM)


def hand_on(at, at_ref):
    for index in range(5):
        at_ref[index] = at[index]


def load_copies(plan, at, pieces, target, sem, rows, early):
    if len(pieces) == 1:
        return [pltpu.make_async_copy(pieces[0], target, sem)]
    half = rows // plan.shards // 2
    copies = []
    for piece, first, count, dz, dx, dc, dy in plan.piece_list(early):
        shard = (at[0] ^ dz) * 4 + (at[1] ^ dx) * 2 + (at[2] ^ dc)
        row = shard * 2 * half
        if dy is not None:
            row = row + (at[3] ^ dy) * half
        size = count * half
        copies.append(
            pltpu.make_async_copy(
                pieces[piece].at[pl.ds(first * half, size)], target.at[pl.ds(pl.multiple_of(row, half), size)], sem
            )
        )
    return copies


def fetch(plan, at, groups, sems):
    for index in range(len(groups)):
        for copy in load_copies(plan, at, *groups[index][:2], sems.at[index], *groups[index][2:]):
            copy.start()


def wait_for(plan, at, groups, sems, index):
    for copy in load_copies(plan, at, *groups[index][:2], sems.at[index], *groups[index][2:]):
        copy.wait()


def first_step(action):
    pl.when(pl.program_id(0) == 0)(action)


def project_kernel(plan, count, at, rows_ref, *refs):
    pieces, (out_ref, turned_ref, at_ref, weight, bias, sems) = refs[:count], refs[count:]
    depth = weight.shape[0]

    def load():
        hand_on(at, at_ref)
        groups = [(pieces, weight, weight.shape[0], True)]
        fetch(plan, at, groups, sems)
        wait_for(plan, at, groups, sems, 0)
        bias[...] = weight[:, 3 * depth :].astype(F32).T[:8]

    turned_ref[...] = rows_ref[...].T
    first_step(load)
    for block, row in ((0, 0), (1, None), (2, 1)):
        span = slice(block * depth, (block + 1) * depth)
        result = nn(rows_ref[...], weight[:, span])
        if row is not None:
            result = result + bias[row : row + 1]
        out_ref[:, span] = result.astype(LOW)


def project(plan, at, rows, pieces, depth, width, tile=256, after=()):
    count = len(pieces)
    height = rows.shape[0]
    return pl.pallas_call(
        later(functools.partial(project_kernel, plan, count), 1, after),
        out_shape=(jax.ShapeDtypeStruct((height, width), LOW), jax.ShapeDtypeStruct((depth, height), LOW), AT),
        grid_spec=pltpu.PrefetchScalarGridSpec(
            num_scalar_prefetch=1,
            grid=(height // tile,),
            in_specs=[ANY] * len(after)
            + [
                pl.BlockSpec((tile, depth), lambda i, at: (i, 0)),
            ]
            + [ANY] * count,
            out_specs=(
                pl.BlockSpec((tile, width), lambda i, at: (i, 0)),
                pl.BlockSpec((depth, tile), lambda i, at: (0, i)),
                AT_SPEC,
            ),
            scratch_shapes=[
                pltpu.VMEM((depth, width + EXTRA), LOW),
                pltpu.VMEM((8, depth), F32),
                pltpu.SemaphoreType.DMA((1,)),
            ],
        ),
        compiler_params=params(),
        cost_estimate=cost(2 * height * depth * width),
    )(at, *after, rows, *pieces)


def slot_rows(lengths_ref, block, row_count):
    along = lax.broadcasted_iota(jnp.int32, (1, row_count), 1)
    down = lax.broadcasted_iota(jnp.int32, (row_count, 1), 0)
    bound, lane_slot, row_slot = 0, jnp.zeros_like(along), jnp.zeros_like(down)
    for slot in range(SLOTS):
        bound = bound + lengths_ref[block, slot]
        lane_slot = lane_slot + (along >= bound).astype(jnp.int32)
        row_slot = row_slot + (down >= bound).astype(jnp.int32)
    return lane_slot, row_slot


def query_rows(lane_slot):
    line = lax.broadcasted_iota(jnp.int32, (8, lane_slot.shape[1]), 0)
    return jnp.where(line == lane_slot, -BIG, 0.0)


def key_columns(row_slot, offset):
    column = lax.broadcasted_iota(jnp.int32, (row_slot.shape[0], 128), 1) - offset
    barred = (column >= 0) & (column <= SLOTS) & ((column != row_slot) | (row_slot == SLOTS))
    return jnp.where(barred, 1.0, 0.0).astype(LOW)


def attend_kernel(lengths_ref, at, q_ref, k_ref, v_ref, out_ref, turned_ref, log_ref, at_ref):
    hand_on(at, at_ref)
    block = pl.program_id(0) // (H // 2)
    row_count = q_ref.shape[0]
    lane_slot, row_slot = slot_rows(lengths_ref, block, row_count)
    inside = lane_slot < SLOTS
    lane = lax.broadcasted_iota(jnp.int32, (row_count, 128), 1)
    barred = query_rows(lane_slot).astype(LOW)
    padded = jnp.concatenate([barred, jnp.zeros((HD - 8, row_count), LOW)], axis=0)
    q_turned = (q_ref[...].astype(F32) * SCALE).T.astype(LOW)
    v_turned = v_ref[...].astype(F32).T
    v_low = v_turned.astype(LOW)
    ones = jnp.ones((16, row_count), LOW)
    results = []
    for head in range(2):
        own = (lane < HD) if head == 0 else (lane >= HD)
        keyed = jnp.where(own, k_ref[...], key_columns(row_slot, HD * (1 - head)))
        half = q_turned[head * HD : (head + 1) * HD]
        query = jnp.concatenate([half, padded] if head == 0 else [padded, half], axis=0)
        scores = nn(keyed, query)
        highest = jnp.max(scores, axis=0, keepdims=True)
        weights = jnp.exp(scores - highest)
        low = weights.astype(LOW)
        values = jnp.concatenate([v_low[head * HD : (head + 1) * HD], ones], axis=0)
        mixed = nn(values, low)
        total = mixed[HD : HD + 1]
        result = mixed[:HD] / total
        results.append(jnp.where(inside, result, v_turned[head * HD : (head + 1) * HD]))
        log_ref[0, head : head + 1] = jnp.where(inside, highest + jnp.log(total), BIG)
    turned = jnp.concatenate(results, axis=0)
    turned_ref[...] = turned.astype(LOW)
    out_ref[...] = turned.T.astype(LOW)


def attend(at, lengths, projected, after=()):
    rows = projected.shape[0]
    blocks, pairs = rows // CAP, H // 2
    width = H * HD

    def column(part):
        return pl.BlockSpec((CAP, 128), lambda i, n, at: (i // pairs, part * pairs + i % pairs))

    return pl.pallas_call(
        later(attend_kernel, 2, after),
        out_shape=(
            jax.ShapeDtypeStruct((rows, width), LOW),
            jax.ShapeDtypeStruct((width, rows), LOW),
            jax.ShapeDtypeStruct((blocks * pairs, 8, CAP), F32),
            AT,
        ),
        grid_spec=pltpu.PrefetchScalarGridSpec(
            num_scalar_prefetch=2,
            grid=(blocks * pairs,),
            in_specs=[ANY] * len(after) + [column(0), column(1), column(2)],
            out_specs=(
                column(0),
                pl.BlockSpec((128, CAP), lambda i, n, at: (i % pairs, i // pairs)),
                pl.BlockSpec((1, 8, CAP), lambda i, n, at: (i, 0, 0)),
                AT_SPEC,
            ),
        ),
        compiler_params=params(),
        cost_estimate=cost(4 * rows * CAP * width, 12),
    )(lengths, at, *after, projected, projected, projected)


def three(value):
    first = value.astype(LOW).astype(F32)
    rest = value - first
    second = rest.astype(LOW).astype(F32)
    return first, second, rest - second


def attend_back_kernel(lengths_ref, at, q_ref, k_ref, v_ref, att_ref, grad_ref, log_ref, dq_ref, dk_ref, dv_ref, sums_ref, at_ref):
    hand_on(at, at_ref)
    block, pair = pl.program_id(0) // (H // 2), pl.program_id(0) % (H // 2)
    row_count = q_ref.shape[0]
    lane_slot, row_slot = slot_rows(lengths_ref, block, row_count)
    outside = lane_slot >= SLOTS
    lane = lax.broadcasted_iota(jnp.int32, (row_count, 128), 1)
    barred = query_rows(lane_slot)
    q_scaled = (q_ref[...].astype(F32) * SCALE)
    q_turned = q_scaled.T.astype(LOW)
    k_scaled = k_ref[...].astype(F32) * SCALE
    k_turned = k_scaled.T.astype(LOW)
    grad_wide = grad_ref[...].astype(F32).T
    grad_turned = grad_wide
    mixed = grad_turned * att_ref[...].astype(F32)
    grad_turned = grad_turned.astype(LOW)
    line = lax.broadcasted_iota(jnp.int32, (8, row_count), 0)
    none = jnp.zeros((HD - 16, row_count), F32)

    def lines(value):
        first, second, third = three(value)
        return jnp.where(
            line == 0, -first, jnp.where(line == 1, -second, jnp.where(line == 2, -third, 0.0))
        )

    dqs, dks, dvs = [], [], []
    for head in range(2):
        own = (lane < HD) if head == 0 else (lane >= HD)
        start = HD * (1 - head)
        unit = (lane >= start + 8) & (lane < start + 11)
        keyed = jnp.where(own, k_ref[...], jnp.where(unit, jnp.ones((), LOW), key_columns(row_slot, start)))
        valued = jnp.where(own, v_ref[...], jnp.where(unit, jnp.ones((), LOW), jnp.zeros((), LOW)))
        extra = jnp.concatenate([barred, lines(log_ref[0, head : head + 1]), none], axis=0).astype(LOW)
        half = slice(head * HD, (head + 1) * HD)
        query = jnp.concatenate([q_turned[half], extra] if head == 0 else [extra, q_turned[half]], axis=0)
        weights = jnp.exp(nn(keyed, query))
        inner = jnp.sum(mixed[half], axis=0, keepdims=True)
        extra = jnp.concatenate([jnp.zeros_like(barred), lines(inner), none], axis=0).astype(LOW)
        grad = jnp.concatenate([grad_turned[half], extra] if head == 0 else [extra, grad_turned[half]], axis=0)
        moved = (weights * nn(valued, grad)).astype(LOW)
        dvs.append(nt(grad_turned[half], weights.astype(LOW)))
        dks.append(nt(q_turned[half], moved))
        dqs.append(nn(k_turned[half], moved))
    dq = jnp.concatenate(dqs, axis=0).T.astype(LOW)
    dq_ref[...] = dq
    dk_ref[...] = jnp.concatenate(dks, axis=0).T.astype(LOW)
    dv = jnp.concatenate(dvs, axis=0)
    dv = jnp.where(outside, dv + grad_wide, dv).T.astype(LOW)
    dv_ref[...] = dv

    @first_step
    def _():
        sums_ref[...] = jnp.zeros_like(sums_ref)

    span = pl.ds(pl.multiple_of(pair * 128, 128), 128)
    sums_ref[0:1, span] += jnp.sum(dq.astype(F32), axis=0, keepdims=True)
    sums_ref[1:2, span] += jnp.sum(dv.astype(F32), axis=0, keepdims=True)


def attend_back(at, lengths, projected, turned, grad_attended, logs, after=()):
    rows = projected.shape[0]
    blocks, pairs = rows // CAP, H // 2
    width = H * HD

    def column(part):
        return pl.BlockSpec((CAP, 128), lambda i, n, at: (i // pairs, part * pairs + i % pairs))

    return pl.pallas_call(
        later(attend_back_kernel, 2, after),
        out_shape=(jax.ShapeDtypeStruct((rows, width), LOW),) * 3 + (jax.ShapeDtypeStruct((8, width), F32), AT),
        grid_spec=pltpu.PrefetchScalarGridSpec(
            num_scalar_prefetch=2,
            grid=(blocks * pairs,),
            in_specs=[ANY] * len(after)
            + [
                column(0), column(1), column(2),
                pl.BlockSpec((128, CAP), lambda i, n, at: (i % pairs, i // pairs)),
                column(0),
                pl.BlockSpec((1, 8, CAP), lambda i, n, at: (i, 0, 0)),
            ],
            out_specs=(column(0),) * 3 + (pl.BlockSpec((8, width), lambda i, n, at: (0, 0)), AT_SPEC),
        ),
        compiler_params=params(),
        cost_estimate=cost(10 * rows * CAP * width, 5),
    )(lengths, at, *after, projected, projected, projected, turned, grad_attended, logs)


def norm(values):
    centre = jnp.mean(values, axis=-1, keepdims=True)
    centred = values - centre
    scale = lax.rsqrt(jnp.mean(centred * centred, axis=-1, keepdims=True) + EPSILON)
    return centred * scale, scale


def norm_back(grad, normal, scale):
    return scale * (
        grad
        - jnp.mean(grad, axis=-1, keepdims=True)
        - normal * jnp.mean(grad * normal, axis=-1, keepdims=True)
    )


ROOT_HALF = 0.7071067811865476
ROOT_TAU = 0.3989422804014327


def up_kernel(plan, chunk, at, rows_ref, att_ref, *refs):
    pieces = refs[:-11]
    (
        active_ref, slope_ref, normal_ref, scale_ref, first_ref, turned_ref, small_ref, at_ref, w_wide, wide_ref, sems,
    ) = refs[-11:]
    depth = w_wide.shape[0]
    hidden = w_wide.shape[1] - depth - EXTRA
    groups = [(pieces, w_wide, depth, False)]

    def load():
        hand_on(at, at_ref)
        fetch(plan, at, groups, sems)
        wait_for(plan, at, groups, sems, 0)
        table = w_wide[:, hidden + depth :].astype(F32).T
        small_ref[...] = table[:8]
        part = depth // plan.shards
        for shard in range(plan.shards):
            for line in range(hidden // depth):
                start = (shard * (hidden // depth) + line) * part
                wide_ref[0:1, start : start + part] = table[8 + line : 9 + line, shard * part : (shard + 1) * part]

    first_step(load)

    def small(index):
        return small_ref[index : index + 1]

    residual = rows_ref[...].astype(F32) + nn(att_ref[...], w_wide[:, hidden : hidden + depth]) + small(0)
    normal, scale = norm(residual)
    normal_ref[...] = normal.astype(LOW)
    scale_ref[...] = jnp.broadcast_to(scale, scale_ref.shape)
    first = normal * small(2) + small(3)
    first_ref[...] = first
    low = first.astype(LOW)
    turned_ref[...] = low.T
    for start in range(0, hidden, chunk):
        span = slice(start, start + chunk)
        wide = nn(low, w_wide[:, span]) + wide_ref[0:1, span]
        cumulative = 0.5 * (1.0 + lax.erf(wide * ROOT_HALF))
        active_ref[:, span] = (wide * cumulative).astype(LOW)
        slope_ref[:, span] = (cumulative + wide * (ROOT_TAU * jnp.exp(-0.5 * wide * wide))).astype(LOW)


def tiled(tile, width):
    return pl.BlockSpec((tile, width), lambda i, at: (i, 0))


def turned_tile(tile, width):
    return pl.BlockSpec((width, tile), lambda i, at: (0, i))


def whole_block(height, width):
    return pl.BlockSpec((height, width), lambda i, at: (0, 0))


def up(plan, at, rows, attended, hidden, pieces, tile=256, chunk=1024, after=()):
    height, depth = rows.shape
    return pl.pallas_call(
        later(functools.partial(up_kernel, plan, chunk), 1, after),
        out_shape=(
            jax.ShapeDtypeStruct((height, hidden), LOW),
            jax.ShapeDtypeStruct((height, hidden), LOW),
            jax.ShapeDtypeStruct((height, depth), LOW),
            jax.ShapeDtypeStruct((height, 128), F32),
            jax.ShapeDtypeStruct((height, depth), F32),
            jax.ShapeDtypeStruct((depth, height), LOW),
            jax.ShapeDtypeStruct((8, depth), F32),
            AT,
        ),
        grid_spec=pltpu.PrefetchScalarGridSpec(
            num_scalar_prefetch=1,
            grid=(height // tile,),
            in_specs=[ANY] * len(after) + [tiled(tile, depth), tiled(tile, depth)] + [ANY] * len(pieces),
            out_specs=(
                tiled(tile, hidden), tiled(tile, hidden), tiled(tile, depth), tiled(tile, 128),
                tiled(tile, depth), turned_tile(tile, depth), whole_block(8, depth), AT_SPEC,
            ),
            scratch_shapes=[
                pltpu.VMEM((depth, hidden + depth + EXTRA), LOW),
                pltpu.VMEM((8, hidden), F32),
                pltpu.SemaphoreType.DMA((1,)),
            ],
        ),
        compiler_params=params(),
        cost_estimate=cost(2 * height * depth * (depth + hidden)),
    )(at, *after, rows, attended, *pieces)


def over_kernel(plan, chunk, at, first_ref, active_ref, cot_ref, small_ref, *refs):
    pieces = refs[:-6]
    result_ref, second_ref, sums_ref, at_ref, w_contract, sems = refs[-6:]
    hidden = w_contract.shape[0]
    groups = [(pieces, w_contract, hidden, False)]

    def load():
        hand_on(at, at_ref)
        fetch(plan, at, groups, sems)
        sums_ref[...] = jnp.zeros_like(sums_ref)
        wait_for(plan, at, groups, sems, 0)

    first_step(load)

    def small(index):
        return small_ref[index : index + 1].astype(F32)

    def add(index, value):
        sums_ref[index : index + 1] += jnp.sum(value, axis=0, keepdims=True)

    normal, scale = norm(first_ref[...] + small(1) + nn(active_ref[...], w_contract[...]))
    result_ref[...] = (normal * small(4) + small(5)).astype(LOW)
    cot = cot_ref[...].astype(F32)
    add(4, cot * normal)
    add(5, cot)
    second = norm_back(cot * small(4), normal, scale).astype(LOW)
    second_ref[...] = second
    add(1, second.astype(F32))


def over(plan, at, first, active, cot, small, pieces, tile=256, chunk=1024, after=()):
    height, depth = first.shape
    hidden = active.shape[1]
    return pl.pallas_call(
        later(functools.partial(over_kernel, plan, chunk), 1, after),
        out_shape=(
            jax.ShapeDtypeStruct((height, depth), LOW),
            jax.ShapeDtypeStruct((height, depth), LOW),
            jax.ShapeDtypeStruct((8, depth), F32),
            AT,
        ),
        grid_spec=pltpu.PrefetchScalarGridSpec(
            num_scalar_prefetch=1,
            grid=(height // tile,),
            in_specs=[ANY] * len(after)
            + [tiled(tile, depth), tiled(tile, hidden), tiled(tile, depth), whole_block(8, depth)]
            + [ANY] * len(pieces),
            out_specs=(
                tiled(tile, depth), tiled(tile, depth), whole_block(8, depth), AT_SPEC,
            ),
            scratch_shapes=[pltpu.VMEM((hidden, depth), LOW), pltpu.SemaphoreType.DMA((1,))],
        ),
        compiler_params=params(),
        cost_estimate=cost(2 * height * depth * hidden),
    )(at, *after, first, active, cot, small, *pieces)


def down_kernel(plan, counts, chunk, at, second_ref, slope_ref, normal_ref, scale_ref, small_ref, *refs):
    first_count, second_count = counts
    wide_pieces, contract_pieces = refs[:first_count], refs[first_count : first_count + second_count]
    expanded_ref, branch_ref, grad_att_ref, sums_ref, wide_sums_ref, at_ref, w_wide, w_contract, sems = refs[
        first_count + second_count :
    ]
    hidden, depth = w_contract.shape

    groups = [(contract_pieces, w_contract, hidden, False), (wide_pieces, w_wide, depth, False)]

    def load():
        hand_on(at, at_ref)
        fetch(plan, at, groups, sems)
        sums_ref[...] = jnp.zeros_like(sums_ref)
        wide_sums_ref[...] = jnp.zeros_like(wide_sums_ref)
        wait_for(plan, at, groups, sems, 0)

    first_step(load)

    def add(index, value):
        sums_ref[index : index + 1] += jnp.sum(value, axis=0, keepdims=True)

    second = second_ref[...]
    total = second.astype(F32)
    for start in range(0, hidden, chunk):
        span = slice(start, start + chunk)
        grad = (nt(second, w_contract[span]) * slope_ref[:, span].astype(F32)).astype(LOW)
        expanded_ref[:, span] = grad
        wide_sums_ref[0:1, span] += jnp.sum(grad.astype(F32), axis=0, keepdims=True)
        if start == 0:
            first_step(lambda: wait_for(plan, at, groups, sems, 1))
        total = total + nt(grad, w_wide[:, span])
    normal = normal_ref[...].astype(F32)
    add(2, total * normal)
    add(3, total)
    branch = norm_back(total * small_ref[2:3].astype(F32), normal, scale_ref[:, 0:1]).astype(LOW)
    branch_ref[...] = branch
    add(0, branch.astype(F32))
    grad_att_ref[...] = nt(branch, w_wide[:, hidden : hidden + depth]).astype(LOW)


def down(plan, at, second, slope, normal, scale, small, wide_pieces, contract_pieces, tile=256, chunk=1024, after=()):
    height, depth = second.shape
    hidden = slope.shape[1]

    def tiled(width):
        return pl.BlockSpec((tile, width), lambda i, at: (i, 0))

    def whole(height, width):
        return pl.BlockSpec((height, width), lambda i, at: (0, 0))

    return pl.pallas_call(
        later(functools.partial(down_kernel, plan, (len(wide_pieces), len(contract_pieces)), chunk), 1, after),
        out_shape=(
            jax.ShapeDtypeStruct((height, hidden), LOW),
            jax.ShapeDtypeStruct((height, depth), LOW),
            jax.ShapeDtypeStruct((height, depth), LOW),
            jax.ShapeDtypeStruct((8, depth), F32),
            jax.ShapeDtypeStruct((8, hidden), F32),
            AT,
        ),
        grid_spec=pltpu.PrefetchScalarGridSpec(
            num_scalar_prefetch=1,
            grid=(height // tile,),
            in_specs=[ANY] * len(after)
            + [tiled(depth), tiled(hidden), tiled(depth), tiled(128), whole(8, depth)]
            + [ANY] * (len(wide_pieces) + len(contract_pieces)),
            out_specs=(tiled(hidden), tiled(depth), tiled(depth), whole(8, depth), whole(8, hidden), AT_SPEC),
            scratch_shapes=[
                pltpu.VMEM((depth, hidden + depth + EXTRA), LOW),
                pltpu.VMEM((hidden, depth), LOW),
                pltpu.SemaphoreType.DMA((2,)),
            ],
        ),
        compiler_params=params(),
        cost_estimate=cost(2 * height * depth * (depth + 2 * hidden)),
    )(at, *after, second, slope, normal, scale, small, *wide_pieces, *contract_pieces)


def source(at, flip, group, k):
    shard = (at[0] ^ k) * 4 + (at[1] ^ (group % 2)) * 2 + (at[2] ^ flip)
    return shard * 2 + (at[3] ^ (group // 2))


def outer_tall_kernel(at, left, right, out, at_ref):
    hand_on(at, at_ref)
    out[...] = tn(left[...], right[...]).astype(LOW)


def outer_tall(at, left, right, tile=512, after=()):
    height, rows = left.shape
    width = right.shape[1]
    return pl.pallas_call(
        later(outer_tall_kernel, 1, after),
        out_shape=(jax.ShapeDtypeStruct((rows, width), LOW), AT),
        grid_spec=pltpu.PrefetchScalarGridSpec(
            num_scalar_prefetch=1,
            grid=(rows // tile,),
            in_specs=[ANY] * len(after)
            + [pl.BlockSpec((height, tile), lambda i, at: (0, i)), whole_block(height, width)],
            out_specs=(tiled(tile, width), AT_SPEC),
        ),
        compiler_params=params(),
        cost_estimate=cost(2 * height * rows * width),
    )(at, *after, left, right)


def outer_row_kernel(count, tile, at, turned, extra, *refs):
    rights, (out, at_ref) = refs[:count], refs[count:]
    step = pl.program_id(0)
    total = out.shape[1] - EXTRA
    steps = total // tile // count
    for place in range(count * steps):

        @pl.when(step == place)
        def _(place=place):
            out[:, place * tile : (place + 1) * tile] = nn(turned[...], rights[place // steps][...]).astype(LOW)

    @first_step
    def _():
        hand_on(at, at_ref)
        lines = jnp.zeros((EXTRA - extra.shape[0], extra.shape[1]), F32)
        out[:, total:] = jnp.concatenate([extra[...], lines], axis=0).T.astype(LOW)


def outer_row(at, turned, rights, extra, tile=512, after=()):
    rows, height = turned.shape
    steps = rights[0].shape[1] // tile
    count = len(rights)
    width = count * steps * tile

    def column(index):
        return pl.BlockSpec((height, tile), lambda i, at: (0, jnp.clip(i - index * steps, 0, steps - 1)))

    return pl.pallas_call(
        later(functools.partial(outer_row_kernel, count, tile), 1, after),
        out_shape=(jax.ShapeDtypeStruct((rows, width + EXTRA), LOW), AT),
        grid_spec=pltpu.PrefetchScalarGridSpec(
            num_scalar_prefetch=1,
            grid=(count * steps,),
            in_specs=[ANY] * len(after)
            + [whole_block(rows, height), whole_block(*extra.shape)]
            + [column(index) for index in range(count)],
            out_specs=(whole_block(rows, width + EXTRA), AT_SPEC),
        ),
        compiler_params=params(),
        cost_estimate=cost(2 * height * rows * width),
    )(at, *after, turned, extra, *rights)


def outer_wide_kernel(flip, owners, firsts, tile, extra, at, *refs):
    count = max(owners) + 1
    turned, rights = refs[:count], refs[count : count + len(owners)]
    if extra:
        extra_ref, out, at_ref, lines, held, sem = refs[-6:]
    else:
        out, at_ref, held, sem = refs[-4:]
    step = pl.program_id(0)
    half = held.shape[1] // 16

    def load():
        hand_on(at, at_ref)
        copies = []
        for index, ref in enumerate(turned):
            for group in range(4):
                for k in range(4):
                    row = pl.multiple_of(source(at, flip, group, k) * half, half)
                    copies.append(
                        pltpu.make_async_copy(
                            ref.at[pl.ds(row, half)], held.at[index, pl.ds((group * 4 + k) * half, half)], sem
                        )
                    )
        for copy in copies:
            copy.start()
        for copy in copies:
            copy.wait()

    first_step(load)
    if extra:
        @first_step
        def _():
            rest = jnp.zeros((EXTRA - extra_ref.shape[0], extra_ref.shape[1]), F32)
            lines[...] = jnp.concatenate([extra_ref[...], rest], axis=0).T.astype(LOW)
            for group in range(4):
                for k in range(4):
                    row = pl.multiple_of(source(at, flip, group, k) * half, half)
                    out[group * 4 + k, :, tile * firsts[-1] :] = lines[pl.ds(row, half), :]

    for index, owner in enumerate(owners):
        if extra:
            for place in range(firsts[index], firsts[index + 1]):

                @pl.when(step == place)
                def _(index=index, owner=owner, place=place):
                    result = nn(held[owner], rights[index][...]).astype(LOW)
                    out[:, :, place * tile : (place + 1) * tile] = result.reshape(16, half, tile)

            continue

        @pl.when((step >= firsts[index]) & (step < firsts[index + 1]))
        def _(index=index, owner=owner):
            result = nn(held[owner], rights[index][...]).astype(LOW)
            out[...] = result.reshape(out.shape)


def outer_wide(at, turned, rights, owners, flip, tile=1024, extra=None, after=()):
    rows, height = turned[0].shape
    half = rows // 32
    counts = [right.shape[1] // tile for right in rights]
    firsts = [sum(counts[:i]) for i in range(len(counts) + 1)]
    width = tile * firsts[-1]
    more = [] if extra is None else [extra]
    wide = width + EXTRA * len(more)
    block = pl.BlockSpec((16, half, tile), lambda i, at: (0, 0, i))
    if more:
        block = pl.BlockSpec((16, half, wide), lambda i, at: (0, 0, 0))

    def column(index):
        return pl.BlockSpec((height, tile), lambda i, at: (0, jnp.clip(i - firsts[index], 0, counts[index] - 1)))

    return pl.pallas_call(
        later(functools.partial(outer_wide_kernel, flip, tuple(owners), tuple(firsts), tile, bool(more)), 1, after),
        out_shape=(jax.ShapeDtypeStruct((16, half, wide), LOW), AT),
        grid_spec=pltpu.PrefetchScalarGridSpec(
            num_scalar_prefetch=1,
            grid=(firsts[-1],),
            in_specs=[ANY] * len(after)
            + [ANY] * len(turned)
            + [column(index) for index in range(len(rights))]
            + [whole_block(*line.shape) for line in more],
            out_specs=(block, AT_SPEC),
            scratch_shapes=[pltpu.VMEM((rows, EXTRA), LOW) for line in more]
            + [pltpu.VMEM((len(turned), rows // 2, height), LOW), pltpu.SemaphoreType.DMA],
        ),
        compiler_params=params(),
        cost_estimate=cost(height * rows * width),
    )(at, *after, *turned, *rights, *more)


def owned_sum(whole):
    return lax.psum_scatter(whole, "fsdp", scatter_dimension=0, tiled=True)


def copies_sum(plan, at, owned):
    if plan.copies == 2:
        owned = owned + at[4].astype(LOW)
        return owned.astype(F32) + plan.other_copy(owned).astype(F32)
    return lax.psum(owned, "rep").astype(F32)


def back_kernel(plan, count, at, branch_ref, dq_ref, dk_ref, dv_ref, *refs):
    pieces, (out_ref, at_ref, weight, sems) = refs[:count], refs[count:]
    width = dq_ref.shape[1]

    def load():
        hand_on(at, at_ref)
        groups = [(pieces, weight, weight.shape[0], True)]
        fetch(plan, at, groups, sems)
        wait_for(plan, at, groups, sems, 0)

    first_step(load)

    total = branch_ref[...].astype(F32)
    for index, ref in enumerate((dq_ref, dk_ref, dv_ref)):
        total = total + nt(ref[...], weight[:, index * width : (index + 1) * width])
    out_ref[...] = total.astype(LOW)


def back(plan, at, branch, dq, dk, dv, pieces, tile=256, after=()):
    count = len(pieces)
    height, depth = branch.shape
    width = dq.shape[1]
    tiled = pl.BlockSpec((tile, depth), lambda i, at: (i, 0))
    return pl.pallas_call(
        later(functools.partial(back_kernel, plan, count), 1, after),
        out_shape=(jax.ShapeDtypeStruct((height, depth), LOW), AT),
        grid_spec=pltpu.PrefetchScalarGridSpec(
            num_scalar_prefetch=1,
            grid=(height // tile,),
            in_specs=[ANY] * len(after)
            + [tiled] * 4 + [ANY] * count,
            out_specs=(tiled, AT_SPEC),
            scratch_shapes=[pltpu.VMEM((depth, 3 * width + EXTRA), LOW), pltpu.SemaphoreType.DMA((1,))],
        ),
        compiler_params=params(),
        cost_estimate=cost(6 * height * depth * width),
    )(at, *after, branch, dq, dk, dv, *pieces)


def body(
    tokens, seq_lengths, out_cotangent, project_in, project_out, expand, contract,
    query_bias, value_bias, out_bias, expand_bias, contract_bias,
    first_gain, first_shift, second_gain, second_shift,
    *, shards, copies,
):
    plan = Plan(shards, copies)
    at = place()
    depth = tokens.shape[1]
    hidden = expand.shape[1]
    part, wide_part = query_bias.shape[0], expand_bias.shape[0]

    def columns(*vectors):
        table = jnp.stack([vector for vector in vectors], axis=1)
        return jnp.pad(table, ((0, 0), (0, EXTRA - len(vectors))))

    zero = jnp.zeros_like(query_bias)
    in_shard = jnp.concatenate([project_in, columns(query_bias, value_bias)], axis=1)
    wide_bias = tuple(expand_bias[i * part : (i + 1) * part] for i in range(wide_part // part))
    small = (out_bias, contract_bias, first_gain, first_shift, second_gain, second_shift, zero, zero)
    wide_shard = jnp.concatenate([expand, project_out, columns(*small, *wide_bias)], axis=1)
    width = project_in.shape[1]
    if plan.split:
        in_beside, in_parts = plan.gather_z(at, in_shard, True)
        in_far, in_across, in_other = plan.gather_xy(at, in_shard, in_parts, True)
        unused, wide_parts = plan.gather_z(pinned(at, in_parts[2]), wide_shard)
        in_corners = plan.gather_corner(at, in_shard, in_across, in_other, True)
        in_main = (in_shard, in_beside, in_far, in_across, in_other)
        at_wide = pinned(at, *wide_parts)
        in_cores = plan.gather_core(at, *in_main) + plan.gather_core(at_wide, *in_corners)
        in_pieces = list(in_main + in_corners) + in_cores
        at_core = pinned(at_wide, *in_corners)
        wide_far, wide_across, wide_other = plan.gather_xy(at_core, wide_shard, wide_parts)
        contract_pieces = [lax.all_gather(contract + pinned(at_core, wide_across, wide_other)[4].astype(LOW), "fsdp", axis=0, tiled=True)]
        wide_corners = plan.gather_corner(at_core, wide_shard, wide_across, wide_other)
    else:
        in_pieces, wide_pieces, contract_pieces = (
            [lax.all_gather(shard, "fsdp", axis=0, tiled=True)] for shard in (in_shard, wide_shard, contract)
        )
    first_after = [wide_across, wide_other] if plan.split else []
    projected, tokens_turned, at = project(plan, at, tokens, in_pieces, depth, width, after=first_after)
    if plan.split:
        wide_main = (wide_shard, wide_far, wide_across, wide_other)
        attended, attended_turned, logs, at = attend(at, seq_lengths, projected, after=wide_corners)
        wide_pieces = list(wide_main + wide_corners)
        wide_pieces += plan.gather_core(at, *wide_main) + plan.gather_core(at, *wide_corners)
    else:
        attended, attended_turned, logs, at = attend(at, seq_lengths, projected)
    active, slope, normal, scale, first, first_turned, table, at = up(plan, at, tokens, attended, hidden, wide_pieces)
    result, second, sums, at = over(plan, at, first, active, out_cotangent, table, contract_pieces)
    whole, at = outer_tall(at, active, second)
    contract_owned = owned_sum(whole)
    grad_expanded, branch, grad_attended, more_sums, wide_sums, at = down(
        plan, at, second, slope, normal, scale, table, wide_pieces, contract_pieces
    )
    lines = wide_sums[0].reshape(shards, wide_part // part, part).transpose(1, 0, 2).reshape(-1, depth)
    lines = jnp.concatenate([sums[:6] + more_sums[:6], lines], axis=0)
    lines = jnp.pad(lines, ((0, 14 - lines.shape[0]), (0, 0)))
    if plan.split:
        turned, rights, owners = (first_turned, attended_turned), (grad_expanded, branch), (0, 1)
        theirs, at = outer_wide(at, turned, rights, owners, 1)
        e_got = plan.flip(theirs, 1)
        e_mine, at = outer_wide(at, turned, rights, owners, 0)
        e_corners = plan.scatter_corner(at, e_mine, e_got)
        dq, dk, dv, back_sums, at = attend_back(at, seq_lengths, projected, attended_turned, grad_attended, logs)
        e_across, e_other = plan.scatter_xy(at, e_mine, e_got, *e_corners)
        extra = jnp.concatenate([back_sums[:2], lines], axis=0)
        turned, rights, owners = (tokens_turned,), (dq, dk, dv), (0, 0, 0)
        theirs, at = outer_wide(at, turned, rights, owners, 1, extra=extra, after=[*e_corners, contract_owned])
        contract_sum = copies_sum(plan, at, contract_owned)
        i_got = plan.flip(theirs, 1)
        i_mine, at = outer_wide(at, turned, rights, owners, 0, extra=extra)
        e_parts = plan.scatter_z(at, e_mine, e_got, e_across, e_other)
        i_corners = plan.scatter_corner(at, i_mine, i_got)
        grad_tokens, at = back(plan, at, branch, dq, dk, dv, in_pieces, after=[i_got])
        i_across, i_other = plan.scatter_xy(at, i_mine, i_got, *i_corners)
        e_ends = plan.scatter_end(at, e_parts)
        i_parts = plan.scatter_z(at, i_mine, i_got, i_across, i_other)
        owned = jnp.concatenate(plan.scatter_end(at, i_parts), axis=0)
        grad_wide = jnp.concatenate(e_ends, axis=0)
        grad_expand, grad_project_out = grad_wide[:, :hidden], grad_wide[:, hidden:]
    else:
        none = jnp.zeros((8, depth), F32)
        whole, at = outer_row(at, first_turned, (grad_expanded,), none)
        grad_expand = copies_sum(plan, at, owned_sum(whole))[:, :hidden]
        whole, at = outer_row(at, attended_turned, (branch,), none)
        grad_project_out = copies_sum(plan, at, owned_sum(whole))[:, :depth]
        dq, dk, dv, back_sums, at = attend_back(at, seq_lengths, projected, attended_turned, grad_attended, logs)
        extra = jnp.concatenate([back_sums[:2], lines], axis=0)
        whole, at = outer_row(at, tokens_turned, (dq, dk, dv), extra)
        owned = copies_sum(plan, at, owned_sum(whole))
        contract_sum = copies_sum(plan, at, contract_owned)
        grad_tokens, at = back(plan, at, branch, dq, dk, dv, in_pieces)
    grad_contract = contract_sum
    grad_project_in = owned[:, :width]
    small = owned[:, width : width + 8 + wide_part // part].T
    grad_query, grad_value, grad_out, grad_down, gain_one, shift_one, gain_two, shift_two = (small[i] for i in range(8))
    grad_wide_bias = small[8:].reshape(-1)
    return (
        result, grad_tokens, grad_project_in, grad_project_out, grad_expand, grad_contract,
        grad_query, grad_value, grad_out, grad_wide_bias, grad_down,
        gain_one, shift_one, gain_two, shift_two,
    )


def solution(mesh):
    split, row, vector = P(("fsdp", "rep"), None), P("fsdp", None), P("fsdp")
    return jax.shard_map(
        functools.partial(body, shards=mesh.shape["fsdp"], copies=mesh.shape["rep"]),
        mesh=mesh,
        in_specs=(split,) * 3 + (row,) * 4 + (vector,) * 9,
        out_specs=(split,) * 2 + (row,) * 4 + (vector,) * 9,
        check_vma=False,
    )
```

time: 621 us -> 507 us (0.82)
  blocking collectives: 93.1 us -> 0 us
  starting transfers between devices: 93.4 us -> 39.4 us
  waiting for transfers between devices: 172 us -> 129 us
  Pallas kernels: 200 us -> 228 us
  between operations: 1.94 us -> 29.6 us
  other arithmetic: 29.6 us -> 44.3 us
  local copies, waits for them, and re-layouts: 21.7 us -> 32.1 us
    unnamed x1 -> x0, blocking collectives: 62.8 us -> none
    ppermute x64 -> x27, starting transfers between devices: 65.2 us -> 28.8 us  [flip(): lax.ppermute(value, 'fsdp', [(i, i ^ bits) for i in range(self.shards)])]
    ppermute x64 -> x27, waiting for transfers between devices: 118 us -> 83.4 us  [flip(): lax.ppermute(value, 'fsdp', [(i, i ^ bits) for i in range(self.shards)])]
    pallas_call x9 -> x12, Pallas kernels: 200 us -> 228 us  [the longest x4 46.8 us: outer_wide(): pl.pallas_call(later(functools.partial(outer_wide_kernel, flip, tuple(own...]
    all_gather x1 -> x0, blocking collectives: 25.1 us -> none  [body(): packed = lax.all_gather(packed, 'fsdp', axis=0, tiled=True)]
    ppermute x20 -> x11, starting transfers between devices: 28.3 us -> 10.3 us  [other_copy(): return lax.ppermute(value, 'rep', [(0, 1), (1, 0)])]
    add x0 -> x16, other arithmetic: none -> 16.3 us  [the longest x8 8.28 us: gather_core(): piece + at[4].astype(LOW)]
    ppermute x20 -> x11, waiting for transfers between devices: 53.5 us -> 42.9 us  [other_copy(): return lax.ppermute(value, 'rep', [(0, 1), (1, 0)])]
  transfers between devices with their start and end apart: 84 -> 40, of which waited for: 28 -> 21; matrix products, arithmetic and copies ran while one was open for 8% -> 13% of each run, Pallas kernels for 22% -> 36%
where the time goes in v2:
time: 507 us; the launch traced here: 502 us
  Pallas kernels  228 us (45%)
  waiting for transfers between devices  129 us (25%)
  other arithmetic  44.3 us (9%)
  starting transfers between devices  39.4 us (8%)
  local copies, waits for them, and re-layouts  32.1 us (6%)
  between operations  29.6 us (6%)
    ppermute x27, waiting for transfers between devices, flip(): lax.ppermute(value, 'fsdp', [(i, i ^ bits) for i in range(self.shards)])  83.4 us
    pallas_call x4, Pallas kernels, outer_wide(): pl.pallas_call(later(functools.partial(outer_wide_kernel, flip, tuple(own...  46.8 us
    ppermute x11, waiting for transfers between devices, other_copy(): return lax.ppermute(value, 'rep', [(0, 1), (1, 0)])  42.9 us
    pallas_call x1, Pallas kernels, down(): pl.pallas_call(later(functools.partial(down_kernel, plan, (len(wide_piece...  34.8 us
    pallas_call x1, Pallas kernels, attend_back(): pl.pallas_call(later(attend_back_kernel, 2, after), out_shape=(jax.ShapeD...  32.9 us
    ppermute x27, starting transfers between devices, flip(): lax.ppermute(value, 'fsdp', [(i, i ^ bits) for i in range(self.shards)])  28.8 us
    pallas_call x1, Pallas kernels, up(): pl.pallas_call(later(functools.partial(up_kernel, plan, chunk), 1, after)...  25.7 us
    pallas_call x1, Pallas kernels, attend(): pl.pallas_call(later(attend_kernel, 2, after), out_shape=(jax.ShapeDtypeS...  24.4 us
  transfers between devices with their start and end apart: 40, of which 21 were waited for; matrix products, arithmetic and copies ran while one was open for 13% of the time, Pallas kernels for 36%

profile of v2, /device:TPU:0, one launch (start us, length us, event | category | flops | bytes accessed | tf_op | source)
XLA Modules:
  0.0 501.8 jit_solution(1091779328064524877)
XLA Ops:
  9.9 4.1 collective-permute-start.5
  20.2 8.9 %collective-permute-done = bf16[32,3200]{1,0:T(8,128)(2,1)S(1)} collective-permute-done((bf16[32,3200]{1,0:T(8,128)(2,1)S(1)}, bf16[32,3200]{1,0:T(8,128)(2,1)S(1)}, u32[]{:S(2)}, u32[]{:S(2)}) %collective-permute-start) | collective-permute-done | bytes 204832 | tf_op jit(solution)/shard_map/ppermute | solution.py:71
  44.1 5.2 %collective-permute-done.3 = bf16[32,5248]{1,0:T(8,128)(2,1)S(1)} collective-permute-done((bf16[32,5248]{1,0:T(8,128)(2,1)S(1)}, bf16[32,5248]{1,0:T(8,128)(2,1)S(1)}, u32[]{:S(2)}, u32[]{:S(2)}) %collective-permute-start.3) | collective-permute-done | bytes 335904 | tf_op jit(solution)/shard_map/ppermute | solution.py:71
  50.5 18.8 %collective-permute-done.2 = bf16[32,5248]{1,0:T(8,128)(2,1)S(1)} collective-permute-done((bf16[32,5248]{1,0:T(8,128)(2,1)S(1)}, bf16[32,5248]{1,0:T(8,128)(2,1)S(1)}, u32[]{:S(2)}, u32[]{:S(2)}) %collective-permute-start.2) | collective-permute-done | bytes 335904 | tf_op jit(solution)/shard_map/ppermute | solution.py:71
  75.3 4.4 collective-permute-done.7.refs_9_.refs_11_
  98.6 21.4 %collective-permute-done.11.refs_2_.refs_6_.refs_9_ = bf16[96,5248]{1,0:T(8,128)(2,1)} collective-permute-done((bf16[96,5248]{1,0:T(8,128)(2,1)}, bf16[96,5248]{1,0:T(8,128)(2,1)}, u32[]{:S(2)}, u32[]{:S(2)}) %collective-permute-start.11) | collective-permute-done | bytes 1007648 | tf_op jit(solution)/shard_map/ppermute | solution.py:74
  124.4 5.6 %collective-permute-done.10.refs_1_.refs_5_.refs_8_ = bf16[128,5248]{1,0:T(8,128)(2,1)S(1)} collective-permute-done((bf16[128,5248]{1,0:T(8,128)(2,1)}, bf16[128,5248]{1,0:T(8,128)(2,1)S(1)}, u32[]{:S(2)}, u32[]{:S(2)}) %collective-permute-start.10) | collective-permute-done | bytes 1343520 | tf_op jit(solution)/shard_map/ppermute | solution.py:71
  136.1 14.2 %shard_map.271 = (bf16[1024,3072]{1,0:T(8,128)(2,1)}, bf16[1024,1024]{1,0:T(8,128)(2,1)}, s32[5]{0:T(128)}) custom-call(s32[5]{0:T(128)} %copy-done.28, bf16[128,5248]{1,0:T(8,128)(2,1)} %copy-done.2, bf16[96,5248]{1,0:T(8,128)(2,1)} %collective-permute-done.11.refs_2_.refs_6_.refs_9_, bf16[1024,1024]{1,0:T(8,128)(2,1)} %refs_1_.1, ...), custom_call_target="tpu_custom_call" | custom-call | flops 12884901888 | bytes 40265320 | tf_op jit(solution)/shard_map/pallas_call | solution.py:233
  151.1 24.4 %shard_map.272 = (bf16[1024,1024]{1,0:T(8,128)(2,1)}, bf16[1024,1024]{1,0:T(8,128)(2,1)}, f32[16,8,512]{2,1,0:T(8,128)}, s32[5]{0:T(128)}) custom-call(s32[2,4]{1,0:T(2,128)} %refs_0_.3, s32[5]{0:T(128)} %get-tuple-element.57.refs_1_, bf16[64,5248]{1,0:T(8,128)(2,1)} %copy-done.11, bf16[64,5248]{1,0:T(8,128)(2,1)} %collective-permute-done.16.refs_3_.refs_8_.refs_11_, ...), custom_call_target="tpu_custom_call" | custom-call | flops 25769803776 | bytes 80530640 | tf_op jit(solution)/shard_map/pallas_call | solution.py:324
  185.1 5.8 %collective-permute-done.18.refs_10_.refs_13_ = bf16[128,5248]{1,0:T(8,128)(2,1)S(1)} collective-permute-done((bf16[128,5248]{1,0:T(8,128)(2,1)S(1)}, bf16[128,5248]{1,0:T(8,128)(2,1)S(1)}, u32[]{:S(2)}, u32[]{:S(2)}) %collective-permute-start.18) | collective-permute-done | bytes 1343520 | tf_op jit(solution)/shard_map/ppermute | solution.py:71
  193.3 25.7 %shard_map.273 = (bf16[1024,4096]{1,0:T(8,128)(2,1)}, bf16[1024,4096]{1,0:T(8,128)(2,1)}, bf16[1024,1024]{1,0:T(8,128)(2,1)}, f32[1024,128]{1,0:T(8,128)}, f32[1...) custom-call(s32[5]{0:T(128)} %get-tuple-element.59.refs_0_, ...), custom_call_target="tpu_custom_call" | custom-call | flops 21474836480 | bytes 67108864 | tf_op jit(solution)/shard_map/pallas_call | solution.py:517
  219.0 20.6 %shard_map.274 = (bf16[1024,1024]{1,0:T(8,128)(2,1)}, bf16[1024,1024]{1,0:T(8,128)(2,1)}, f32[8,1024]{1,0:T(8,128)}, s32[5]{0:T(128)}) custom-call(s32[5]{0:T(128)} %get-tuple-element.61.refs_0_, f32[1024,1024]{1,0:T(8,128)} %get-tuple-element.62.refs_1_, bf16[1024,4096]{1,0:T(8,128)(2,1)} %get-tuple-element.63.refs_2_.refs_1_, bf16[1024,1024]{1,0:T(8,128)(2,1)} %refs_3_.3, ...), custom_call_target="tpu_custom_call" | custom-call | flops 17179869184 | bytes 53687092 | tf_op jit(solution)/shard_map/pallas_call | solution.py:581
  239.6 15.1 %shard_map.275 = (bf16[4096,1024]{1,0:T(8,128)(2,1)}, s32[5]{0:T(128)}) custom-call(s32[5]{0:T(128)} %get-tuple-element.66.refs_0_, bf16[1024,4096]{1,0:T(8,128)(2,1)} %get-tuple-element.63.refs_2_.refs_1_, bf16[1024,1024]{1,0:T(8,128)(2,1)} %get-tuple-element.67.refs_2_.refs_1_), custom_call_target="tpu_custom_call" | custom-call | flops 17179869184 | bytes 53687092 | tf_op jit(solution)/shard_map/pallas_call | solution.py:697
  254.8 34.8 %shard_map.276 = (bf16[1024,4096]{1,0:T(8,128)(2,1)}, bf16[1024,1024]{1,0:T(8,128)(2,1)}, bf16[1024,1024]{1,0:T(8,128)(2,1)}, f32[8,1024]{1,0:T(8,128)}, f32[8,4096]{1,0:T(8,128)}, /*index=5*/s32[5]{0:T(128)}) custom-call(s32[5]{0:T(128)} %get-tuple-element.68.refs_0_, bf16[1024,1024]{1,0:T(8,128)(2,1)} %get-tuple-element.67.refs_2_.refs_1_, ...), custom_call_target="tpu_custom_call" | custom-call | flops 38654705664 | bytes 120795952 | tf_op jit(solution)/shard_map/pallas_call | solution.py:656
  289.6 12.9 %shard_map.277 = (bf16[16,32,5120]{2,1,0:T(8,128)(2,1)}, s32[5]{0:T(128)}) custom-call(s32[5]{0:T(128)} %get-tuple-element.72.refs_0_, bf16[1024,1024]{1,0:T(8,128)(2,1)} %get-tuple-element.73.refs_1_, bf16[1024,1024]{1,0:T(8,128)(2,1)} %get-tuple-element.74.refs_2_.refs_5_, bf16[1024,4096]{1,0:T(8,128)(2,1)} %get-tuple-element.75.refs_3_, ...), custom_call_target="tpu_custom_call" | custom-call | flops 10737418240 | bytes 33554432 | tf_op jit(solution)/shard_map/pallas_call | solution.py:825
  302.9 12.9 %shard_map.278 = (bf16[16,32,5120]{2,1,0:T(8,128)(2,1)}, s32[5]{0:T(128)}) custom-call(s32[5]{0:T(128)} %get-tuple-element.77.refs_0_, bf16[1024,1024]{1,0:T(8,128)(2,1)} %get-tuple-element.73.refs_1_, bf16[1024,1024]{1,0:T(8,128)(2,1)} %get-tuple-element.74.refs_2_.refs_5_, bf16[1024,4096]{1,0:T(8,128)(2,1)} %get-tuple-element.75.refs_3_, ...), custom_call_target="tpu_custom_call" | custom-call | flops 10737418240 | bytes 33554432 | tf_op jit(solution)/shard_map/pallas_call | solution.py:825
  320.7 32.9 %shard_map.279 = (bf16[1024,1024]{1,0:T(8,128)(2,1)}, bf16[1024,1024]{1,0:T(8,128)(2,1)}, bf16[1024,1024]{1,0:T(8,128)(2,1)}, f32[8,1024]{1,0:T(8,128)}, s32[5]{0:T(128)}) custom-call(s32[2,4]{1,0:T(2,128)} %refs_0_.3, s32[5]{0:T(128)} %get-tuple-element.78.refs_1_, bf16[1024,3072]{1,0:T(8,128)(2,1)} %get-tuple-element.58.refs_4_.refs_5_.refs_6_.refs_2_.refs_3_, ...), custom_call_target="tpu_custom_call" | custom-call | flops 26843545600 | bytes 83886080 | tf_op jit(solution)/shard_map/pallas_call | solution.py:422
  365.1 10.6 %shard_map.280 = (bf16[16,32,3200]{2,1,0:T(8,128)(2,1)}, s32[5]{0:T(128)}) custom-call(s32[5]{0:T(128)} %get-tuple-element.81.refs_0_, bf16[2,32,5120]{2,1,0:T(8,128)(2,1)} %copy-done.14, bf16[2,32,5120]{2,1,0:T(8,128)(2,1)} %copy-done.13, bf16[256,1024]{1,0:T(8,128)(2,1)} %reduce-scatter.2.cloned.1.call-done.refs_3_, ...), custom_call_target="tpu_custom_call" | custom-call | flops 6442450944 | bytes 20132660 | tf_op jit(solution)/shard_map/pallas_call | solution.py:825
  382.8 10.3 %shard_map.281 = (bf16[16,32,3200]{2,1,0:T(8,128)(2,1)}, s32[5]{0:T(128)}) custom-call(s32[5]{0:T(128)} %get-tuple-element.93.refs_0_, bf16[1024,1024]{1,0:T(8,128)(2,1)} %get-tuple-element.85.refs_4_.refs_1_, bf16[1024,1024]{1,0:T(8,128)(2,1)} %get-tuple-element.86.refs_5_.refs_2_.refs_3_, bf16[1024,1024]{1,0:T(8,128)(2,1)} %get-tuple-element.87.refs_6_.refs_3_.refs_4_, ...), custom_call_target="tpu_custom_call" | custom-call | flops 6442450944 | bytes 20132660 | tf_op jit(solution)/shard_map/pallas_call | solution.py:825
  395.0 13.9 %collective-permute-done.32 = bf16[4,32,5120]{2,1,0:T(8,128)(2,1)} collective-permute-done((bf16[4,32,5120]{2,1,0:T(8,128)(2,1)}, bf16[4,32,5120]{2,1,0:T(8,128)(2,1)}, u32[]{:S(2)}, u32[]{:S(2)}) %collective-permute-start.32) | collective-permute-done | bytes 1310752 | tf_op jit(solution)/shard_map/ppermute | solution.py:74
  413.0 13.4 %shard_map.282 = (bf16[1024,1024]{1,0:T(8,128)(2,1)}, s32[5]{0:T(128)}) custom-call(s32[5]{0:T(128)} %get-tuple-element.94.refs_0_, bf16[16,32,3200]{2,1,0:T(8,128)(2,1)} %collective-permute-done.22.refs_1_, bf16[1024,1024]{1,0:T(8,128)(2,1)} %get-tuple-element.76.refs_4_.refs_2_, bf16[1024,1024]{1,0:T(8,128)(2,1)} %get-tuple-element.86.refs_5_.refs_2_.refs_3_, ...), custom_call_target="tpu_custom_call" | custom-call | flops 12884901888 | bytes 40265320 | tf_op jit(solution)/shard_map/pallas_call | solution.py:878
  445.8 6.8 %collective-permute-done.35 = bf16[32,5120]{1,0:T(8,128)(2,1)S(1)} collective-permute-done((bf16[32,5120]{1,0:T(8,128)(2,1)S(1)}, bf16[32,5120]{1,0:T(8,128)(2,1)S(1)}, u32[]{:S(2)}, u32[]{:S(2)}) %collective-permute-start.35) | collective-permute-done | bytes 327712 | tf_op jit(solution)/shard_map/ppermute | solution.py:71
  452.6 11.2 %collective-permute-done.34 = bf16[32,5120]{1,0:T(8,128)(2,1)S(1)} collective-permute-done((bf16[32,5120]{1,0:T(8,128)(2,1)S(1)}, bf16[32,5120]{1,0:T(8,128)(2,1)S(1)}, u32[]{:S(2)}, u32[]{:S(2)}) %collective-permute-start.34) | collective-permute-done | bytes 327712 | tf_op jit(solution)/shard_map/ppermute | solution.py:71
  478.5 7.4 %collective-permute-done.28 = bf16[32,3200]{1,0:T(8,128)(2,1)S(1)} collective-permute-done((bf16[32,3200]{1,0:T(8,128)(2,1)S(1)}, bf16[32,3200]{1,0:T(8,128)(2,1)S(1)}, u32[]{:S(2)}, u32[]{:S(2)}) %collective-permute-start.28) | collective-permute-done | bytes 204832 | tf_op jit(solution)/shard_map/ppermute | solution.py:71
  (232 shorter events, 130.9 us)
Async XLA Ops:
  7.2 211.8 %all-gather.2.cloned.1.call-start = ((), (), s32[]{:S(2)}) async-start(), calls=%async_computation.1 | async-start | bytes 8912896 | tf_op jit(solution)/shard_map/all_gather | solution.py:927
  9.9 23.2 %collective-permute-start.5 = (bf16[32,3200]{1,0:T(8,128)(2,1)S(1)}, bf16[32,3200]{1,0:T(8,128)(2,1)S(1)}, u32[]{:S(2)}, u32[]{:S(2)}) collective-permute-start(bf16[32,3200]{1,0:T(8,128)(2,1)S(1)} %constant_dynamic-slice_fusion.5), channel_id=1, source_target_pairs={{0,16},{2,18},{4,20},{6,22},{8,24},{10,26},{12,28},{14,30},{16,0},... | collective-permute-start | bytes 614408 | tf_op jit(solution)/shard_map/ppermute | solution.py:71
  14.0 18.3 %collective-permute-start.4 = (bf16[32,3200]{1,0:T(8,128)(2,1)S(1)}, bf16[32,3200]{1,0:T(8,128)(2,1)S(1)}, u32[]{:S(2)}, u32[]{:S(2)}) collective-permute-start(bf16[32,3200]{1,0:T(8,128)(2,1)S(1)} %constant_dynamic-slice_fusion.5), channel_id=1, source_target_pairs={{0,8},{2,10},{4,12},{6,14},{8,0},{10,2},{12,4},{14,6},{16,24},{18,... | collective-permute-start | bytes 614408 | tf_op jit(solution)/shard_map/ppermute | solution.py:71
  34.5 37.8 %collective-permute-start.8 = (bf16[96,3200]{1,0:T(8,128)(2,1)S(1)}, bf16[96,3200]{1,0:T(8,128)(2,1)S(1)}, u32[]{:S(2)}, u32[]{:S(2)}) collective-permute-start(bf16[96,3200]{1,0:T(8,128)(2,1)S(1)} %get-tuple-element.140.refs_6_.refs_8_), channel_id=1, source_target_pairs={{0,4},{2,6},{4,0},{6,2},{8,12},{10,14},{12,8},{14,10},{16,20},{18,... | collective-permute-start | bytes 1843208 | tf_op jit(solution)/shard_map/ppermute | solution.py:71
  36.1 36.9 %collective-permute-start.6 = (bf16[96,3200]{1,0:T(8,128)(2,1)S(1)}, bf16[96,3200]{1,0:T(8,128)(2,1)S(1)}, u32[]{:S(2)}, u32[]{:S(2)}) collective-permute-start(bf16[96,3200]{1,0:T(8,128)(2,1)S(1)} %get-tuple-element.140.refs_6_.refs_8_), channel_id=1, source_target_pairs={{0,1},{1,0},{2,3},{3,2},{4,5},{5,4},{6,7},{7,6},{8,9},{9,8},{10,11... | collective-permute-start | bytes 1843208 | tf_op jit(solution)/shard_map/ppermute | solution.py:74
  40.2 29.1 %collective-permute-start.2 = (bf16[32,5248]{1,0:T(8,128)(2,1)S(1)}, bf16[32,5248]{1,0:T(8,128)(2,1)S(1)}, u32[]{:S(2)}, u32[]{:S(2)}) collective-permute-start(bf16[32,5248]{1,0:T(8,128)(2,1)S(1)} %constant_dynamic-slice_fusion.4), channel_id=1, source_target_pairs={{0,16},{2,18},{4,20},{6,22},{8,24},{10,26},{12,28},{14,30},{16,0},... | collective-permute-start | bytes 1007624 | tf_op jit(solution)/shard_map/ppermute | solution.py:71
  43.6 26.9 %collective-permute-start.1 = (bf16[32,5248]{1,0:T(8,128)(2,1)S(1)}, bf16[32,5248]{1,0:T(8,128)(2,1)S(1)}, u32[]{:S(2)}, u32[]{:S(2)}) collective-permute-start(bf16[32,5248]{1,0:T(8,128)(2,1)S(1)} %constant_dynamic-slice_fusion.4), channel_id=1, source_target_pairs={{0,8},{2,10},{4,12},{6,14},{8,0},{10,2},{12,4},{14,6},{16,24},{18,... | collective-permute-start | bytes 1007624 | tf_op jit(solution)/shard_map/ppermute | solution.py:71
  75.3 60.7 %collective-permute-start.13 = (bf16[416,3200]{1,0:T(8,128)(2,1)}, bf16[416,3200]{1,0:T(8,128)(2,1)}, u32[]{:S(2)}, u32[]{:S(2)}) collective-permute-start(bf16[416,3200]{1,0:T(8,128)(2,1)} %constant_dynamic-update-slice_fusion.3), channel_id=1, source_target_pairs={{0,2},{2,0},{4,6},{6,4},{8,10},{10,8},{12,14},{14,12},{16,18},{18,... | collective-permute-start | bytes 7987208 | tf_op jit(solution)/shard_map/ppermute | solution.py:71
  91.8 44.3 %collective-permute-start.14 = (bf16[96,3200]{1,0:T(8,128)(2,1)}, bf16[96,3200]{1,0:T(8,128)(2,1)}, u32[]{:S(2)}, u32[]{:S(2)}) collective-permute-start(bf16[96,3200]{1,0:T(8,128)(2,1)} %pad_maximum_fusion.9), channel_id=1, source_target_pairs={{0,2},{2,0},{4,6},{6,4},{8,10},{10,8},{12,14},{14,12},{16,18},{18,... | collective-permute-start | bytes 1843208 | tf_op jit(solution)/shard_map/ppermute | solution.py:71
  95.0 25.0 %collective-permute-start.11 = (bf16[96,5248]{1,0:T(8,128)(2,1)}, bf16[96,5248]{1,0:T(8,128)(2,1)}, u32[]{:S(2)}, u32[]{:S(2)}) collective-permute-start(bf16[96,5248]{1,0:T(8,128)(2,1)} %pad_maximum_fusion.5.refs_4_.refs_7_), channel_id=1, source_target_pairs={{0,1},{1,0},{2,3},{3,2},{4,5},{5,4},{6,7},{7,6},{8,9},{9,8},{10,11... | collective-permute-start | bytes 3022856 | tf_op jit(solution)/shard_map/ppermute | solution.py:74
  97.4 32.5 %collective-permute-start.10 = (bf16[128,5248]{1,0:T(8,128)(2,1)}, bf16[128,5248]{1,0:T(8,128)(2,1)S(1)}, u32[]{:S(2)}, u32[]{:S(2)}) collective-permute-start(bf16[128,5248]{1,0:T(8,128)(2,1)} %pad_maximum_fusion.1), channel_id=1, source_target_pairs={{0,4},{2,6},{4,0},{6,2},{8,12},{10,14},{12,8},{14,10},{16,20},{18,... | collective-permute-start | bytes 4030472 | tf_op jit(solution)/shard_map/ppermute | solution.py:71
  123.8 26.4 %collective-permute-start.15 = (bf16[64,5248]{1,0:T(8,128)(2,1)}, bf16[64,5248]{1,0:T(8,128)(2,1)S(1)}, u32[]{:S(2)}, u32[]{:S(2)}) collective-permute-start(bf16[64,5248]{1,0:T(8,128)(2,1)} %pad_maximum_fusion.8), channel_id=1, source_target_pairs={{0,4},{2,6},{4,0},{6,2},{8,12},{10,14},{12,8},{14,10},{16,20},{18,... | collective-permute-start | bytes 2015240 | tf_op jit(solution)/shard_map/ppermute | solution.py:71
  133.3 231.8 %reduce-scatter.2.cloned.1.call-start = ((), (), s32[]{:S(2)}) async-start(), calls=%async_computation.2 | async-start | bytes 8912896 | tf_op jit(solution)/shard_map/reduce_scatter | solution.py:845
  319.8 38.2 %collective-permute-start.21 = (bf16[2,32,5120]{2,1,0:T(8,128)(2,1)S(1)}, bf16[2,32,5120]{2,1,0:T(8,128)(2,1)S(1)}, u32[]{:S(2)}, u32[]{:S(2)}) collective-permute-start(bf16[2,32,5120]{2,1,0:T(8,128)(2,1)S(1)} %get-tuple-element.117), channel_id=1, source_target_pairs={{0,1},{1,0},{2,3},{3,2},{4,5},{5,4},{6,7},{7,6},{8,9},{9,8},{10,11... | collective-permute-start | bytes 1966088 | tf_op jit(solution)/shard_map/ppermute | solution.py:74
  320.6 37.5 %collective-permute-start.20 = (bf16[2,32,5120]{2,1,0:T(8,128)(2,1)S(1)}, bf16[2,32,5120]{2,1,0:T(8,128)(2,1)S(1)}, u32[]{:S(2)}, u32[]{:S(2)}) collective-permute-start(bf16[2,32,5120]{2,1,0:T(8,128)(2,1)S(1)} %get-tuple-element.118), channel_id=1, source_target_pairs={{0,4},{2,6},{4,0},{6,2},{8,12},{10,14},{12,8},{14,10},{16,20},{18,... | collective-permute-start | bytes 1966088 | tf_op jit(solution)/shard_map/ppermute | solution.py:71
  375.7 37.3 %collective-permute-start.22 = (bf16[16,32,3200]{2,1,0:T(8,128)(2,1)}, bf16[16,32,3200]{2,1,0:T(8,128)(2,1)}, u32[]{:S(2)}, u32[]{:S(2)}) collective-permute-start(bf16[16,32,3200]{2,1,0:T(8,128)(2,1)} %get-tuple-element.95), channel_id=1, source_target_pairs={{0,2},{2,0},{4,6},{6,4},{8,10},{10,8},{12,14},{14,12},{16,18},{18,... | collective-permute-start | bytes 9830408 | tf_op jit(solution)/shard_map/ppermute | solution.py:71
  377.0 31.9 %collective-permute-start.32 = (bf16[4,32,5120]{2,1,0:T(8,128)(2,1)}, bf16[4,32,5120]{2,1,0:T(8,128)(2,1)}, u32[]{:S(2)}, u32[]{:S(2)}) collective-permute-start(bf16[4,32,5120]{2,1,0:T(8,128)(2,1)} %pad_maximum_fusion.4), channel_id=1, source_target_pairs={{0,1},{1,0},{2,3},{3,2},{4,5},{5,4},{6,7},{7,6},{8,9},{9,8},{10,11... | collective-permute-start | bytes 3932168 | tf_op jit(solution)/shard_map/ppermute | solution.py:74
  378.6 31.0 %collective-permute-start.31 = (bf16[4,32,5120]{2,1,0:T(8,128)(2,1)S(1)}, bf16[4,32,5120]{2,1,0:T(8,128)(2,1)}, u32[]{:S(2)}, u32[]{:S(2)}) collective-permute-start(bf16[4,32,5120]{2,1,0:T(8,128)(2,1)S(1)} %pad_maximum_fusion.3), channel_id=1, source_target_pairs={{0,4},{2,6},{4,0},{6,2},{8,12},{10,14},{12,8},{14,10},{16,20},{18,... | collective-permute-start | bytes 3932168 | tf_op jit(solution)/shard_map/ppermute | solution.py:71
  382.2 54.6 %collective-permute-start.37 = (bf16[256,1024]{1,0:T(8,128)(2,1)}, bf16[256,1024]{1,0:T(8,128)(2,1)}, u32[]{:S(2)}, u32[]{:S(2)}) collective-permute-start(bf16[256,1024]{1,0:T(8,128)(2,1)} %broadcast_add_fusion.6), channel_id=1, source_target_pairs={{0,1},{1,0},{2,3},{3,2},{4,5},{5,4},{6,7},{7,6},{8,9},{9,8},{10,11... | collective-permute-start | bytes 1572872 | tf_op jit(solution)/shard_map/ppermute | solution.py:74
  434.9 17.7 %collective-permute-start.35 = (bf16[32,5120]{1,0:T(8,128)(2,1)S(1)}, bf16[32,5120]{1,0:T(8,128)(2,1)S(1)}, u32[]{:S(2)}, u32[]{:S(2)}) collective-permute-start(bf16[32,5120]{1,0:T(8,128)(2,1)S(1)} %get-tuple-element.126), channel_id=1, source_target_pairs={{0,24},{2,26},{4,28},{6,30},{8,16},{10,18},{12,20},{14,22},{16,8},... | collective-permute-start | bytes 983048 | tf_op jit(solution)/shard_map/ppermute | solution.py:71
  436.8 27.0 %collective-permute-start.34 = (bf16[32,5120]{1,0:T(8,128)(2,1)S(1)}, bf16[32,5120]{1,0:T(8,128)(2,1)S(1)}, u32[]{:S(2)}, u32[]{:S(2)}) collective-permute-start(bf16[32,5120]{1,0:T(8,128)(2,1)S(1)} %get-tuple-element.127), channel_id=1, source_target_pairs={{0,16},{2,18},{4,20},{6,22},{8,24},{10,26},{12,28},{14,30},{16,0},... | collective-permute-start | bytes 983048 | tf_op jit(solution)/shard_map/ppermute | solution.py:71
  444.4 21.1 %collective-permute-start.26 = (bf16[4,32,3200]{2,1,0:T(8,128)(2,1)S(1)}, bf16[4,32,3200]{2,1,0:T(8,128)(2,1)S(1)}, u32[]{:S(2)}, u32[]{:S(2)}) collective-permute-start(bf16[4,32,3200]{2,1,0:T(8,128)(2,1)S(1)} %pad_maximum_fusion.7), channel_id=1, source_target_pairs={{0,1},{1,0},{2,3},{3,2},{4,5},{5,4},{6,7},{7,6},{8,9},{9,8},{10,11... | collective-permute-start | bytes 2457608 | tf_op jit(solution)/shard_map/ppermute | solution.py:74
  445.2 20.3 %collective-permute-start.24 = (bf16[4,32,3200]{2,1,0:T(8,128)(2,1)S(1)}, bf16[4,32,3200]{2,1,0:T(8,128)(2,1)S(1)}, u32[]{:S(2)}, u32[]{:S(2)}) collective-permute-start(bf16[4,32,3200]{2,1,0:T(8,128)(2,1)S(1)} %pad_maximum_fusion.6), channel_id=1, source_target_pairs={{0,4},{2,6},{4,0},{6,2},{8,12},{10,14},{12,8},{14,10},{16,20},{18,... | collective-permute-start | bytes 2457608 | tf_op jit(solution)/shard_map/ppermute | solution.py:71
  469.4 16.5 %collective-permute-start.28 = (bf16[32,3200]{1,0:T(8,128)(2,1)S(1)}, bf16[32,3200]{1,0:T(8,128)(2,1)S(1)}, u32[]{:S(2)}, u32[]{:S(2)}) collective-permute-start(bf16[32,3200]{1,0:T(8,128)(2,1)S(1)} %get-tuple-element.130), channel_id=1, source_target_pairs={{0,16},{2,18},{4,20},{6,22},{8,24},{10,26},{12,28},{14,30},{16,0},... | collective-permute-start | bytes 614408 | tf_op jit(solution)/shard_map/ppermute | solution.py:71
  (48 other events, 691.5 us)
Sparse Core Ops, SparseCore 0:
  133.4 74.0 all-gather.1
  254.9 110.1 reduce-scatter.1

commit v3 on v2

--- a/solution.py
+++ b/solution.py
@@ -14,6 +14,7 @@
 EPSILON = 1e-12
 SCALE = 0.125
 BIG = 1e30
+PAIRS = 4
 EXTRA = 128
 HASTE = 1
 LOW = jnp.bfloat16
@@ -281,21 +282,30 @@
 
 def attend_kernel(lengths_ref, at, q_ref, k_ref, v_ref, out_ref, turned_ref, log_ref, at_ref):
     hand_on(at, at_ref)
-    block = pl.program_id(0) // (H // 2)
+    block = pl.program_id(0) // (H // 2 // PAIRS)
     row_count = q_ref.shape[0]
     lane_slot, row_slot = slot_rows(lengths_ref, block, row_count)
     inside = lane_slot < SLOTS
     lane = lax.broadcasted_iota(jnp.int32, (row_count, 128), 1)
     barred = query_rows(lane_slot).astype(LOW)
     padded = jnp.concatenate([barred, jnp.zeros((HD - 8, row_count), LOW)], axis=0)
-    q_turned = (q_ref[...].astype(F32) * SCALE).T.astype(LOW)
-    v_turned = v_ref[...].astype(F32).T
+    for pair in range(PAIRS):
+        attend_pair(
+            pair, inside, lane, row_slot, padded, q_ref, k_ref, v_ref, out_ref, turned_ref, log_ref
+        )
+
+
+def attend_pair(pair, inside, lane, row_slot, padded, q_ref, k_ref, v_ref, out_ref, turned_ref, log_ref):
+    row_count = q_ref.shape[0]
+    columns = slice(pair * 128, (pair + 1) * 128)
+    q_turned = (q_ref[:, columns].astype(F32) * SCALE).T.astype(LOW)
+    v_turned = v_ref[:, columns].astype(F32).T
     v_low = v_turned.astype(LOW)
     ones = jnp.ones((16, row_count), LOW)
     results = []
     for head in range(2):
         own = (lane < HD) if head == 0 else (lane >= HD)
-        keyed = jnp.where(own, k_ref[...], key_columns(row_slot, HD * (1 - head)))
+        keyed = jnp.where(own, k_ref[:, columns], key_columns(row_slot, HD * (1 - head)))
         half = q_turned[head * HD : (head + 1) * HD]
         query = jnp.concatenate([half, padded] if head == 0 else [padded, half], axis=0)
         scores = nn(keyed, query)
@@ -307,19 +317,19 @@
         total = mixed[HD : HD + 1]
         result = mixed[:HD] / total
         results.append(jnp.where(inside, result, v_turned[head * HD : (head + 1) * HD]))
-        log_ref[0, head : head + 1] = jnp.where(inside, highest + jnp.log(total), BIG)
+        log_ref[0, 2 * pair + head : 2 * pair + head + 1] = jnp.where(inside, highest + jnp.log(total), BIG)
     turned = jnp.concatenate(results, axis=0)
-    turned_ref[...] = turned.astype(LOW)
-    out_ref[...] = turned.T.astype(LOW)
+    turned_ref[columns] = turned.astype(LOW)
+    out_ref[:, columns] = turned.T.astype(LOW)
 
 
 def attend(at, lengths, projected, after=()):
     rows = projected.shape[0]
-    blocks, pairs = rows // CAP, H // 2
+    blocks, pairs = rows // CAP, H // 2 // PAIRS
     width = H * HD
 
     def column(part):
-        return pl.BlockSpec((CAP, 128), lambda i, n, at: (i // pairs, part * pairs + i % pairs))
+        return pl.BlockSpec((CAP, 128 * PAIRS), lambda i, n, at: (i // pairs, part * pairs + i % pairs))
 
     return pl.pallas_call(
         later(attend_kernel, 2, after),
@@ -335,7 +345,7 @@
             in_specs=[ANY] * len(after) + [column(0), column(1), column(2)],
             out_specs=(
                 column(0),
-                pl.BlockSpec((128, CAP), lambda i, n, at: (i % pairs, i // pairs)),
+                pl.BlockSpec((128 * PAIRS, CAP), lambda i, n, at: (i % pairs, i // pairs)),
                 pl.BlockSpec((1, 8, CAP), lambda i, n, at: (i, 0, 0)),
                 AT_SPEC,
             ),
@@ -354,19 +364,34 @@
 
 def attend_back_kernel(lengths_ref, at, q_ref, k_ref, v_ref, att_ref, grad_ref, log_ref, dq_ref, dk_ref, dv_ref, sums_ref, at_ref):
     hand_on(at, at_ref)
-    block, pair = pl.program_id(0) // (H // 2), pl.program_id(0) % (H // 2)
+    block, step = pl.program_id(0) // (H // 2 // PAIRS), pl.program_id(0) % (H // 2 // PAIRS)
     row_count = q_ref.shape[0]
     lane_slot, row_slot = slot_rows(lengths_ref, block, row_count)
     outside = lane_slot >= SLOTS
     lane = lax.broadcasted_iota(jnp.int32, (row_count, 128), 1)
     barred = query_rows(lane_slot)
-    q_scaled = (q_ref[...].astype(F32) * SCALE)
+    refs = (q_ref, k_ref, v_ref, att_ref, grad_ref, log_ref, dq_ref, dk_ref, dv_ref, sums_ref)
+
+    @first_step
+    def _():
+        sums_ref[...] = jnp.zeros_like(sums_ref)
+
+    for pair in range(PAIRS):
+        attend_back_pair(pair, step, row_slot, outside, lane, barred, *refs)
+
+
+def attend_back_pair(
+    pair, step, row_slot, outside, lane, barred, q_ref, k_ref, v_ref, att_ref, grad_ref, log_ref, dq_ref, dk_ref, dv_ref, sums_ref
+):
+    row_count = q_ref.shape[0]
+    columns = slice(pair * 128, (pair + 1) * 128)
+    q_scaled = (q_ref[:, columns].astype(F32) * SCALE)
     q_turned = q_scaled.T.astype(LOW)
-    k_scaled = k_ref[...].astype(F32) * SCALE
+    k_scaled = k_ref[:, columns].astype(F32) * SCALE
     k_turned = k_scaled.T.astype(LOW)
-    grad_wide = grad_ref[...].astype(F32).T
+    grad_wide = grad_ref[:, columns].astype(F32).T
     grad_turned = grad_wide
-    mixed = grad_turned * att_ref[...].astype(F32)
+    mixed = grad_turned * att_ref[columns].astype(F32)
     grad_turned = grad_turned.astype(LOW)
     line = lax.broadcasted_iota(jnp.int32, (8, row_count), 0)
     none = jnp.zeros((HD - 16, row_count), F32)
@@ -382,9 +407,9 @@
         own = (lane < HD) if head == 0 else (lane >= HD)
         start = HD * (1 - head)
         unit = (lane >= start + 8) & (lane < start + 11)
-        keyed = jnp.where(own, k_ref[...], jnp.where(unit, jnp.ones((), LOW), key_columns(row_slot, start)))
-        valued = jnp.where(own, v_ref[...], jnp.where(unit, jnp.ones((), LOW), jnp.zeros((), LOW)))
-        extra = jnp.concatenate([barred, lines(log_ref[0, head : head + 1]), none], axis=0).astype(LOW)
+        keyed = jnp.where(own, k_ref[:, columns], jnp.where(unit, jnp.ones((), LOW), key_columns(row_slot, start)))
+        valued = jnp.where(own, v_ref[:, columns], jnp.where(unit, jnp.ones((), LOW), jnp.zeros((), LOW)))
+        extra = jnp.concatenate([barred, lines(log_ref[0, 2 * pair + head : 2 * pair + head + 1]), none], axis=0).astype(LOW)
         half = slice(head * HD, (head + 1) * HD)
         query = jnp.concatenate([q_turned[half], extra] if head == 0 else [extra, q_turned[half]], axis=0)
         weights = jnp.exp(nn(keyed, query))
@@ -396,28 +421,24 @@
         dks.append(nt(q_turned[half], moved))
         dqs.append(nn(k_turned[half], moved))
     dq = jnp.concatenate(dqs, axis=0).T.astype(LOW)
-    dq_ref[...] = dq
-    dk_ref[...] = jnp.concatenate(dks, axis=0).T.astype(LOW)
+    dq_ref[:, columns] = dq
+    dk_ref[:, columns] = jnp.concatenate(dks, axis=0).T.astype(LOW)
     dv = jnp.concatenate(dvs, axis=0)
     dv = jnp.where(outside, dv + grad_wide, dv).T.astype(LOW)
-    dv_ref[...] = dv
-
-    @first_step
-    def _():
-        sums_ref[...] = jnp.zeros_like(sums_ref)
-
-    span = pl.ds(pl.multiple_of(pair * 128, 128), 128)
+    dv_ref[:, columns] = dv
+
+    span = pl.ds(pl.multiple_of((step * PAIRS + pair) * 128, 128), 128)
     sums_ref[0:1, span] += jnp.sum(dq.astype(F32), axis=0, keepdims=True)
     sums_ref[1:2, span] += jnp.sum(dv.astype(F32), axis=0, keepdims=True)
 
 
 def attend_back(at, lengths, projected, turned, grad_attended, logs, after=()):
     rows = projected.shape[0]
-    blocks, pairs = rows // CAP, H // 2
+    blocks, pairs = rows // CAP, H // 2 // PAIRS
     width = H * HD
 
     def column(part):
-        return pl.BlockSpec((CAP, 128), lambda i, n, at: (i // pairs, part * pairs + i % pairs))
+        return pl.BlockSpec((CAP, 128 * PAIRS), lambda i, n, at: (i // pairs, part * pairs + i % pairs))
 
     return pl.pallas_call(
         later(attend_back_kernel, 2, after),
@@ -428,7 +449,7 @@
             in_specs=[ANY] * len(after)
             + [
                 column(0), column(1), column(2),
-                pl.BlockSpec((128, CAP), lambda i, n, at: (i % pairs, i // pairs)),
+                pl.BlockSpec((128 * PAIRS, CAP), lambda i, n, at: (i % pairs, i // pairs)),
                 column(0),
                 pl.BlockSpec((1, 8, CAP), lambda i, n, at: (i, 0, 0)),
             ],
@@ -922,7 +943,7 @@
         at_wide = pinned(at, *wide_parts)
         in_cores = plan.gather_core(at, *in_main) + plan.gather_core(at_wide, *in_corners)
         in_pieces = list(in_main + in_corners) + in_cores
-        at_core = pinned(at_wide, *in_corners)
+        at_core = at_wide
         wide_far, wide_across, wide_other = plan.gather_xy(at_core, wide_shard, wide_parts)
         contract_pieces = [lax.all_gather(contract + pinned(at_core, wide_across, wide_other)[4].astype(LOW), "fsdp", axis=0, tiled=True)]
         wide_corners = plan.gather_corner(at_core, wide_shard, wide_across, wide_other)

time: 507 us -> 492 us (0.970)
  Pallas kernels: 228 us -> 218 us
  waiting for transfers between devices: 129 us -> 121 us
  local copies, waits for them, and re-layouts: 32.1 us -> 37.3 us
    ppermute x11, waiting for transfers between devices: 42.9 us -> 20.7 us  [other_copy(): return lax.ppermute(value, 'rep', [(0, 1), (1, 0)])]
    ppermute x27, waiting for transfers between devices: 83.4 us -> 93.4 us  [flip(): lax.ppermute(value, 'fsdp', [(i, i ^ bits) for i in range(self.shards)])]
    pallas_call x1, Pallas kernels: 32.9 us -> 27.3 us  [attend_back(): pl.pallas_call(later(attend_back_kernel, 2, after), out_shape=(jax.ShapeD...]
    unnamed x69 -> x61, local copies, waits for them, and re-layouts: 8.27 us -> 11.3 us
  transfers between devices with their start and end apart: 40 -> 40, of which waited for: 21 -> 18; matrix products, arithmetic and copies ran while one was open for 13% -> 14% of each run, Pallas kernels for 36% -> 35%
where the time goes in v3:
time: 492 us; the launch traced here: 487 us
  Pallas kernels  218 us (44%)
  waiting for transfers between devices  121 us (25%)
  starting transfers between devices  42.1 us (9%)
  other arithmetic  40.9 us (8%)
  local copies, waits for them, and re-layouts  37.3 us (8%)
  between operations  28.1 us (6%)
    ppermute x27, waiting for transfers between devices, flip(): lax.ppermute(value, 'fsdp', [(i, i ^ bits) for i in range(self.shards)])  93.4 us
    pallas_call x4, Pallas kernels, outer_wide(): pl.pallas_call(later(functools.partial(outer_wide_kernel, flip, tuple(own...  47 us
    pallas_call x1, Pallas kernels, down(): pl.pallas_call(later(functools.partial(down_kernel, plan, (len(wide_piece...  34.4 us
    ppermute x27, starting transfers between devices, flip(): lax.ppermute(value, 'fsdp', [(i, i ^ bits) for i in range(self.shards)])  31.8 us
    pallas_call x1, Pallas kernels, attend_back(): pl.pallas_call(later(attend_back_kernel, 2, after), out_shape=(jax.ShapeD...  27.3 us
    pallas_call x1, Pallas kernels, up(): pl.pallas_call(later(functools.partial(up_kernel, plan, chunk), 1, after)...  25.8 us
    ppermute x11, waiting for transfers between devices, other_copy(): return lax.ppermute(value, 'rep', [(0, 1), (1, 0)])  20.7 us
    pallas_call x1, Pallas kernels, over(): pl.pallas_call(later(functools.partial(over_kernel, plan, chunk), 1, afte...  20.7 us
  transfers between devices with their start and end apart: 40, of which 18 were waited for; matrix products, arithmetic and copies ran while one was open for 14% of the time, Pallas kernels for 35%

profile of v3, /device:TPU:0, one launch (start us, length us, event | category | flops | bytes accessed | tf_op | source)
XLA Modules:
  0.0 487.1 jit_solution(11098630431176772040)
XLA Ops:
  10.7 4.0 collective-permute-start.8
  20.9 9.1 %collective-permute-done = bf16[32,3200]{1,0:T(8,128)(2,1)S(1)} collective-permute-done((bf16[32,3200]{1,0:T(8,128)(2,1)}, bf16[32,3200]{1,0:T(8,128)(2,1)S(1)}, u32[]{:S(2)}, u32[]{:S(2)}) %collective-permute-start) | collective-permute-done | bytes 204832 | tf_op jit(solution)/shard_map/ppermute | solution.py:72
  48.2 16.4 %collective-permute-done.2 = bf16[32,5248]{1,0:T(8,128)(2,1)S(1)} collective-permute-done((bf16[32,5248]{1,0:T(8,128)(2,1)S(1)}, bf16[32,5248]{1,0:T(8,128)(2,1)S(1)}, u32[]{:S(2)}, u32[]{:S(2)}) %collective-permute-start.2) | collective-permute-done | bytes 335904 | tf_op jit(solution)/shard_map/ppermute | solution.py:72
  86.1 26.5 %collective-permute-done.11.refs_9_.refs_11_ = bf16[32,3200]{1,0:T(8,128)(2,1)S(1)} collective-permute-done((bf16[32,3200]{1,0:T(8,128)(2,1)S(1)}, bf16[32,3200]{1,0:T(8,128)(2,1)S(1)}, u32[]{:S(2)}, u32[]{:S(2)}) %collective-permute-start.11) | collective-permute-done | bytes 204832 | tf_op jit(solution)/shard_map/ppermute | solution.py:72
  125.0 14.3 %shard_map.271 = (bf16[1024,3072]{1,0:T(8,128)(2,1)}, bf16[1024,1024]{1,0:T(8,128)(2,1)}, s32[5]{0:T(128)}) custom-call(s32[5]{0:T(128)} %copy-done.24, bf16[128,5248]{1,0:T(8,128)(2,1)} %copy-done.2, bf16[96,5248]{1,0:T(8,128)(2,1)} %collective-permute-done.5.refs_2_.refs_6_.refs_9_, bf16[1024,1024]{1,0:T(8,128)(2,1)} %refs_1_.1, ...), custom_call_target="tpu_custom_call" | custom-call | flops 12884901888 | bytes 40265320 | tf_op jit(solution)/shard_map/pallas_call | solution.py:234
  142.0 20.0 %shard_map.272 = (bf16[1024,1024]{1,0:T(8,128)(2,1)}, bf16[1024,1024]{1,0:T(8,128)(2,1)}, f32[4,8,512]{2,1,0:T(8,128)}, s32[5]{0:T(128)}) custom-call(s32[2,4]{1,0:T(2,128)} %refs_0_.3, s32[5]{0:T(128)} %get-tuple-element.57.refs_1_, bf16[64,5248]{1,0:T(8,128)(2,1)} %copy-done.9, bf16[64,5248]{1,0:T(8,128)(2,1)} %collective-permute-done.16.refs_3_.refs_8_.refs_11_, ...), custom_call_target="tpu_custom_call" | custom-call | flops 25769803776 | bytes 80530640 | tf_op jit(solution)/shard_map/pallas_call | solution.py:334
  171.6 5.9 %collective-permute-done.18.refs_10_.refs_13_ = bf16[128,5248]{1,0:T(8,128)(2,1)S(1)} collective-permute-done((bf16[128,5248]{1,0:T(8,128)(2,1)S(1)}, bf16[128,5248]{1,0:T(8,128)(2,1)S(1)}, u32[]{:S(2)}, u32[]{:S(2)}) %collective-permute-start.18) | collective-permute-done | bytes 1343520 | tf_op jit(solution)/shard_map/ppermute | solution.py:72
  179.8 25.8 %shard_map.273 = (bf16[1024,4096]{1,0:T(8,128)(2,1)}, bf16[1024,4096]{1,0:T(8,128)(2,1)}, bf16[1024,1024]{1,0:T(8,128)(2,1)}, f32[1024,128]{1,0:T(8,128)}, f32[1...) custom-call(s32[5]{0:T(128)} %get-tuple-element.59.refs_0_, ...), custom_call_target="tpu_custom_call" | custom-call | flops 21474836480 | bytes 67108864 | tf_op jit(solution)/shard_map/pallas_call | solution.py:538
  205.6 20.7 %shard_map.274 = (bf16[1024,1024]{1,0:T(8,128)(2,1)}, bf16[1024,1024]{1,0:T(8,128)(2,1)}, f32[8,1024]{1,0:T(8,128)}, s32[5]{0:T(128)}) custom-call(s32[5]{0:T(128)} %get-tuple-element.61.refs_0_, f32[1024,1024]{1,0:T(8,128)} %get-tuple-element.62.refs_1_, bf16[1024,4096]{1,0:T(8,128)(2,1)} %get-tuple-element.63.refs_2_.refs_1_, bf16[1024,1024]{1,0:T(8,128)(2,1)} %refs_3_.3, ...), custom_call_target="tpu_custom_call" | custom-call | flops 17179869184 | bytes 53687092 | tf_op jit(solution)/shard_map/pallas_call | solution.py:602
  226.3 15.2 %shard_map.275 = (bf16[4096,1024]{1,0:T(8,128)(2,1)}, s32[5]{0:T(128)}) custom-call(s32[5]{0:T(128)} %get-tuple-element.66.refs_0_, bf16[1024,4096]{1,0:T(8,128)(2,1)} %get-tuple-element.63.refs_2_.refs_1_, bf16[1024,1024]{1,0:T(8,128)(2,1)} %get-tuple-element.67.refs_2_.refs_1_), custom_call_target="tpu_custom_call" | custom-call | flops 17179869184 | bytes 53687092 | tf_op jit(solution)/shard_map/pallas_call | solution.py:718
  241.5 34.4 %shard_map.276 = (bf16[1024,4096]{1,0:T(8,128)(2,1)}, bf16[1024,1024]{1,0:T(8,128)(2,1)}, bf16[1024,1024]{1,0:T(8,128)(2,1)}, f32[8,1024]{1,0:T(8,128)}, f32[8,4096]{1,0:T(8,128)}, /*index=5*/s32[5]{0:T(128)}) custom-call(s32[5]{0:T(128)} %get-tuple-element.68.refs_0_, bf16[1024,1024]{1,0:T(8,128)(2,1)} %get-tuple-element.67.refs_2_.refs_1_, ...), custom_call_target="tpu_custom_call" | custom-call | flops 38654705664 | bytes 120795952 | tf_op jit(solution)/shard_map/pallas_call | solution.py:677
  275.9 12.9 %shard_map.277 = (bf16[16,32,5120]{2,1,0:T(8,128)(2,1)}, s32[5]{0:T(128)}) custom-call(s32[5]{0:T(128)} %get-tuple-element.72.refs_0_, bf16[1024,1024]{1,0:T(8,128)(2,1)} %get-tuple-element.73.refs_1_, bf16[1024,1024]{1,0:T(8,128)(2,1)} %get-tuple-element.74.refs_2_.refs_5_, bf16[1024,4096]{1,0:T(8,128)(2,1)} %get-tuple-element.75.refs_3_, ...), custom_call_target="tpu_custom_call" | custom-call | flops 10737418240 | bytes 33554432 | tf_op jit(solution)/shard_map/pallas_call | solution.py:846
  289.2 13.1 %shard_map.278 = (bf16[16,32,5120]{2,1,0:T(8,128)(2,1)}, s32[5]{0:T(128)}) custom-call(s32[5]{0:T(128)} %get-tuple-element.77.refs_0_, bf16[1024,1024]{1,0:T(8,128)(2,1)} %get-tuple-element.73.refs_1_, bf16[1024,1024]{1,0:T(8,128)(2,1)} %get-tuple-element.74.refs_2_.refs_5_, bf16[1024,4096]{1,0:T(8,128)(2,1)} %get-tuple-element.75.refs_3_, ...), custom_call_target="tpu_custom_call" | custom-call | flops 10737418240 | bytes 33554432 | tf_op jit(solution)/shard_map/pallas_call | solution.py:846
  307.7 27.3 %shard_map.279 = (bf16[1024,1024]{1,0:T(8,128)(2,1)}, bf16[1024,1024]{1,0:T(8,128)(2,1)}, bf16[1024,1024]{1,0:T(8,128)(2,1)}, f32[8,1024]{1,0:T(8,128)}, s32[5]{0:T(128)}) custom-call(s32[2,4]{1,0:T(2,128)} %refs_0_.3, s32[5]{0:T(128)} %get-tuple-element.78.refs_1_, bf16[1024,3072]{1,0:T(8,128)(2,1)} %get-tuple-element.58.refs_4_.refs_5_.refs_6_.refs_2_.refs_3_, ...), custom_call_target="tpu_custom_call" | custom-call | flops 26843545600 | bytes 83886080 | tf_op jit(solution)/shard_map/pallas_call | solution.py:443
  340.4 3.9 add_convert_fusion.3
  344.3 6.5 %reduce-scatter.2.cloned.1.call-done.refs_3_ = bf16[256,1024]{1,0:T(8,128)(2,1)} async-done(((bf16[4096,1024]{1,0:T(8,128)(2,1)}), bf16[256,1024]{1,0:T(8,128)(2,1)}) %reduce-scatter.2.cloned.1.call-update) | async-done | bytes 524304 | tf_op jit(solution)/shard_map/reduce_scatter | solution.py:866
  350.8 10.4 %shard_map.280 = (bf16[16,32,3200]{2,1,0:T(8,128)(2,1)}, s32[5]{0:T(128)}) custom-call(s32[5]{0:T(128)} %get-tuple-element.81.refs_0_, bf16[2,32,5120]{2,1,0:T(8,128)(2,1)} %copy-done.12, bf16[2,32,5120]{2,1,0:T(8,128)(2,1)} %copy-done.11, bf16[256,1024]{1,0:T(8,128)(2,1)} %reduce-scatter.2.cloned.1.call-done.refs_3_, ...), custom_call_target="tpu_custom_call" | custom-call | flops 6442450944 | bytes 20132660 | tf_op jit(solution)/shard_map/pallas_call | solution.py:846
  368.2 10.6 %shard_map.281 = (bf16[16,32,3200]{2,1,0:T(8,128)(2,1)}, s32[5]{0:T(128)}) custom-call(s32[5]{0:T(128)} %get-tuple-element.93.refs_0_, bf16[1024,1024]{1,0:T(8,128)(2,1)} %get-tuple-element.85.refs_4_.refs_1_, bf16[1024,1024]{1,0:T(8,128)(2,1)} %get-tuple-element.86.refs_5_.refs_2_.refs_3_, bf16[1024,1024]{1,0:T(8,128)(2,1)} %get-tuple-element.87.refs_6_.refs_3_.refs_4_, ...), custom_call_target="tpu_custom_call" | custom-call | flops 6442450944 | bytes 20132660 | tf_op jit(solution)/shard_map/pallas_call | solution.py:846
  380.7 13.6 %collective-permute-done.32 = bf16[4,32,5120]{2,1,0:T(8,128)(2,1)} collective-permute-done((bf16[4,32,5120]{2,1,0:T(8,128)(2,1)}, bf16[4,32,5120]{2,1,0:T(8,128)(2,1)}, u32[]{:S(2)}, u32[]{:S(2)}) %collective-permute-start.32) | collective-permute-done | bytes 1310752 | tf_op jit(solution)/shard_map/ppermute | solution.py:75
  398.5 13.4 %shard_map.282 = (bf16[1024,1024]{1,0:T(8,128)(2,1)}, s32[5]{0:T(128)}) custom-call(s32[5]{0:T(128)} %get-tuple-element.94.refs_0_, bf16[16,32,3200]{2,1,0:T(8,128)(2,1)} %collective-permute-done.22.refs_1_, bf16[1024,1024]{1,0:T(8,128)(2,1)} %get-tuple-element.76.refs_4_.refs_2_, bf16[1024,1024]{1,0:T(8,128)(2,1)} %get-tuple-element.86.refs_5_.refs_2_.refs_3_, ...), custom_call_target="tpu_custom_call" | custom-call | flops 12884901888 | bytes 40265320 | tf_op jit(solution)/shard_map/pallas_call | solution.py:899
  431.2 6.8 %collective-permute-done.35 = bf16[32,5120]{1,0:T(8,128)(2,1)S(1)} collective-permute-done((bf16[32,5120]{1,0:T(8,128)(2,1)S(1)}, bf16[32,5120]{1,0:T(8,128)(2,1)S(1)}, u32[]{:S(2)}, u32[]{:S(2)}) %collective-permute-start.35) | collective-permute-done | bytes 327712 | tf_op jit(solution)/shard_map/ppermute | solution.py:72
  438.0 11.2 %collective-permute-done.34 = bf16[32,5120]{1,0:T(8,128)(2,1)S(1)} collective-permute-done((bf16[32,5120]{1,0:T(8,128)(2,1)S(1)}, bf16[32,5120]{1,0:T(8,128)(2,1)S(1)}, u32[]{:S(2)}, u32[]{:S(2)}) %collective-permute-start.34) | collective-permute-done | bytes 327712 | tf_op jit(solution)/shard_map/ppermute | solution.py:72
  459.9 4.0 collective-permute-done.29
  463.9 7.5 %collective-permute-done.28 = bf16[32,3200]{1,0:T(8,128)(2,1)S(1)} collective-permute-done((bf16[32,3200]{1,0:T(8,128)(2,1)S(1)}, bf16[32,3200]{1,0:T(8,128)(2,1)S(1)}, u32[]{:S(2)}, u32[]{:S(2)}) %collective-permute-start.28) | collective-permute-done | bytes 204832 | tf_op jit(solution)/shard_map/ppermute | solution.py:72
  (220 shorter events, 125.6 us)
Async XLA Ops:
  7.2 198.4 %all-gather.2.cloned.1.call-start = ((), (), s32[]{:S(2)}) async-start(), calls=%async_computation.1 | async-start | bytes 8912896 | tf_op jit(solution)/shard_map/all_gather | solution.py:948
  10.7 30.9 %collective-permute-start.8 = (bf16[32,3200]{1,0:T(8,128)(2,1)}, bf16[32,3200]{1,0:T(8,128)(2,1)}, u32[]{:S(2)}, u32[]{:S(2)}) collective-permute-start(bf16[32,3200]{1,0:T(8,128)(2,1)} %constant_dynamic-slice_fusion.5), channel_id=1, source_target_pairs={{0,16},{2,18},{4,20},{6,22},{8,24},{10,26},{12,28},{14,30},{16,0},... | collective-permute-start | bytes 614408 | tf_op jit(solution)/shard_map/ppermute | solution.py:72
  14.7 25.1 %collective-permute-start.7 = (bf16[32,3200]{1,0:T(8,128)(2,1)}, bf16[32,3200]{1,0:T(8,128)(2,1)}, u32[]{:S(2)}, u32[]{:S(2)}) collective-permute-start(bf16[32,3200]{1,0:T(8,128)(2,1)} %constant_dynamic-slice_fusion.5), channel_id=1, source_target_pairs={{0,8},{2,10},{4,12},{6,14},{8,0},{10,2},{12,4},{14,6},{16,24},{18,... | collective-permute-start | bytes 614408 | tf_op jit(solution)/shard_map/ppermute | solution.py:72
  16.3 22.2 %collective-permute-start.6 = (bf16[64,3200]{1,0:T(8,128)(2,1)S(1)}, bf16[64,3200]{1,0:T(8,128)(2,1)S(1)}, u32[]{:S(2)}, u32[]{:S(2)}) collective-permute-start(bf16[64,3200]{1,0:T(8,128)(2,1)S(1)} %get-tuple-element.136.refs_4_.refs_6_), channel_id=1, source_target_pairs={{0,4},{2,6},{4,0},{6,2},{8,12},{10,14},{12,8},{14,10},{16,20},{18,... | collective-permute-start | bytes 1228808 | tf_op jit(solution)/shard_map/ppermute | solution.py:72
  35.0 29.7 %collective-permute-start.2 = (bf16[32,5248]{1,0:T(8,128)(2,1)S(1)}, bf16[32,5248]{1,0:T(8,128)(2,1)S(1)}, u32[]{:S(2)}, u32[]{:S(2)}) collective-permute-start(bf16[32,5248]{1,0:T(8,128)(2,1)S(1)} %constant_dynamic-slice_fusion.4), channel_id=1, source_target_pairs={{0,16},{2,18},{4,20},{6,22},{8,24},{10,26},{12,28},{14,30},{16,0},... | collective-permute-start | bytes 1007624 | tf_op jit(solution)/shard_map/ppermute | solution.py:72
  38.5 27.4 %collective-permute-start.1 = (bf16[32,5248]{1,0:T(8,128)(2,1)S(1)}, bf16[32,5248]{1,0:T(8,128)(2,1)S(1)}, u32[]{:S(2)}, u32[]{:S(2)}) collective-permute-start(bf16[32,5248]{1,0:T(8,128)(2,1)S(1)} %constant_dynamic-slice_fusion.4), channel_id=1, source_target_pairs={{0,8},{2,10},{4,12},{6,14},{8,0},{10,2},{12,4},{14,6},{16,24},{18,... | collective-permute-start | bytes 1007624 | tf_op jit(solution)/shard_map/ppermute | solution.py:72
  44.0 34.9 %collective-permute-start.10 = (bf16[96,3200]{1,0:T(8,128)(2,1)}, bf16[96,3200]{1,0:T(8,128)(2,1)}, u32[]{:S(2)}, u32[]{:S(2)}) collective-permute-start(bf16[96,3200]{1,0:T(8,128)(2,1)} %get-tuple-element.138.refs_6_.refs_8_), channel_id=1, source_target_pairs={{0,1},{1,0},{2,3},{3,2},{4,5},{5,4},{6,7},{7,6},{8,9},{9,8},{10,11... | collective-permute-start | bytes 1843208 | tf_op jit(solution)/shard_map/ppermute | solution.py:75
  45.6 34.9 %collective-permute-start.9 = (bf16[96,3200]{1,0:T(8,128)(2,1)}, bf16[96,3200]{1,0:T(8,128)(2,1)}, u32[]{:S(2)}, u32[]{:S(2)}) collective-permute-start(bf16[96,3200]{1,0:T(8,128)(2,1)} %get-tuple-element.138.refs_6_.refs_8_), channel_id=1, source_target_pairs={{0,4},{2,6},{4,0},{6,2},{8,12},{10,14},{12,8},{14,10},{16,20},{18,... | collective-permute-start | bytes 1843208 | tf_op jit(solution)/shard_map/ppermute | solution.py:72
  73.3 40.9 %collective-permute-start.5 = (bf16[96,5248]{1,0:T(8,128)(2,1)}, bf16[96,5248]{1,0:T(8,128)(2,1)}, u32[]{:S(2)}, u32[]{:S(2)}) collective-permute-start(bf16[96,5248]{1,0:T(8,128)(2,1)} %pad_maximum_fusion.5.refs_4_.refs_7_), channel_id=1, source_target_pairs={{0,1},{1,0},{2,3},{3,2},{4,5},{5,4},{6,7},{7,6},{8,9},{9,8},{10,11... | collective-permute-start | bytes 3022856 | tf_op jit(solution)/shard_map/ppermute | solution.py:75
  76.8 42.8 %collective-permute-start.4 = (bf16[128,5248]{1,0:T(8,128)(2,1)}, bf16[128,5248]{1,0:T(8,128)(2,1)S(1)}, u32[]{:S(2)}, u32[]{:S(2)}) collective-permute-start(bf16[128,5248]{1,0:T(8,128)(2,1)} %pad_maximum_fusion.1), channel_id=1, source_target_pairs={{0,4},{2,6},{4,0},{6,2},{8,12},{10,14},{12,8},{14,10},{16,20},{18,... | collective-permute-start | bytes 4030472 | tf_op jit(solution)/shard_map/ppermute | solution.py:72
  79.9 32.6 %collective-permute-start.11 = (bf16[32,3200]{1,0:T(8,128)(2,1)S(1)}, bf16[32,3200]{1,0:T(8,128)(2,1)S(1)}, u32[]{:S(2)}, u32[]{:S(2)}) collective-permute-start(bf16[32,3200]{1,0:T(8,128)(2,1)S(1)} %dynamic_slice.32), channel_id=1, source_target_pairs={{0,4},{2,6},{4,0},{6,2},{8,12},{10,14},{12,8},{14,10},{16,20},{18,... | collective-permute-start | bytes 614408 | tf_op jit(solution)/shard_map/ppermute | solution.py:72
  81.5 31.7 %collective-permute-start.12 = (bf16[64,3200]{1,0:T(8,128)(2,1)S(1)}, bf16[64,3200]{1,0:T(8,128)(2,1)S(1)}, u32[]{:S(2)}, u32[]{:S(2)}) collective-permute-start(bf16[64,3200]{1,0:T(8,128)(2,1)S(1)} %dynamic_slice.33), channel_id=1, source_target_pairs={{0,1},{1,0},{2,3},{3,2},{4,5},{5,4},{6,7},{7,6},{8,9},{9,8},{10,11... | collective-permute-start | bytes 1228808 | tf_op jit(solution)/shard_map/ppermute | solution.py:75
  86.1 38.9 %collective-permute-start.13 = (bf16[416,3200]{1,0:T(8,128)(2,1)}, bf16[416,3200]{1,0:T(8,128)(2,1)}, u32[]{:S(2)}, u32[]{:S(2)}) collective-permute-start(bf16[416,3200]{1,0:T(8,128)(2,1)} %constant_dynamic-update-slice_fusion.3), channel_id=1, source_target_pairs={{0,2},{2,0},{4,6},{6,4},{8,10},{10,8},{12,14},{14,12},{16,18},{18,... | collective-permute-start | bytes 7987208 | tf_op jit(solution)/shard_map/ppermute | solution.py:72
  118.0 22.0 %collective-permute-start.15 = (bf16[64,5248]{1,0:T(8,128)(2,1)}, bf16[64,5248]{1,0:T(8,128)(2,1)S(1)}, u32[]{:S(2)}, u32[]{:S(2)}) collective-permute-start(bf16[64,5248]{1,0:T(8,128)(2,1)} %pad_maximum_fusion.8), channel_id=1, source_target_pairs={{0,4},{2,6},{4,0},{6,2},{8,12},{10,14},{12,8},{14,10},{16,20},{18,... | collective-permute-start | bytes 2015240 | tf_op jit(solution)/shard_map/ppermute | solution.py:72
  122.9 228.0 %reduce-scatter.2.cloned.1.call-start = ((), (), s32[]{:S(2)}) async-start(), calls=%async_computation.2 | async-start | bytes 8912896 | tf_op jit(solution)/shard_map/reduce_scatter | solution.py:866
  306.4 33.1 %collective-permute-start.21 = (bf16[2,32,5120]{2,1,0:T(8,128)(2,1)S(1)}, bf16[2,32,5120]{2,1,0:T(8,128)(2,1)S(1)}, u32[]{:S(2)}, u32[]{:S(2)}) collective-permute-start(bf16[2,32,5120]{2,1,0:T(8,128)(2,1)S(1)} %get-tuple-element.115), channel_id=1, source_target_pairs={{0,1},{1,0},{2,3},{3,2},{4,5},{5,4},{6,7},{7,6},{8,9},{9,8},{10,11... | collective-permute-start | bytes 1966088 | tf_op jit(solution)/shard_map/ppermute | solution.py:75
  306.4 33.1 %collective-permute-start.20 = (bf16[2,32,5120]{2,1,0:T(8,128)(2,1)S(1)}, bf16[2,32,5120]{2,1,0:T(8,128)(2,1)S(1)}, u32[]{:S(2)}, u32[]{:S(2)}) collective-permute-start(bf16[2,32,5120]{2,1,0:T(8,128)(2,1)S(1)} %get-tuple-element.116), channel_id=1, source_target_pairs={{0,4},{2,6},{4,0},{6,2},{8,12},{10,14},{12,8},{14,10},{16,20},{18,... | collective-permute-start | bytes 1966088 | tf_op jit(solution)/shard_map/ppermute | solution.py:72
  361.2 37.3 %collective-permute-start.22 = (bf16[16,32,3200]{2,1,0:T(8,128)(2,1)}, bf16[16,32,3200]{2,1,0:T(8,128)(2,1)}, u32[]{:S(2)}, u32[]{:S(2)}) collective-permute-start(bf16[16,32,3200]{2,1,0:T(8,128)(2,1)} %get-tuple-element.95), channel_id=1, source_target_pairs={{0,2},{2,0},{4,6},{6,4},{8,10},{10,8},{12,14},{14,12},{16,18},{18,... | collective-permute-start | bytes 9830408 | tf_op jit(solution)/shard_map/ppermute | solution.py:72
  362.5 31.9 %collective-permute-start.32 = (bf16[4,32,5120]{2,1,0:T(8,128)(2,1)}, bf16[4,32,5120]{2,1,0:T(8,128)(2,1)}, u32[]{:S(2)}, u32[]{:S(2)}) collective-permute-start(bf16[4,32,5120]{2,1,0:T(8,128)(2,1)} %pad_maximum_fusion.4), channel_id=1, source_target_pairs={{0,1},{1,0},{2,3},{3,2},{4,5},{5,4},{6,7},{7,6},{8,9},{9,8},{10,11... | collective-permute-start | bytes 3932168 | tf_op jit(solution)/shard_map/ppermute | solution.py:75
  364.0 31.0 %collective-permute-start.31 = (bf16[4,32,5120]{2,1,0:T(8,128)(2,1)S(1)}, bf16[4,32,5120]{2,1,0:T(8,128)(2,1)}, u32[]{:S(2)}, u32[]{:S(2)}) collective-permute-start(bf16[4,32,5120]{2,1,0:T(8,128)(2,1)S(1)} %pad_maximum_fusion.3), channel_id=1, source_target_pairs={{0,4},{2,6},{4,0},{6,2},{8,12},{10,14},{12,8},{14,10},{16,20},{18,... | collective-permute-start | bytes 3932168 | tf_op jit(solution)/shard_map/ppermute | solution.py:72
  367.6 54.6 %collective-permute-start.37 = (bf16[256,1024]{1,0:T(8,128)(2,1)}, bf16[256,1024]{1,0:T(8,128)(2,1)}, u32[]{:S(2)}, u32[]{:S(2)}) collective-permute-start(bf16[256,1024]{1,0:T(8,128)(2,1)} %broadcast_add_fusion.6), channel_id=1, source_target_pairs={{0,1},{1,0},{2,3},{3,2},{4,5},{5,4},{6,7},{7,6},{8,9},{9,8},{10,11... | collective-permute-start | bytes 1572872 | tf_op jit(solution)/shard_map/ppermute | solution.py:75
  422.3 27.0 %collective-permute-start.34 = (bf16[32,5120]{1,0:T(8,128)(2,1)S(1)}, bf16[32,5120]{1,0:T(8,128)(2,1)S(1)}, u32[]{:S(2)}, u32[]{:S(2)}) collective-permute-start(bf16[32,5120]{1,0:T(8,128)(2,1)S(1)} %get-tuple-element.125), channel_id=1, source_target_pairs={{0,16},{2,18},{4,20},{6,22},{8,24},{10,26},{12,28},{14,30},{16,0},... | collective-permute-start | bytes 983048 | tf_op jit(solution)/shard_map/ppermute | solution.py:72
  429.8 21.1 %collective-permute-start.26 = (bf16[4,32,3200]{2,1,0:T(8,128)(2,1)S(1)}, bf16[4,32,3200]{2,1,0:T(8,128)(2,1)S(1)}, u32[]{:S(2)}, u32[]{:S(2)}) collective-permute-start(bf16[4,32,3200]{2,1,0:T(8,128)(2,1)S(1)} %pad_maximum_fusion.7), channel_id=1, source_target_pairs={{0,1},{1,0},{2,3},{3,2},{4,5},{5,4},{6,7},{7,6},{8,9},{9,8},{10,11... | collective-permute-start | bytes 2457608 | tf_op jit(solution)/shard_map/ppermute | solution.py:75
  430.6 20.3 %collective-permute-start.24 = (bf16[4,32,3200]{2,1,0:T(8,128)(2,1)S(1)}, bf16[4,32,3200]{2,1,0:T(8,128)(2,1)S(1)}, u32[]{:S(2)}, u32[]{:S(2)}) collective-permute-start(bf16[4,32,3200]{2,1,0:T(8,128)(2,1)S(1)} %pad_maximum_fusion.6), channel_id=1, source_target_pairs={{0,4},{2,6},{4,0},{6,2},{8,12},{10,14},{12,8},{14,10},{16,20},{18,... | collective-permute-start | bytes 2457608 | tf_op jit(solution)/shard_map/ppermute | solution.py:72
  (44 other events, 648.5 us)
Sparse Core Ops, SparseCore 0:
  123.0 73.3 all-gather.1
  241.6 109.1 reduce-scatter.1

commit v4 on v3

--- a/solution.py
+++ b/solution.py
@@ -980,10 +980,10 @@
         e_across, e_other = plan.scatter_xy(at, e_mine, e_got, *e_corners)
         extra = jnp.concatenate([back_sums[:2], lines], axis=0)
         turned, rights, owners = (tokens_turned,), (dq, dk, dv), (0, 0, 0)
-        theirs, at = outer_wide(at, turned, rights, owners, 1, extra=extra, after=[*e_corners, contract_owned])
+        theirs, at = outer_wide(at, turned, rights, owners, 1, extra=extra, after=e_corners)
+        i_got = plan.flip(theirs, 1)
+        i_mine, at = outer_wide(at, turned, rights, owners, 0, extra=extra, after=[contract_owned])
         contract_sum = copies_sum(plan, at, contract_owned)
-        i_got = plan.flip(theirs, 1)
-        i_mine, at = outer_wide(at, turned, rights, owners, 0, extra=extra)
         e_parts = plan.scatter_z(at, e_mine, e_got, e_across, e_other)
         i_corners = plan.scatter_corner(at, i_mine, i_got)
         grad_tokens, at = back(plan, at, branch, dq, dk, dv, in_pieces, after=[i_got])

time: 492 us -> 513 us (1.043)
  waiting for transfers between devices: 121 us -> 144 us
    reduce_scatter x1, waiting for transfers between devices: 6.53 us -> 41.6 us  [owned_sum(): return lax.psum_scatter(whole, 'fsdp', scatter_dimension=0, tiled=True)]
    ppermute x11, waiting for transfers between devices: 20.7 us -> 9.37 us  [other_copy(): return lax.ppermute(value, 'rep', [(0, 1), (1, 0)])]
    unnamed x61 -> x63, local copies, waits for them, and re-layouts: 11.3 us -> 13 us
  transfers between devices with their start and end apart: 40 -> 40, of which waited for: 18 -> 15; matrix products, arithmetic and copies ran while one was open for 14% -> 12% of each run, Pallas kernels for 35% -> 27%
where the time goes in v4:
time: 513 us; the launch traced here: 508 us
  Pallas kernels  217 us (42%)
  waiting for transfers between devices  144 us (28%)
  starting transfers between devices  43.4 us (8%)
  other arithmetic  37.2 us (7%)
  local copies, waits for them, and re-layouts  37 us (7%)
  between operations  28.8 us (6%)
    ppermute x27, waiting for transfers between devices, flip(): lax.ppermute(value, 'fsdp', [(i, i ^ bits) for i in range(self.shards)])  93.3 us
    pallas_call x4, Pallas kernels, outer_wide(): pl.pallas_call(later(functools.partial(outer_wide_kernel, flip, tuple(own...  47.3 us
    reduce_scatter x1, waiting for transfers between devices, owned_sum(): return lax.psum_scatter(whole, 'fsdp', scatter_dimension=0, tiled=True)  41.6 us
    pallas_call x1, Pallas kernels, down(): pl.pallas_call(later(functools.partial(down_kernel, plan, (len(wide_piece...  32.8 us
    ppermute x27, starting transfers between devices, flip(): lax.ppermute(value, 'fsdp', [(i, i ^ bits) for i in range(self.shards)])  31.5 us
    pallas_call x1, Pallas kernels, attend_back(): pl.pallas_call(later(attend_back_kernel, 2, after), out_shape=(jax.ShapeD...  27.5 us
    pallas_call x1, Pallas kernels, up(): pl.pallas_call(later(functools.partial(up_kernel, plan, chunk), 1, after)...  25.8 us
    pallas_call x1, Pallas kernels, over(): pl.pallas_call(later(functools.partial(over_kernel, plan, chunk), 1, afte...  20.8 us
  transfers between devices with their start and end apart: 40, of which 15 were waited for; matrix products, arithmetic and copies ran while one was open for 12% of the time, Pallas kernels for 27%

profile of v4, /device:TPU:0, one launch (start us, length us, event | category | flops | bytes accessed | tf_op | source)
XLA Modules:
  0.0 507.8 jit_solution(13152524537547301844)
XLA Ops:
  10.6 4.0 collective-permute-start.8
  20.9 9.1 %collective-permute-done = bf16[32,3200]{1,0:T(8,128)(2,1)S(1)} collective-permute-done((bf16[32,3200]{1,0:T(8,128)(2,1)}, bf16[32,3200]{1,0:T(8,128)(2,1)S(1)}, u32[]{:S(2)}, u32[]{:S(2)}) %collective-permute-start) | collective-permute-done | bytes 204832 | tf_op jit(solution)/shard_map/ppermute | solution.py:72
  48.2 16.4 %collective-permute-done.2 = bf16[32,5248]{1,0:T(8,128)(2,1)S(1)} collective-permute-done((bf16[32,5248]{1,0:T(8,128)(2,1)S(1)}, bf16[32,5248]{1,0:T(8,128)(2,1)S(1)}, u32[]{:S(2)}, u32[]{:S(2)}) %collective-permute-start.2) | collective-permute-done | bytes 335904 | tf_op jit(solution)/shard_map/ppermute | solution.py:72
  86.0 26.5 %collective-permute-done.11.refs_9_.refs_11_ = bf16[32,3200]{1,0:T(8,128)(2,1)S(1)} collective-permute-done((bf16[32,3200]{1,0:T(8,128)(2,1)S(1)}, bf16[32,3200]{1,0:T(8,128)(2,1)S(1)}, u32[]{:S(2)}, u32[]{:S(2)}) %collective-permute-start.11) | collective-permute-done | bytes 204832 | tf_op jit(solution)/shard_map/ppermute | solution.py:72
  125.0 14.3 %shard_map.271 = (bf16[1024,3072]{1,0:T(8,128)(2,1)}, bf16[1024,1024]{1,0:T(8,128)(2,1)}, s32[5]{0:T(128)}) custom-call(s32[5]{0:T(128)} %copy-done.24, bf16[128,5248]{1,0:T(8,128)(2,1)} %copy-done.4, bf16[96,5248]{1,0:T(8,128)(2,1)} %collective-permute-done.5.refs_2_.refs_6_.refs_9_, bf16[1024,1024]{1,0:T(8,128)(2,1)} %refs_1_.1, ...), custom_call_target="tpu_custom_call" | custom-call | flops 12884901888 | bytes 40265320 | tf_op jit(solution)/shard_map/pallas_call | solution.py:234
  142.0 20.0 %shard_map.272 = (bf16[1024,1024]{1,0:T(8,128)(2,1)}, bf16[1024,1024]{1,0:T(8,128)(2,1)}, f32[4,8,512]{2,1,0:T(8,128)}, s32[5]{0:T(128)}) custom-call(s32[2,4]{1,0:T(2,128)} %refs_0_.3, s32[5]{0:T(128)} %get-tuple-element.57.refs_1_, bf16[64,5248]{1,0:T(8,128)(2,1)} %copy-done.10, bf16[64,5248]{1,0:T(8,128)(2,1)} %collective-permute-done.16.refs_3_.refs_8_.refs_11_, ...), custom_call_target="tpu_custom_call" | custom-call | flops 25769803776 | bytes 80530640 | tf_op jit(solution)/shard_map/pallas_call | solution.py:334
  171.6 5.9 %collective-permute-done.18.refs_10_.refs_13_ = bf16[128,5248]{1,0:T(8,128)(2,1)S(1)} collective-permute-done((bf16[128,5248]{1,0:T(8,128)(2,1)S(1)}, bf16[128,5248]{1,0:T(8,128)(2,1)S(1)}, u32[]{:S(2)}, u32[]{:S(2)}) %collective-permute-start.18) | collective-permute-done | bytes 1343520 | tf_op jit(solution)/shard_map/ppermute | solution.py:72
  179.8 25.8 %shard_map.273 = (bf16[1024,4096]{1,0:T(8,128)(2,1)}, bf16[1024,4096]{1,0:T(8,128)(2,1)}, bf16[1024,1024]{1,0:T(8,128)(2,1)}, f32[1024,128]{1,0:T(8,128)}, f32[1...) custom-call(s32[5]{0:T(128)} %get-tuple-element.59.refs_0_, ...), custom_call_target="tpu_custom_call" | custom-call | flops 21474836480 | bytes 67108864 | tf_op jit(solution)/shard_map/pallas_call | solution.py:538
  205.6 20.8 %shard_map.274 = (bf16[1024,1024]{1,0:T(8,128)(2,1)}, bf16[1024,1024]{1,0:T(8,128)(2,1)}, f32[8,1024]{1,0:T(8,128)}, s32[5]{0:T(128)}) custom-call(s32[5]{0:T(128)} %get-tuple-element.61.refs_0_, f32[1024,1024]{1,0:T(8,128)} %get-tuple-element.62.refs_1_, bf16[1024,4096]{1,0:T(8,128)(2,1)} %get-tuple-element.63.refs_2_.refs_1_, bf16[1024,1024]{1,0:T(8,128)(2,1)} %refs_3_.3, ...), custom_call_target="tpu_custom_call" | custom-call | flops 17179869184 | bytes 53687092 | tf_op jit(solution)/shard_map/pallas_call | solution.py:602
  226.4 15.1 %shard_map.275 = (bf16[4096,1024]{1,0:T(8,128)(2,1)}, s32[5]{0:T(128)}) custom-call(s32[5]{0:T(128)} %get-tuple-element.66.refs_0_, bf16[1024,4096]{1,0:T(8,128)(2,1)} %get-tuple-element.63.refs_2_.refs_1_, bf16[1024,1024]{1,0:T(8,128)(2,1)} %get-tuple-element.67.refs_2_.refs_1_), custom_call_target="tpu_custom_call" | custom-call | flops 17179869184 | bytes 53687092 | tf_op jit(solution)/shard_map/pallas_call | solution.py:718
  241.6 32.8 %shard_map.276 = (bf16[1024,4096]{1,0:T(8,128)(2,1)}, bf16[1024,1024]{1,0:T(8,128)(2,1)}, bf16[1024,1024]{1,0:T(8,128)(2,1)}, f32[8,1024]{1,0:T(8,128)}, f32[8,4096]{1,0:T(8,128)}, /*index=5*/s32[5]{0:T(128)}) custom-call(s32[5]{0:T(128)} %get-tuple-element.68.refs_0_, bf16[1024,1024]{1,0:T(8,128)(2,1)} %get-tuple-element.67.refs_2_.refs_1_, ...), custom_call_target="tpu_custom_call" | custom-call | flops 38654705664 | bytes 120795952 | tf_op jit(solution)/shard_map/pallas_call | solution.py:677
  274.4 12.8 %shard_map.277 = (bf16[16,32,5120]{2,1,0:T(8,128)(2,1)}, s32[5]{0:T(128)}) custom-call(s32[5]{0:T(128)} %get-tuple-element.72.refs_0_, bf16[1024,1024]{1,0:T(8,128)(2,1)} %get-tuple-element.73.refs_1_, bf16[1024,1024]{1,0:T(8,128)(2,1)} %get-tuple-element.74.refs_2_.refs_5_, bf16[1024,4096]{1,0:T(8,128)(2,1)} %get-tuple-element.75.refs_3_, ...), custom_call_target="tpu_custom_call" | custom-call | flops 10737418240 | bytes 33554432 | tf_op jit(solution)/shard_map/pallas_call | solution.py:846
  287.5 13.3 %shard_map.278 = (bf16[16,32,5120]{2,1,0:T(8,128)(2,1)}, s32[5]{0:T(128)}) custom-call(s32[5]{0:T(128)} %get-tuple-element.77.refs_0_, bf16[1024,1024]{1,0:T(8,128)(2,1)} %get-tuple-element.73.refs_1_, bf16[1024,1024]{1,0:T(8,128)(2,1)} %get-tuple-element.74.refs_2_.refs_5_, bf16[1024,4096]{1,0:T(8,128)(2,1)} %get-tuple-element.75.refs_3_, ...), custom_call_target="tpu_custom_call" | custom-call | flops 10737418240 | bytes 33554432 | tf_op jit(solution)/shard_map/pallas_call | solution.py:846
  306.2 27.5 %shard_map.279 = (bf16[1024,1024]{1,0:T(8,128)(2,1)}, bf16[1024,1024]{1,0:T(8,128)(2,1)}, bf16[1024,1024]{1,0:T(8,128)(2,1)}, f32[8,1024]{1,0:T(8,128)}, s32[5]{0:T(128)}) custom-call(s32[2,4]{1,0:T(2,128)} %refs_0_.3, s32[5]{0:T(128)} %get-tuple-element.78.refs_1_, bf16[1024,3072]{1,0:T(8,128)(2,1)} %get-tuple-element.58.refs_4_.refs_5_.refs_6_.refs_2_.refs_3_, ...), custom_call_target="tpu_custom_call" | custom-call | flops 26843545600 | bytes 83886080 | tf_op jit(solution)/shard_map/pallas_call | solution.py:443
  337.1 10.5 %shard_map.280 = (bf16[16,32,3200]{2,1,0:T(8,128)(2,1)}, s32[5]{0:T(128)}) custom-call(s32[5]{0:T(128)} %get-tuple-element.81.refs_0_, bf16[2,32,5120]{2,1,0:T(8,128)(2,1)} %copy-done.12, bf16[2,32,5120]{2,1,0:T(8,128)(2,1)} %collective-permute-done.21.refs_2_, bf16[1024,1024]{1,0:T(8,128)(2,1)} %get-tuple-element.84.refs_3_.refs_2_, ...), custom_call_target="tpu_custom_call" | custom-call | flops 6442450944 | bytes 20132660 | tf_op jit(solution)/shard_map/pallas_call | solution.py:846
  349.0 4.0 add_convert_fusion.3
  358.5 41.6 %reduce-scatter.2.cloned.1.call-done.refs_1_ = bf16[256,1024]{1,0:T(8,128)(2,1)} async-done(((bf16[4096,1024]{1,0:T(8,128)(2,1)}), bf16[256,1024]{1,0:T(8,128)(2,1)}) %reduce-scatter.2.cloned.1.call-update) | async-done | bytes 524304 | tf_op jit(solution)/shard_map/reduce_scatter | solution.py:866
  400.1 10.6 %shard_map.281 = (bf16[16,32,3200]{2,1,0:T(8,128)(2,1)}, s32[5]{0:T(128)}) custom-call(s32[5]{0:T(128)} %get-tuple-element.92.refs_0_, bf16[256,1024]{1,0:T(8,128)(2,1)} %reduce-scatter.2.cloned.1.call-done.refs_1_, bf16[1024,1024]{1,0:T(8,128)(2,1)} %get-tuple-element.84.refs_3_.refs_2_, bf16[1024,1024]{1,0:T(8,128)(2,1)} %get-tuple-element.85.refs_4_.refs_3_, ...), custom_call_target="tpu_custom_call" | custom-call | flops 6442450944 | bytes 20132660 | tf_op jit(solution)/shard_map/pallas_call | solution.py:846
  412.4 13.5 %shard_map.282 = (bf16[1024,1024]{1,0:T(8,128)(2,1)}, s32[5]{0:T(128)}) custom-call(s32[5]{0:T(128)} %get-tuple-element.94.refs_0_, bf16[16,32,3200]{2,1,0:T(8,128)(2,1)} %copy-done.1, bf16[1024,1024]{1,0:T(8,128)(2,1)} %get-tuple-element.76.refs_4_.refs_2_, bf16[1024,1024]{1,0:T(8,128)(2,1)} %get-tuple-element.85.refs_4_.refs_3_, ...), custom_call_target="tpu_custom_call" | custom-call | flops 12884901888 | bytes 40265320 | tf_op jit(solution)/shard_map/pallas_call | solution.py:899
  444.9 7.5 %collective-permute-done.33 = bf16[32,5120]{1,0:T(8,128)(2,1)S(1)} collective-permute-done((bf16[32,5120]{1,0:T(8,128)(2,1)S(1)}, bf16[32,5120]{1,0:T(8,128)(2,1)S(1)}, u32[]{:S(2)}, u32[]{:S(2)}) %collective-permute-start.33) | collective-permute-done | bytes 327712 | tf_op jit(solution)/shard_map/ppermute | solution.py:72
  456.9 11.4 %collective-permute-done.34 = bf16[32,5120]{1,0:T(8,128)(2,1)S(1)} collective-permute-done((bf16[32,5120]{1,0:T(8,128)(2,1)S(1)}, bf16[32,5120]{1,0:T(8,128)(2,1)S(1)}, u32[]{:S(2)}, u32[]{:S(2)}) %collective-permute-start.34) | collective-permute-done | bytes 327712 | tf_op jit(solution)/shard_map/ppermute | solution.py:72
  470.3 4.2 collective-permute-done.26
  481.4 4.0 collective-permute-done.29
  485.4 6.6 %collective-permute-done.28 = bf16[32,3200]{1,0:T(8,128)(2,1)S(1)} collective-permute-done((bf16[32,3200]{1,0:T(8,128)(2,1)S(1)}, bf16[32,3200]{1,0:T(8,128)(2,1)S(1)}, u32[]{:S(2)}, u32[]{:S(2)}) %collective-permute-start.28) | collective-permute-done | bytes 204832 | tf_op jit(solution)/shard_map/ppermute | solution.py:72
  (220 shorter events, 120.6 us)
Async XLA Ops:
  7.2 198.4 %all-gather.2.cloned.1.call-start = ((), (), s32[]{:S(2)}) async-start(), calls=%async_computation.1 | async-start | bytes 8912896 | tf_op jit(solution)/shard_map/all_gather | solution.py:948
  10.6 30.9 %collective-permute-start.8 = (bf16[32,3200]{1,0:T(8,128)(2,1)}, bf16[32,3200]{1,0:T(8,128)(2,1)}, u32[]{:S(2)}, u32[]{:S(2)}) collective-permute-start(bf16[32,3200]{1,0:T(8,128)(2,1)} %constant_dynamic-slice_fusion.5), channel_id=1, source_target_pairs={{0,16},{2,18},{4,20},{6,22},{8,24},{10,26},{12,28},{14,30},{16,0},... | collective-permute-start | bytes 614408 | tf_op jit(solution)/shard_map/ppermute | solution.py:72
  14.7 25.1 %collective-permute-start.7 = (bf16[32,3200]{1,0:T(8,128)(2,1)}, bf16[32,3200]{1,0:T(8,128)(2,1)}, u32[]{:S(2)}, u32[]{:S(2)}) collective-permute-start(bf16[32,3200]{1,0:T(8,128)(2,1)} %constant_dynamic-slice_fusion.5), channel_id=1, source_target_pairs={{0,8},{2,10},{4,12},{6,14},{8,0},{10,2},{12,4},{14,6},{16,24},{18,... | collective-permute-start | bytes 614408 | tf_op jit(solution)/shard_map/ppermute | solution.py:72
  16.3 22.2 %collective-permute-start.6 = (bf16[64,3200]{1,0:T(8,128)(2,1)S(1)}, bf16[64,3200]{1,0:T(8,128)(2,1)S(1)}, u32[]{:S(2)}, u32[]{:S(2)}) collective-permute-start(bf16[64,3200]{1,0:T(8,128)(2,1)S(1)} %get-tuple-element.136.refs_4_.refs_6_), channel_id=1, source_target_pairs={{0,4},{2,6},{4,0},{6,2},{8,12},{10,14},{12,8},{14,10},{16,20},{18,... | collective-permute-start | bytes 1228808 | tf_op jit(solution)/shard_map/ppermute | solution.py:72
  35.0 29.7 %collective-permute-start.2 = (bf16[32,5248]{1,0:T(8,128)(2,1)S(1)}, bf16[32,5248]{1,0:T(8,128)(2,1)S(1)}, u32[]{:S(2)}, u32[]{:S(2)}) collective-permute-start(bf16[32,5248]{1,0:T(8,128)(2,1)S(1)} %constant_dynamic-slice_fusion.4), channel_id=1, source_target_pairs={{0,16},{2,18},{4,20},{6,22},{8,24},{10,26},{12,28},{14,30},{16,0},... | collective-permute-start | bytes 1007624 | tf_op jit(solution)/shard_map/ppermute | solution.py:72
  38.5 27.4 %collective-permute-start.1 = (bf16[32,5248]{1,0:T(8,128)(2,1)S(1)}, bf16[32,5248]{1,0:T(8,128)(2,1)S(1)}, u32[]{:S(2)}, u32[]{:S(2)}) collective-permute-start(bf16[32,5248]{1,0:T(8,128)(2,1)S(1)} %constant_dynamic-slice_fusion.4), channel_id=1, source_target_pairs={{0,8},{2,10},{4,12},{6,14},{8,0},{10,2},{12,4},{14,6},{16,24},{18,... | collective-permute-start | bytes 1007624 | tf_op jit(solution)/shard_map/ppermute | solution.py:72
  44.0 34.9 %collective-permute-start.10 = (bf16[96,3200]{1,0:T(8,128)(2,1)}, bf16[96,3200]{1,0:T(8,128)(2,1)}, u32[]{:S(2)}, u32[]{:S(2)}) collective-permute-start(bf16[96,3200]{1,0:T(8,128)(2,1)} %get-tuple-element.138.refs_6_.refs_8_), channel_id=1, source_target_pairs={{0,1},{1,0},{2,3},{3,2},{4,5},{5,4},{6,7},{7,6},{8,9},{9,8},{10,11... | collective-permute-start | bytes 1843208 | tf_op jit(solution)/shard_map/ppermute | solution.py:75
  45.6 34.9 %collective-permute-start.9 = (bf16[96,3200]{1,0:T(8,128)(2,1)}, bf16[96,3200]{1,0:T(8,128)(2,1)}, u32[]{:S(2)}, u32[]{:S(2)}) collective-permute-start(bf16[96,3200]{1,0:T(8,128)(2,1)} %get-tuple-element.138.refs_6_.refs_8_), channel_id=1, source_target_pairs={{0,4},{2,6},{4,0},{6,2},{8,12},{10,14},{12,8},{14,10},{16,20},{18,... | collective-permute-start | bytes 1843208 | tf_op jit(solution)/shard_map/ppermute | solution.py:72
  73.3 40.9 %collective-permute-start.5 = (bf16[96,5248]{1,0:T(8,128)(2,1)}, bf16[96,5248]{1,0:T(8,128)(2,1)}, u32[]{:S(2)}, u32[]{:S(2)}) collective-permute-start(bf16[96,5248]{1,0:T(8,128)(2,1)} %pad_maximum_fusion.5.refs_4_.refs_7_), channel_id=1, source_target_pairs={{0,1},{1,0},{2,3},{3,2},{4,5},{5,4},{6,7},{7,6},{8,9},{9,8},{10,11... | collective-permute-start | bytes 3022856 | tf_op jit(solution)/shard_map/ppermute | solution.py:75
  76.8 42.8 %collective-permute-start.4 = (bf16[128,5248]{1,0:T(8,128)(2,1)}, bf16[128,5248]{1,0:T(8,128)(2,1)S(1)}, u32[]{:S(2)}, u32[]{:S(2)}) collective-permute-start(bf16[128,5248]{1,0:T(8,128)(2,1)} %pad_maximum_fusion.1), channel_id=1, source_target_pairs={{0,4},{2,6},{4,0},{6,2},{8,12},{10,14},{12,8},{14,10},{16,20},{18,... | collective-permute-start | bytes 4030472 | tf_op jit(solution)/shard_map/ppermute | solution.py:72
  79.9 32.6 %collective-permute-start.11 = (bf16[32,3200]{1,0:T(8,128)(2,1)S(1)}, bf16[32,3200]{1,0:T(8,128)(2,1)S(1)}, u32[]{:S(2)}, u32[]{:S(2)}) collective-permute-start(bf16[32,3200]{1,0:T(8,128)(2,1)S(1)} %dynamic_slice.32), channel_id=1, source_target_pairs={{0,4},{2,6},{4,0},{6,2},{8,12},{10,14},{12,8},{14,10},{16,20},{18,... | collective-permute-start | bytes 614408 | tf_op jit(solution)/shard_map/ppermute | solution.py:72
  81.5 31.7 %collective-permute-start.12 = (bf16[64,3200]{1,0:T(8,128)(2,1)S(1)}, bf16[64,3200]{1,0:T(8,128)(2,1)S(1)}, u32[]{:S(2)}, u32[]{:S(2)}) collective-permute-start(bf16[64,3200]{1,0:T(8,128)(2,1)S(1)} %dynamic_slice.33), channel_id=1, source_target_pairs={{0,1},{1,0},{2,3},{3,2},{4,5},{5,4},{6,7},{7,6},{8,9},{9,8},{10,11... | collective-permute-start | bytes 1228808 | tf_op jit(solution)/shard_map/ppermute | solution.py:75
  86.0 38.9 %collective-permute-start.13 = (bf16[416,3200]{1,0:T(8,128)(2,1)}, bf16[416,3200]{1,0:T(8,128)(2,1)}, u32[]{:S(2)}, u32[]{:S(2)}) collective-permute-start(bf16[416,3200]{1,0:T(8,128)(2,1)} %constant_dynamic-update-slice_fusion.3), channel_id=1, source_target_pairs={{0,2},{2,0},{4,6},{6,4},{8,10},{10,8},{12,14},{14,12},{16,18},{18,... | collective-permute-start | bytes 7987208 | tf_op jit(solution)/shard_map/ppermute | solution.py:72
  118.0 22.0 %collective-permute-start.15 = (bf16[64,5248]{1,0:T(8,128)(2,1)}, bf16[64,5248]{1,0:T(8,128)(2,1)S(1)}, u32[]{:S(2)}, u32[]{:S(2)}) collective-permute-start(bf16[64,5248]{1,0:T(8,128)(2,1)} %pad_maximum_fusion.8), channel_id=1, source_target_pairs={{0,4},{2,6},{4,0},{6,2},{8,12},{10,14},{12,8},{14,10},{16,20},{18,... | collective-permute-start | bytes 2015240 | tf_op jit(solution)/shard_map/ppermute | solution.py:72
  122.9 277.3 %reduce-scatter.2.cloned.1.call-start = ((), (), s32[]{:S(2)}) async-start(), calls=%async_computation.2 | async-start | bytes 8912896 | tf_op jit(solution)/shard_map/reduce_scatter | solution.py:866
  305.1 31.2 %collective-permute-start.21 = (bf16[2,32,5120]{2,1,0:T(8,128)(2,1)S(1)}, bf16[2,32,5120]{2,1,0:T(8,128)(2,1)}, u32[]{:S(2)}, u32[]{:S(2)}) collective-permute-start(bf16[2,32,5120]{2,1,0:T(8,128)(2,1)S(1)} %get-tuple-element.115), channel_id=1, source_target_pairs={{0,1},{1,0},{2,3},{3,2},{4,5},{5,4},{6,7},{7,6},{8,9},{9,8},{10,11... | collective-permute-start | bytes 1966088 | tf_op jit(solution)/shard_map/ppermute | solution.py:75
  305.2 31.1 %collective-permute-start.20 = (bf16[2,32,5120]{2,1,0:T(8,128)(2,1)S(1)}, bf16[2,32,5120]{2,1,0:T(8,128)(2,1)S(1)}, u32[]{:S(2)}, u32[]{:S(2)}) collective-permute-start(bf16[2,32,5120]{2,1,0:T(8,128)(2,1)S(1)} %get-tuple-element.116), channel_id=1, source_target_pairs={{0,4},{2,6},{4,0},{6,2},{8,12},{10,14},{12,8},{14,10},{16,20},{18,... | collective-permute-start | bytes 1966088 | tf_op jit(solution)/shard_map/ppermute | solution.py:72
  347.7 63.0 %collective-permute-start.22 = (bf16[16,32,3200]{2,1,0:T(8,128)(2,1)}, bf16[16,32,3200]{2,1,0:T(8,128)(2,1)S(1)}, u32[]{:S(2)}, u32[]{:S(2)}) collective-permute-start(bf16[16,32,3200]{2,1,0:T(8,128)(2,1)} %get-tuple-element.95), channel_id=1, source_target_pairs={{0,2},{2,0},{4,6},{6,4},{8,10},{10,8},{12,14},{14,12},{16,18},{18,... | collective-permute-start | bytes 9830408 | tf_op jit(solution)/shard_map/ppermute | solution.py:72
  354.3 79.3 %collective-permute-start.32 = (bf16[4,32,5120]{2,1,0:T(8,128)(2,1)}, bf16[4,32,5120]{2,1,0:T(8,128)(2,1)}, u32[]{:S(2)}, u32[]{:S(2)}) collective-permute-start(bf16[4,32,5120]{2,1,0:T(8,128)(2,1)} %pad_maximum_fusion.4), channel_id=1, source_target_pairs={{0,1},{1,0},{2,3},{3,2},{4,5},{5,4},{6,7},{7,6},{8,9},{9,8},{10,11... | collective-permute-start | bytes 3932168 | tf_op jit(solution)/shard_map/ppermute | solution.py:75
  357.5 76.1 %collective-permute-start.31 = (bf16[4,32,5120]{2,1,0:T(8,128)(2,1)}, bf16[4,32,5120]{2,1,0:T(8,128)(2,1)}, u32[]{:S(2)}, u32[]{:S(2)}) collective-permute-start(bf16[4,32,5120]{2,1,0:T(8,128)(2,1)} %pad_maximum_fusion.3), channel_id=1, source_target_pairs={{0,4},{2,6},{4,0},{6,2},{8,12},{10,14},{12,8},{14,10},{16,20},{18,... | collective-permute-start | bytes 3932168 | tf_op jit(solution)/shard_map/ppermute | solution.py:72
  441.2 27.2 %collective-permute-start.34 = (bf16[32,5120]{1,0:T(8,128)(2,1)S(1)}, bf16[32,5120]{1,0:T(8,128)(2,1)S(1)}, u32[]{:S(2)}, u32[]{:S(2)}) collective-permute-start(bf16[32,5120]{1,0:T(8,128)(2,1)S(1)} %get-tuple-element.125), channel_id=1, source_target_pairs={{0,16},{2,18},{4,20},{6,22},{8,24},{10,26},{12,28},{14,30},{16,0},... | collective-permute-start | bytes 983048 | tf_op jit(solution)/shard_map/ppermute | solution.py:72
  442.2 26.9 %collective-permute-start.37 = (bf16[256,1024]{1,0:T(8,128)(2,1)S(1)}, bf16[256,1024]{1,0:T(8,128)(2,1)S(1)}, u32[]{:S(2)}, u32[]{:S(2)}) collective-permute-start(bf16[256,1024]{1,0:T(8,128)(2,1)S(1)} %broadcast_add_fusion.6), channel_id=1, source_target_pairs={{0,1},{1,0},{2,3},{3,2},{4,5},{5,4},{6,7},{7,6},{8,9},{9,8},{10,11... | collective-permute-start | bytes 1572872 | tf_op jit(solution)/shard_map/ppermute | solution.py:75
  443.9 30.6 %collective-permute-start.26 = (bf16[4,32,3200]{2,1,0:T(8,128)(2,1)S(1)}, bf16[4,32,3200]{2,1,0:T(8,128)(2,1)S(1)}, u32[]{:S(2)}, u32[]{:S(2)}) collective-permute-start(bf16[4,32,3200]{2,1,0:T(8,128)(2,1)S(1)} %pad_maximum_fusion.7), channel_id=1, source_target_pairs={{0,1},{1,0},{2,3},{3,2},{4,5},{5,4},{6,7},{7,6},{8,9},{9,8},{10,11... | collective-permute-start | bytes 2457608 | tf_op jit(solution)/shard_map/ppermute | solution.py:75
  452.4 22.0 %collective-permute-start.24 = (bf16[4,32,3200]{2,1,0:T(8,128)(2,1)S(1)}, bf16[4,32,3200]{2,1,0:T(8,128)(2,1)S(1)}, u32[]{:S(2)}, u32[]{:S(2)}) collective-permute-start(bf16[4,32,3200]{2,1,0:T(8,128)(2,1)S(1)} %pad_maximum_fusion.6), channel_id=1, source_target_pairs={{0,4},{2,6},{4,0},{6,2},{8,12},{10,14},{12,8},{14,10},{16,20},{18,... | collective-permute-start | bytes 2457608 | tf_op jit(solution)/shard_map/ppermute | solution.py:72
  (45 other events, 663.8 us)
Sparse Core Ops, SparseCore 0:
  123.0 73.3 all-gather.1
  287.6 112.4 reduce-scatter.1
